TPU v7x, 32 devices: a whole 2x2x4 slice. The times are simulated.
32 devices in a mesh: dp: 8 (over y, x, core), fsdp: 4 (over z).
Axes of the slice: x: 2, y: 2, z: 4, core: 2. Of those that a mesh axis runs over, the one named last changes fastest.
Arguments:
- hidden_in: bfloat16 [8192, 2048], P(('dp', 'fsdp')), may hold values from -6 to 6
- piece_starts: int32 [8, 2], P('dp'), may hold values from 0 to 768, as said below
- out_cotangent: bfloat16 [8192, 2048], P(('dp', 'fsdp')), may hold values from -6 to 6
- owners: int32 [1856], replicated, may hold values from 0 to 31, as said below
- master: float32 [2432, 16, 2048], P(('dp', 'fsdp'))
- moment_one: float32 [2432, 16, 2048], P(('dp', 'fsdp'))
- moment_two: float32 [2432, 16, 2048], P(('dp', 'fsdp')), as said below
- gain_master: float32 [2, 2048], P(None, ('dp', 'fsdp')), may hold values from 0.5 to 1.5
- gain_one: float32 [2, 2048], P(None, ('dp', 'fsdp'))
- gain_two: float32 [2, 2048], P(None, ('dp', 'fsdp')), as said below
Outputs:
- block_out: bfloat16 [8192, 2048], P(('dp', 'fsdp'))
- input_grad: float32 [8192, 2048], P(('dp', 'fsdp'))
- weight_grad: float32 [2432, 16, 2048], P(('dp', 'fsdp'))
- new_master: float32 [2432, 16, 2048], P(('dp', 'fsdp'))
- new_moment_one: float32 [2432, 16, 2048], P(('dp', 'fsdp'))
- new_moment_two: float32 [2432, 16, 2048], P(('dp', 'fsdp'))
- gain_grad: float32 [2, 2048], P(None, ('dp', 'fsdp'))
- new_gains: float32 [2, 2048], P(None, ('dp', 'fsdp'))
- new_gain_one: float32 [2, 2048], P(None, ('dp', 'fsdp'))
- new_gain_two: float32 [2, 2048], P(None, ('dp', 'fsdp'))
Inputs may be any that keep to these rules, and one draw needn't show every extreme that they name: `owners`: within each of the four groups of tiles a device owns at most 8, 6, 41 or 21 tiles of that group, and some device owns exactly that many. `piece_starts`: piece c of a sequence lies within positions c * 512 to (c + 1) * 512 - 1; pieces don't intersect. `moment_two`: positive in every entry. `gain_two`: positive in every entry.
All inputs are finite; a program needn't handle non-finite values.
Results may differ from a plain program's by a relative error of at most 0.015.
The roundings to bfloat16 on the way count: a program that leaves them out, or rounds other values in their place, can miss the bound.
Values may be sent and summed in bfloat16 or wider, within the bound.
A program may use at most 704 MiB of HBM per device.

v0:
```python
import math

import jax
import jax.numpy as jnp
from jax import lax
from jax.sharding import PartitionSpec as P

D = 2048
HEADS = 32
KV_HEADS = 8
HEAD = 64
FF = 8192
PIECE = 256
STEP = 5


norm_eps = 1e-05
adam_eps = 1e-08
beta_one = 0.5
beta_two = 0.5
learn_rate = 0.02
gain_rate = 0.3
decay_rate = 0.1
rope_base = 500000.0
masked_score = -1e30


def section_layout(devices, tile_rows):
    counts = [
        (D + 2 * KV_HEADS * HEAD) // tile_rows,
        HEADS * HEAD // tile_rows,
        2 * FF // tile_rows,
        FF // tile_rows,
    ]
    layout = []
    first_tile = 0
    first_slot = 0
    for number in counts:
        capacity = 5 * number // (4 * devices) + 1
        layout.append((first_tile, number, capacity, first_slot))
        first_tile += number
        first_slot += capacity
    return layout


def tile_lookup(owners, first_tile, number, capacity, devices):
    mine = owners[first_tile : first_tile + number]
    order = jnp.arange(number, dtype=jnp.int32)
    earlier = (mine[:, None] == mine[None, :]) & (order[None, :] < order[:, None])
    ranked = jnp.sum(earlier.astype(jnp.int32), axis=1)
    slot_index = mine * capacity + ranked
    return jnp.full((devices * capacity,), -1, jnp.int32).at[slot_index].set(order)


def tile_columns(tile_map, tile_rows):
    filled = jnp.repeat(tile_map >= 0, tile_rows)
    columns = (
        jnp.maximum(tile_map, 0)[:, None] * tile_rows
        + jnp.arange(tile_rows, dtype=jnp.int32)[None, :]
    ).reshape(-1)
    return (columns, filled)


def contract_fold(left_side, tile_map, tile_rows):

    def fold(carry_sum, shard_piece, offset):
        number = shard_piece.shape[0]
        columns, filled = tile_columns(tile_map, tile_rows)
        picked = jnp.where(
            filled[None, :], jnp.take(left_side, columns, axis=1), jnp.zeros((), left_side.dtype)
        )
        flat_piece = shard_piece.reshape(number * tile_rows, shard_piece.shape[2])
        return jnp.dot(picked, flat_piece, preferred_element_type=jnp.float32)

    return fold


def expand_fold(right_side, tile_map, tile_rows, out_width):

    def fold(carry_sum, shard_piece, offset):
        number = shard_piece.shape[0]
        columns, filled = tile_columns(tile_map, tile_rows)
        target = jnp.where(filled, columns, out_width)
        flat_piece = shard_piece.reshape(number * tile_rows, shard_piece.shape[2])
        products = lax.dot_general(
            right_side, flat_piece, (((1,), (1,)), ((), ())), preferred_element_type=jnp.float32
        )
        return carry_sum.at[:, target].add(products, mode="drop")

    return fold


def grad_term(left_side, right_side, tile_map, tile_rows):
    columns, filled = tile_columns(tile_map, tile_rows)
    picked = jnp.where(
        filled[None, :], jnp.take(left_side, columns, axis=1), jnp.zeros((), left_side.dtype)
    )
    return lax.dot_general(
        picked, right_side, (((0,), (0,)), ((), ())), preferred_element_type=jnp.float32
    )


def piece_labels(positions, starts):
    inside = (positions[:, None] >= starts[None, :]) & (
        positions[:, None] < starts[None, :] + PIECE
    )
    labels = jnp.arange(1, starts.shape[0] + 1, dtype=jnp.int32)
    return jnp.sum(jnp.where(inside, labels[None, :], 0), axis=1) - 1


def attention_mask(query_pos, key_pos, starts):
    query_label = piece_labels(query_pos, starts)
    key_label = piece_labels(key_pos, starts)
    causal = key_pos[None, :] <= query_pos[:, None]
    shared = (query_label[:, None] == key_label[None, :]) & (query_label[:, None] >= 0)
    return causal | shared


def rope_tables(positions):
    half_dim = HEAD // 2
    inverse = rope_base ** (-(jnp.arange(half_dim, dtype=jnp.float32) * 2.0 / HEAD))
    angles = positions[:, None] * inverse[None, :]
    return (jnp.cos(angles)[:, None, :], jnp.sin(angles)[:, None, :])


def rope_apply(values, cosine, sine):
    half_dim = HEAD // 2
    first_half = values[..., :half_dim]
    second_half = values[..., half_dim:]
    return jnp.concatenate(
        [first_half * cosine - second_half * sine, second_half * cosine + first_half * sine],
        axis=-1,
    )


def rope_back(grads, cosine, sine):
    half_dim = HEAD // 2
    first_half = grads[..., :half_dim]
    second_half = grads[..., half_dim:]
    return jnp.concatenate(
        [first_half * cosine + second_half * sine, second_half * cosine - first_half * sine],
        axis=-1,
    )


def adam_step(weights, first_moment, second_moment, grads, step, decay, rate):
    new_one = beta_one * first_moment + (1.0 - beta_one) * grads
    new_two = beta_two * second_moment + (1.0 - beta_two) * grads * grads
    correct_one = 1.0 - beta_one**step
    correct_two = 1.0 - beta_two**step
    update = -rate * (
        new_one / correct_one / (jnp.sqrt(new_two / correct_two) + adam_eps) + decay * weights
    )
    return (new_one, new_two, weights + update)


def shards(
    hidden_in,
    piece_starts,
    out_cotangent,
    owners,
    master,
    moment_one,
    moment_two,
    gain_master,
    gain_one,
    gain_two,
):
    devices = lax.axis_size("dp") * lax.axis_size("fsdp")
    tile_rows = master.shape[1]
    model_width = master.shape[2]
    layout = section_layout(devices, tile_rows)
    lookups = [tile_lookup(owners, entry[0], entry[1], entry[2], devices) for entry in layout]
    weights_low = master.astype(jnp.bfloat16)
    shard_qkv, shard_out, shard_ffn, shard_down = [
        weights_low[entry[3] : entry[3] + entry[2]] for entry in layout
    ]
    map_qkv, map_out, map_ffn, map_down = lookups
    cap_qkv, cap_out, cap_ffn, cap_down = [entry[2] for entry in layout]

    def through_qkv(fold, start_value):
        return fold(
            start_value, lax.all_gather(shard_qkv, ("dp", "fsdp"), axis=0, tiled=True), jnp.int32(0)
        )

    def through_out(fold, start_value):
        return fold(
            start_value, lax.all_gather(shard_out, ("dp", "fsdp"), axis=0, tiled=True), jnp.int32(0)
        )

    def through_ffn(fold, start_value):
        return fold(
            start_value, lax.all_gather(shard_ffn, ("dp", "fsdp"), axis=0, tiled=True), jnp.int32(0)
        )

    def through_down(fold, start_value):
        return fold(
            start_value,
            lax.all_gather(shard_down, ("dp", "fsdp"), axis=0, tiled=True),
            jnp.int32(0),
        )

    gains_low = lax.all_gather(
        gain_master.astype(jnp.bfloat16), ("dp", "fsdp"), axis=1, tiled=True
    ).astype(jnp.float32)
    gain_attn = gains_low[0]
    gain_ffn = gains_low[1]
    tokens = hidden_in.astype(jnp.float32)
    local_len = tokens.shape[0]
    seq_len = local_len * lax.axis_size("fsdp")
    group_size = HEADS // KV_HEADS
    kv_width = KV_HEADS * HEAD
    qkv_width = model_width + 2 * kv_width
    score_scale = 1.0 / math.sqrt(HEAD)
    query_pos = lax.axis_index("fsdp") * local_len + jnp.arange(local_len, dtype=jnp.int32)
    key_pos = jnp.arange(seq_len, dtype=jnp.int32)
    allowed = attention_mask(query_pos, key_pos, piece_starts[0])
    cosine, sine = rope_tables(query_pos.astype(jnp.float32))
    inv_one = lax.rsqrt(jnp.mean(tokens * tokens, axis=1, keepdims=True) + norm_eps)
    normed = (tokens * inv_one * gain_attn).astype(jnp.bfloat16)
    projected = through_qkv(
        expand_fold(normed, map_qkv, tile_rows, qkv_width),
        jnp.zeros((local_len, qkv_width), jnp.float32),
    )
    queries = rope_apply(
        projected[:, :model_width].reshape(local_len, HEADS, HEAD), cosine, sine
    ).astype(jnp.bfloat16)
    queries = queries.reshape(local_len, KV_HEADS, group_size, HEAD)
    keys_local = rope_apply(
        projected[:, model_width : model_width + kv_width].reshape(local_len, KV_HEADS, HEAD),
        cosine,
        sine,
    )
    keys_local = keys_local.astype(jnp.bfloat16).reshape(local_len, kv_width)
    values_local = projected[:, model_width + kv_width :].astype(jnp.bfloat16)
    keys_all, values_all = (
        lax.all_gather(keys_local, "fsdp", axis=0, tiled=True),
        lax.all_gather(values_local, "fsdp", axis=0, tiled=True),
    )
    keys_all = keys_all.reshape(seq_len, KV_HEADS, HEAD)
    values_all = values_all.reshape(seq_len, KV_HEADS, HEAD)

    def masked_scores():
        raw = (
            jnp.einsum("tkgh,skh->kgts", queries, keys_all, preferred_element_type=jnp.float32)
            * score_scale
        )
        return jnp.where(allowed[None, None], raw, masked_score)

    scores = masked_scores()
    row_top = jnp.max(scores, axis=-1, keepdims=True)
    shifted = jnp.exp(scores - row_top)
    row_total = jnp.sum(shifted, axis=-1, keepdims=True)
    log_total = row_top + jnp.log(row_total)
    probs_low = (shifted / row_total).astype(jnp.bfloat16)
    attended = jnp.einsum(
        "kgts,skh->tkgh", probs_low, values_all, preferred_element_type=jnp.float32
    )
    attended = attended.reshape(local_len, model_width).astype(jnp.bfloat16)
    branch = through_out(
        contract_fold(attended, map_out, tile_rows),
        jnp.zeros((local_len, model_width), jnp.float32),
    )
    middle = tokens + branch
    inv_two = lax.rsqrt(jnp.mean(middle * middle, axis=1, keepdims=True) + norm_eps)
    normed_two = (middle * inv_two * gain_ffn).astype(jnp.bfloat16)
    gate_up = through_ffn(
        expand_fold(normed_two, map_ffn, tile_rows, 2 * FF),
        jnp.zeros((local_len, 2 * FF), jnp.float32),
    )
    gate_part = gate_up[:, :FF]
    up_part = gate_up[:, FF:]
    sigmoid_gate = jax.nn.sigmoid(gate_part)
    silu_gate = gate_part * sigmoid_gate
    activated = (silu_gate * up_part).astype(jnp.bfloat16)
    ffn_out = through_down(
        contract_fold(activated, map_down, tile_rows),
        jnp.zeros((local_len, model_width), jnp.float32),
    )
    block_out = (middle + ffn_out).astype(jnp.bfloat16)
    grad_out = out_cotangent.astype(jnp.float32)
    grad_hidden = through_down(
        expand_fold(out_cotangent, map_down, tile_rows, FF), jnp.zeros((local_len, FF), jnp.float32)
    )
    down_grads = lax.psum_scatter(
        grad_term(activated, out_cotangent, map_down, tile_rows),
        ("dp", "fsdp"),
        scatter_dimension=0,
        tiled=True,
    )
    grad_gate = grad_hidden * up_part * sigmoid_gate * (1.0 + gate_part * (1.0 - sigmoid_gate))
    grad_up = grad_hidden * silu_gate
    grad_gate_up = jnp.concatenate([grad_gate, grad_up], axis=1).astype(jnp.bfloat16)
    grad_normed_two = through_ffn(
        contract_fold(grad_gate_up, map_ffn, tile_rows),
        jnp.zeros((local_len, model_width), jnp.float32),
    )
    ffn_grads = lax.psum_scatter(
        grad_term(grad_gate_up, normed_two, map_ffn, tile_rows),
        ("dp", "fsdp"),
        scatter_dimension=0,
        tiled=True,
    )
    scaled_two = grad_normed_two * gain_ffn
    grad_middle = (
        grad_out
        + inv_two * scaled_two
        - middle * inv_two**3 * jnp.mean(scaled_two * middle, axis=1, keepdims=True)
    )
    gain_two_term = jnp.sum(grad_normed_two * middle * inv_two, axis=0)
    grad_branch = grad_middle.astype(jnp.bfloat16)
    grad_attended = through_out(
        expand_fold(grad_branch, map_out, tile_rows, model_width),
        jnp.zeros((local_len, model_width), jnp.float32),
    )
    out_grads = lax.psum_scatter(
        grad_term(attended, grad_branch, map_out, tile_rows),
        ("dp", "fsdp"),
        scatter_dimension=0,
        tiled=True,
    )
    grad_attn_low = grad_attended.astype(jnp.bfloat16).reshape(
        local_len, KV_HEADS, group_size, HEAD
    )
    probs_again = jnp.exp(masked_scores() - log_total)
    grad_probs = jnp.einsum(
        "tkgh,skh->kgts", grad_attn_low, values_all, preferred_element_type=jnp.float32
    )
    row_dot = jnp.sum(probs_again * grad_probs, axis=-1, keepdims=True)
    grad_scores = (probs_again * (grad_probs - row_dot)).astype(jnp.bfloat16)
    grad_queries = (
        jnp.einsum("kgts,skh->tkgh", grad_scores, keys_all, preferred_element_type=jnp.float32)
        * score_scale
    )
    key_terms = (
        jnp.einsum("kgts,tkgh->skh", grad_scores, queries, preferred_element_type=jnp.float32)
        * score_scale
    )
    value_terms = jnp.einsum(
        "kgts,tkgh->skh",
        probs_again.astype(jnp.bfloat16),
        grad_attn_low,
        preferred_element_type=jnp.float32,
    )
    grad_keys, grad_values = (
        lax.psum_scatter(
            key_terms.reshape(seq_len, kv_width), "fsdp", scatter_dimension=0, tiled=True
        ),
        lax.psum_scatter(
            value_terms.reshape(seq_len, kv_width), "fsdp", scatter_dimension=0, tiled=True
        ),
    )
    grad_query_pre = rope_back(grad_queries.reshape(local_len, HEADS, HEAD), cosine, sine).reshape(
        local_len, model_width
    )
    grad_key_pre = rope_back(grad_keys.reshape(local_len, KV_HEADS, HEAD), cosine, sine).reshape(
        local_len, kv_width
    )
    grad_projected = jnp.concatenate([grad_query_pre, grad_key_pre, grad_values], axis=1).astype(
        jnp.bfloat16
    )
    grad_normed = through_qkv(
        contract_fold(grad_projected, map_qkv, tile_rows),
        jnp.zeros((local_len, model_width), jnp.float32),
    )
    qkv_grads = lax.psum_scatter(
        grad_term(grad_projected, normed, map_qkv, tile_rows),
        ("dp", "fsdp"),
        scatter_dimension=0,
        tiled=True,
    )
    weight_grad = jnp.concatenate(
        [
            qkv_grads.reshape(cap_qkv, tile_rows, model_width),
            out_grads.reshape(cap_out, tile_rows, model_width),
            ffn_grads.reshape(cap_ffn, tile_rows, model_width),
            down_grads.reshape(cap_down, tile_rows, model_width),
        ],
        axis=0,
    )
    scaled_one = grad_normed * gain_attn
    input_grad = (
        grad_middle
        + inv_one * scaled_one
        - tokens * inv_one**3 * jnp.mean(scaled_one * tokens, axis=1, keepdims=True)
    )
    gain_one_term = jnp.sum(grad_normed * tokens * inv_one, axis=0)
    gain_grad = lax.psum_scatter(
        jnp.stack([gain_one_term, gain_two_term]), ("dp", "fsdp"), scatter_dimension=1, tiled=True
    )
    device = lax.axis_index(("dp", "fsdp"))
    filled_slots = jnp.concatenate(
        [
            lax.dynamic_slice_in_dim(lookups[index], device * layout[index][2], layout[index][2])
            >= 0
            for index in range(4)
        ]
    )
    step = float(STEP)
    new_one, new_two, new_weights = adam_step(
        master, moment_one, moment_two, weight_grad, step, decay_rate, learn_rate
    )
    keep_slot = filled_slots[:, None, None]
    new_one = jnp.where(keep_slot, new_one, 0.0)
    new_two = jnp.where(keep_slot, new_two, 0.0)
    new_weights = jnp.where(keep_slot, new_weights, 0.0)
    new_gain_one, new_gain_two, new_gains = adam_step(
        gain_master, gain_one, gain_two, gain_grad, step, 0.0, gain_rate
    )
    return (
        block_out,
        input_grad,
        weight_grad,
        new_weights,
        new_one,
        new_two,
        gain_grad,
        new_gains,
        new_gain_one,
        new_gain_two,
    )


def solution(mesh):
    return jax.shard_map(
        shards,
        mesh=mesh,
        in_specs=(
            P(("dp", "fsdp"), None),
            P("dp", None),
            P(("dp", "fsdp"), None),
            P(),
            P(("dp", "fsdp"), None, None),
            P(("dp", "fsdp"), None, None),
            P(("dp", "fsdp"), None, None),
            P(None, ("dp", "fsdp")),
            P(None, ("dp", "fsdp")),
            P(None, ("dp", "fsdp")),
        ),
        out_specs=(
            P(("dp", "fsdp"), None),
            P(("dp", "fsdp"), None),
            P(("dp", "fsdp"), None, None),
            P(("dp", "fsdp"), None, None),
            P(("dp", "fsdp"), None, None),
            P(("dp", "fsdp"), None, None),
            P(None, ("dp", "fsdp")),
            P(None, ("dp", "fsdp")),
            P(None, ("dp", "fsdp")),
            P(None, ("dp", "fsdp")),
        ),
        check_vma=False,
    )
```

profile of v0, /device:TPU:0, one launch (start us, length us, event | category | flops | bytes accessed | tf_op | source)
XLA Modules:
  0.0 7038.2 jit_solution(8954191397768899789)
XLA Ops:
  7.3 4.7 convert_element_type.86
  12.0 2.3 copy-done.1
  15.2 69.9 all-gather
  89.7 43.2 all-gather.8.cloned.1.call-done
  132.9 10.2 convolution_bitcast_fusion.1
  143.2 5.6 copy.52
  148.8 23.6 scatter_custom_fusion.2
  174.1 1.8 slice.110
  175.9 2.6 slice.115
  178.6 3.7 slice.112
  185.2 4.5 scatter_custom_fusion.4
  193.3 2.4 scatter_custom_fusion.3
  198.8 2.6 iota_add_fusion
  201.5 2.0 add.474
  203.4 1.4 select_n.203
  206.9 1.5 fusion.41
  212.7 1.3 compare_select_fusion.5
  214.0 1.5 compare_and_fusion
  216.1 15.0 fusion.64
  231.1 13.2 fusion.3
  244.4 13.8 fusion.27
  258.2 13.4 gather_fusion
  271.7 57.4 all-gather.14.cloned.1.call-done
  329.0 10.0 multiply_reduce_fusion.2
  340.3 235.5 %all-gather.18.cloned.1.call-done = bf16[672,16,2048]{2,1,0:T(8,128)(2,1)} async-done(((bf16[21,16,2048]{2,1,0:T(8,128)(2,1)}), bf16[672,16,2048]{2,1,0:T(8,128)(2,1)}) %all-gather.18.cloned.1.call-update) | async-done | bytes 44040208 | tf_op jit(solution)/shard_map/all_gather | solution.py:199
  575.8 24.5 fusion.65
  600.3 62.2 scatter_custom_fusion.6
  662.5 361.4 %all-gather.16.cloned.1.call-done = bf16[1312,16,2048]{2,1,0:T(8,128)(2,1)} async-done(((bf16[41,16,2048]{2,1,0:T(8,128)(2,1)}), bf16[1312,16,2048]{2,1,0:T(8,128)(2,1)}) %all-gather.16.cloned.1.call-update) | async-done | bytes 85983248 | tf_op jit(solution)/shard_map/all_gather | solution.py:193
  1024.0 40.6 convolution_bitcast_fusion
  1064.5 21.5 copy.54
  1086.1 119.4 %scatter_custom_fusion.5 = f32[256,16384]{0,1:T(8,128)} fusion(s32[20992]{0:T(1024)} %fusion.39, f32[20992,256]{1,0:T(8,128)} %copy.54, f32[]{:T(128)} %constant.72.clone.1), kind=kCustom, calls=%fused_computation.39 | custom fusion | flops 5373952 | bytes 16777728 | tf_op jit(solution)/shard_map/scatter-add | solution.py:88
  1205.5 12.3 multiply_convert_fusion.1
  1217.8 24.5 pad_maximum_fusion.1
  1242.3 52.5 gather_fusion.2
  1294.8 37.9 multiply_reduce_fusion
  1334.7 6.5 convolution_bitcast_fusion.2
  1341.1 2.4 copy.55
  1343.5 17.9 scatter_custom_fusion.7
  1361.5 22.4 fusion
  1384.0 28.0 fusion.2
  1412.0 12.2 bitcast_multiply_fusion.1
  1424.3 15.3 fusion.5
  1440.0 8.8 convolution_multiply_fusion
  1449.3 17.1 reduce-scatter.13.cloned.1.call-done
  1467.5 45.1 reduce-scatter.15.cloned.1.call-done
  1513.8 17.0 gather_fusion.3
  1530.9 13.3 fusion.24
  1544.2 1.4 copy.67
  1545.7 12.0 fusion.32
  1557.7 1.5 copy-done.5
  1559.2 12.9 fusion.35
  1573.4 28.0 gather_fusion.1
  1601.4 33.4 fusion.60
  1634.9 1.5 copy-done.11
  1636.7 64.8 fusion.58
  1704.0 26.4 fusion.16
  1730.5 1.9 fusion.21
  1733.9 196.1 %reduce-scatter.19.cloned.1.call-done = f32[96,2048]{1,0:T(8,128)} async-done(((f32[3072,2048]{1,0:T(8,128)}), f32[96,2048]{1,0:T(8,128)}) %reduce-scatter.19.cloned.1.call-update) | async-done | bytes 786448 | tf_op jit(solution)/shard_map/reduce_scatter | solution.py:316
  1929.9 713.9 %reduce-scatter.17.cloned.1.call-done = f32[128,2048]{1,0:T(8,128)} async-done(((f32[4096,2048]{1,0:T(8,128)}), f32[128,2048]{1,0:T(8,128)}) %reduce-scatter.17.cloned.1.call-update) | async-done | bytes 1048592 | tf_op jit(solution)/shard_map/reduce_scatter | solution.py:366
  2643.8 747.8 %reduce-scatter.21.cloned.1.call-done = f32[336,2048]{1,0:T(8,128)} async-done(((f32[10752,2048]{1,0:T(8,128)}), f32[336,2048]{1,0:T(8,128)}) %reduce-scatter.21.cloned.1.call-update) | async-done | bytes 2752528 | tf_op jit(solution)/shard_map/reduce_scatter | solution.py:285
  3391.7 3607.5 %reduce-scatter.25.cloned.1.call-done = f32[656,2048]{1,0:T(8,128)} async-done(((f32[20992,2048]{1,0:T(8,128)}), f32[656,2048]{1,0:T(8,128)}) %reduce-scatter.25.cloned.1.call-update) | async-done | bytes 5373968
  6999.1 11.3 broadcast_select_fusion
  7010.4 2.9 slice-done.2
  7013.3 17.9 broadcast_select_fusion.1
  (265 shorter events, 35.7 us)
Async XLA Ops:
  7.2 77.9 %slice-start.3 = ((s32[1856]{0:T(1024)}), s32[192]{0:T(256)S(1)}, s32[]{:S(2)}) async-start(s32[1856]{0:T(1024)} %param.21), calls=%async_computation.23 | async-start | bytes 2048 | tf_op jit(solution)/shard_map/slice | solution.py:47
  7.2 78.1 %copy-start.43 = (s32[1856]{0:T(1024)S(1)}, s32[1856]{0:T(1024)}, u32[]{:S(2)}) copy-start(s32[1856]{0:T(1024)} %param.21) | copy-start | bytes 22276
  7.2 7.9 copy-start.57
  7.2 80.8 %copy-start.6 = (bf16[256,2048]{1,0:T(8,128)(2,1)S(1)}, bf16[256,2048]{1,0:T(8,128)(2,1)}, u32[]{:S(2)}) copy-start(bf16[256,2048]{1,0:T(8,128)(2,1)} %param.18) | copy-start | bytes 3145732
  7.2 125.7 %all-gather.8.cloned.1.call-start = ((), (), s32[]{:S(2)}) async-start(), calls=%async_computation.7 | async-start | bytes 17301504 | tf_op jit(solution)/shard_map/all_gather | solution.py:183
  15.1 201.0 %all-gather.12.cloned.1.call-start = ((), (), s32[]{:S(2)}) async-start(), calls=%async_computation.9 | async-start | bytes 1310720 | tf_op jit(solution)/shard_map/all_gather | solution.py:237
  88.9 54.3 copy-start.45
  89.1 126.6 %copy-start.21 = (f32[256,32]{0,1:T(8,128)}, f32[256,32]{0,1:T(8,128)S(1)}, u32[]{:S(2)}) copy-start(f32[256,32]{0,1:T(8,128)S(1)} %get-tuple-element.42) | copy-start | bytes 98308
  89.1 126.6 %copy-start.23 = (f32[256,32]{0,1:T(8,128)}, f32[256,32]{0,1:T(8,128)S(1)}, u32[]{:S(2)}) copy-start(f32[256,32]{0,1:T(8,128)S(1)} %get-tuple-element.43) | copy-start | bytes 98308
  89.7 53.5 copy-start.32
  173.2 71.1 %all-gather.10.cloned.1.call-start = ((), (), s32[]{:S(2)}) async-start(), calls=%async_computation.8 | async-start | bytes 1310720 | tf_op jit(solution)/shard_map/all_gather | solution.py:238
  174.0 155.0 %all-gather.14.cloned.1.call-start = ((), (), s32[]{:S(2)}) async-start(), calls=%async_computation.10 | async-start | bytes 12976128 | tf_op jit(solution)/shard_map/all_gather | solution.py:188
  175.9 399.9 %all-gather.18.cloned.1.call-start = ((), (), s32[]{:S(2)}) async-start(), calls=%async_computation.12 | async-start | bytes 45416448 | tf_op jit(solution)/shard_map/all_gather | solution.py:199
  178.5 845.4 %all-gather.16.cloned.1.call-start = ((), (), s32[]{:S(2)}) async-start(), calls=%async_computation.11 | async-start | bytes 88670208 | tf_op jit(solution)/shard_map/all_gather | solution.py:193
  182.3 1284.1 %reduce-scatter.13.cloned.1.call-start = ((), (), s32[]{:S(2)}) async-start(), calls=%async_computation.13 | async-start | bytes 2621440 | tf_op jit(solution)/shard_map/reduce_scatter | solution.py:346
  183.8 12.0 copy-start.63
  190.3 5.5 copy-start.44
  210.1 118.9 %copy-start.41 = (pred[3072]{0:T(1024)(128)(4,1)}, pred[3072]{0:T(1024)(128)(4,1)S(1)}, u32[]{:S(2)}) copy-start(pred[3072]{0:T(1024)(128)(4,1)S(1)} %compare_and_fusion.3) | copy-start | bytes 9220
  216.1 15.1 copy-start.13
  216.1 15.1 copy-start.15
  258.2 70.8 %copy-start.7 = (bf16[256,2048]{1,0:T(8,128)(2,1)S(1)}, bf16[256,2048]{1,0:T(8,128)(2,1)}, u32[]{:S(2)}) copy-start(bf16[256,2048]{1,0:T(8,128)(2,1)} %param.18) | copy-start | bytes 3145732
  258.2 70.8 %copy-start.39 = (pred[3072]{0:T(1024)(128)(4,1)S(1)}, pred[3072]{0:T(1024)(128)(4,1)}, u32[]{:S(2)}) copy-start(pred[3072]{0:T(1024)(128)(4,1)} %broadcast_in_dim.320) | copy-start | bytes 9220
  329.0 246.8 %copy-start.17 = (bf16[256,2048]{1,0:T(8,128)(2,1)S(1)}, bf16[256,2048]{1,0:T(8,128)(2,1)}, u32[]{:S(2)}) copy-start(bf16[256,2048]{1,0:T(8,128)(2,1)} %param.20) | copy-start | bytes 3145732
  339.7 993.1 %copy-start.50 = (f32[256]{0:T(256)}, f32[256]{0:T(256)S(1)}, u32[]{:S(2)}) copy-start(f32[256]{0:T(256)S(1)} %get-tuple-element.51) | copy-start | bytes 3076
  600.3 423.6 %copy-start.10 = (f32[256,2048]{1,0:T(8,128)S(1)}, f32[256,2048]{1,0:T(8,128)}, u32[]{:S(2)}) copy-start(f32[256,2048]{1,0:T(8,128)} %get-tuple-element.55) | copy-start | bytes 6291460
  600.3 423.6 %copy-start.35 = (f32[1,2048]{1,0:T(1,128)S(1)}, f32[1,2048]{1,0:T(1,128)}, u32[]{:S(2)}) copy-start(f32[1,2048]{1,0:T(1,128)} %get-tuple-element.36) | copy-start | bytes 24580
  1217.8 24.5 copy-start.27
  1242.3 52.5 copy-start.28
  1242.3 52.5 copy-start.30
  1294.8 37.9 copy-start.53
  1341.1 20.4 copy-start.25
  1384.0 28.0 copy-start.14
  1384.0 28.0 copy-start.16
  1424.2 15.4 copy-start.56
  1424.2 15.7 copy-start.26
  1424.2 15.8 copy-start.12
  1424.2 88.4 %reduce-scatter.15.cloned.1.call-start = ((), (), s32[]{:S(2)}) async-start(), calls=%async_computation.14 | async-start | bytes 2621440 | tf_op jit(solution)/shard_map/reduce_scatter | solution.py:349
  1439.6 292.9 %reduce-scatter.23.cloned.1.call-start = ((), (), s32[]{:S(2)}) async-start(), calls=%async_computation.18 | async-start | bytes 1081344
  1440.0 8.9 copy-start.22
  1440.0 8.9 copy-start.24
  1513.8 17.1 copy-start.8
  1513.8 17.1 copy-start.33
  1513.8 17.1 copy-start.46
  1530.9 14.8 copy-start.3
  1530.9 14.8 copy-start.40
  1530.9 14.8 copy-start.42
  1545.6 384.4 %reduce-scatter.19.cloned.1.call-start = ((), (), s32[]{:S(2)}) async-start(), calls=%async_computation.16 | async-start | bytes 25952256 | tf_op jit(solution)/shard_map/reduce_scatter | solution.py:316
  1557.6 1086.2 %reduce-scatter.17.cloned.1.call-start = ((), (), s32[]{:S(2)}) async-start(), calls=%async_computation.15 | async-start | bytes 34603008 | tf_op jit(solution)/shard_map/reduce_scatter | solution.py:366
  1572.1 1819.5 %reduce-scatter.21.cloned.1.call-start = ((), (), s32[]{:S(2)}) async-start(), calls=%async_computation.17 | async-start | bytes 90832896 | tf_op jit(solution)/shard_map/reduce_scatter | solution.py:285
  1573.4 28.0 copy-start.18
  1634.9 5364.3 %reduce-scatter.25.cloned.1.call-start = ((), (), s32[]{:S(2)}) async-start(), calls=%async_computation.19 | async-start | bytes 177340416
  1703.9 26.5 copy-start.65
  1703.9 26.5 copy-start.4
  1703.9 26.5 copy-start.9
  1703.9 26.5 copy-start.19
  1703.9 26.5 copy-start.34
  1703.9 26.5 copy-start.47
  1703.9 26.5 copy-start.52
  1730.4 2.9 copy-start.60
  1730.5 5280.0 %slice-start = ((s8[9961472]{0:T(1024)(128)(4,1)}), s8[1572864]{0:T(1024)(128)(4,1)S(1)}, s32[]{:S(2)}) async-start(s8[9961472]{0:T(1024)(128)(4,1)} %bitcast.135), calls=%async_computation.20 | async-start | bytes 3145728
  1733.3 5277.1 %copy-start.54 = (f32[2,64]{1,0:T(2,128)}, f32[2,64]{1,0:T(2,128)S(1)}, u32[]{:S(2)}) copy-start(f32[2,64]{1,0:T(2,128)S(1)} %copy.68) | copy-start | bytes 1540
  6999.1 11.3 slice-start.1
  6999.1 14.2 slice-start.2
  7010.4 20.8 copy-start
  (19 other events, 26.0 us)
Sparse Core Ops, SparseCore 0:
  15.2 117.6 all-gather.7
  173.4 28.3 all-gather.11
  203.3 28.5 all-gather.9
  234.6 94.3 all-gather.13
  332.2 243.5 all-gather.17
  579.1 444.8 all-gather.15
  1424.3 42.0 reduce-scatter.12
  1469.3 43.1 reduce-scatter.14
  1545.7 134.6 reduce-scatter.22
  1687.8 242.0 reduce-scatter.18
  1932.2 711.5 reduce-scatter.16
  2650.1 741.4 reduce-scatter.20
  3394.2 3604.9 reduce-scatter.24
where the time goes:
time: 7050 us; the launch traced here: 7040 us
  waiting for transfers between devices  6030 us (86%)
  matrix products  380 us (5%)
  other arithmetic  364 us (5%)
  local copies, waits for them, and re-layouts  183 us (3%)
    unnamed x15, waiting for transfers between devices  3610 us
    reduce_scatter x1, waiting for transfers between devices, shards(): lax.psum_scatter(grad_term(activated, out_cotangent, map_down, tile_rows)...  748 us
    reduce_scatter x1, waiting for transfers between devices, shards(): lax.psum_scatter(grad_term(grad_projected, normed, map_qkv, tile_rows), (...  714 us
    all_gather x1, waiting for transfers between devices, through_ffn(): lax.all_gather(shard_ffn, ('dp', 'fsdp'), axis=0, tiled=True)  361 us
    all_gather x1, waiting for transfers between devices, through_down(): lax.all_gather(shard_down, ('dp', 'fsdp'), axis=0, tiled=True)  236 us
    scatter-add x4, other arithmetic, fold(): return carry_sum.at[:, target].add(products, mode='drop')  223 us
    reduce_scatter x1, waiting for transfers between devices, shards(): lax.psum_scatter(grad_term(attended, grad_branch, map_out, tile_rows), ('...  196 us
  transfers between devices with their start and end apart: 13, of which 10 were waited for; matrix products, arithmetic and copies ran while one was open for 6% of the time, Pallas kernels for 0%

commit v1 on v0

--- a/solution.py
+++ b/solution.py
@@ -1,6 +1,9 @@
+import functools
 import math
 
 import jax
+import jax.experimental.pallas as pl
+import jax.experimental.pallas.tpu as pltpu
 import jax.numpy as jnp
 from jax import lax
 from jax.sharding import PartitionSpec as P
@@ -43,61 +46,173 @@
     return layout
 
 
-def tile_lookup(owners, first_tile, number, capacity, devices):
-    mine = owners[first_tile : first_tile + number]
-    order = jnp.arange(number, dtype=jnp.int32)
-    earlier = (mine[:, None] == mine[None, :]) & (order[None, :] < order[:, None])
-    ranked = jnp.sum(earlier.astype(jnp.int32), axis=1)
-    slot_index = mine * capacity + ranked
-    return jnp.full((devices * capacity,), -1, jnp.int32).at[slot_index].set(order)
-
-
-def tile_columns(tile_map, tile_rows):
-    filled = jnp.repeat(tile_map >= 0, tile_rows)
-    columns = (
-        jnp.maximum(tile_map, 0)[:, None] * tile_rows
-        + jnp.arange(tile_rows, dtype=jnp.int32)[None, :]
-    ).reshape(-1)
-    return (columns, filled)
-
-
-def contract_fold(left_side, tile_map, tile_rows):
-
-    def fold(carry_sum, shard_piece, offset):
-        number = shard_piece.shape[0]
-        columns, filled = tile_columns(tile_map, tile_rows)
-        picked = jnp.where(
-            filled[None, :], jnp.take(left_side, columns, axis=1), jnp.zeros((), left_side.dtype)
-        )
-        flat_piece = shard_piece.reshape(number * tile_rows, shard_piece.shape[2])
-        return jnp.dot(picked, flat_piece, preferred_element_type=jnp.float32)
-
-    return fold
-
-
-def expand_fold(right_side, tile_map, tile_rows, out_width):
-
-    def fold(carry_sum, shard_piece, offset):
-        number = shard_piece.shape[0]
-        columns, filled = tile_columns(tile_map, tile_rows)
-        target = jnp.where(filled, columns, out_width)
-        flat_piece = shard_piece.reshape(number * tile_rows, shard_piece.shape[2])
-        products = lax.dot_general(
-            right_side, flat_piece, (((1,), (1,)), ((), ())), preferred_element_type=jnp.float32
-        )
-        return carry_sum.at[:, target].add(products, mode="drop")
-
-    return fold
-
-
-def grad_term(left_side, right_side, tile_map, tile_rows):
-    columns, filled = tile_columns(tile_map, tile_rows)
-    picked = jnp.where(
-        filled[None, :], jnp.take(left_side, columns, axis=1), jnp.zeros((), left_side.dtype)
-    )
-    return lax.dot_general(
-        picked, right_side, (((0,), (0,)), ((), ())), preferred_element_type=jnp.float32
-    )
+def slot_numbers(owners, layout, caps):
+    placed = []
+    for first_tile, number, capacity, first_slot in layout:
+        mine = owners[first_tile : first_tile + number]
+        order = jnp.arange(number, dtype=jnp.int32)
+        earlier = (mine[:, None] == mine[None, :]) & (order[None, :] < order[:, None])
+        ranked = jnp.sum(earlier.astype(jnp.int32), axis=1)
+        placed.append(mine * caps + first_slot + ranked)
+    return placed
+
+
+def filled_mask(owners, layout, device):
+    masks = []
+    for first_tile, number, capacity, first_slot in layout:
+        count = jnp.sum((owners[first_tile : first_tile + number] == device).astype(jnp.int32))
+        masks.append(jnp.arange(capacity, dtype=jnp.int32) < count)
+    return jnp.concatenate(masks)
+
+
+def pick_kernel(table, wall_ref, out_ref, sem):
+    number = out_ref.shape[0]
+
+    @pl.loop(0, number)
+    def _(t):
+        pltpu.make_async_copy(wall_ref.at[table[t]], out_ref.at[t], sem).start()
+
+    pltpu.make_async_copy(out_ref, out_ref, sem).wait()
+
+
+def pick_tiles(table, wall):
+    return pl.pallas_call(
+        pick_kernel,
+        grid_spec=pltpu.PrefetchScalarGridSpec(
+            num_scalar_prefetch=1,
+            grid=(1,),
+            in_specs=[pl.BlockSpec(memory_space=pl.ANY)],
+            out_specs=pl.BlockSpec(memory_space=pl.ANY),
+            scratch_shapes=[pltpu.SemaphoreType.DMA],
+        ),
+        out_shape=jax.ShapeDtypeStruct((table.shape[0],) + wall.shape[1:], wall.dtype),
+        name="pick",
+    )(table, wall)
+
+
+def place_kernel(table, tiles_ref, old_ref, out_ref, sem):
+    number = tiles_ref.shape[0]
+
+    @pl.loop(0, number)
+    def _(t):
+        pltpu.make_async_copy(tiles_ref.at[t], out_ref.at[table[t]], sem).start()
+
+    pltpu.make_async_copy(tiles_ref, tiles_ref, sem).wait()
+
+
+def place_tiles(table, tiles, wall):
+    return pl.pallas_call(
+        place_kernel,
+        grid_spec=pltpu.PrefetchScalarGridSpec(
+            num_scalar_prefetch=1,
+            grid=(1,),
+            in_specs=[pl.BlockSpec(memory_space=pl.ANY)] * 2,
+            out_specs=pl.BlockSpec(memory_space=pl.ANY),
+            scratch_shapes=[pltpu.SemaphoreType.DMA],
+        ),
+        out_shape=jax.ShapeDtypeStruct(wall.shape, wall.dtype),
+        input_output_aliases={2: 0},
+        name="place",
+    )(table, tiles, wall)
+
+
+def ffn_kernel(group, gate_s, up_s, down_s, normed_ref, cot_ref, wall_ref, out_ref, back_ref, grads_ref, held, made, load_sem, store_sem):
+    step = pl.program_id(0)
+    steps = pl.num_programs(0)
+    tables = (gate_s, up_s, down_s)
+    tile_rows = wall_ref.shape[1]
+    width = wall_ref.shape[2]
+    rows = group * tile_rows
+
+    def fetch(at, buf):
+        for kind in range(3):
+            @pl.loop(0, group)
+            def _(t, kind=kind):
+                pltpu.make_async_copy(wall_ref.at[tables[kind][at * group + t]], held.at[buf, kind, t], load_sem.at[buf]).start()
+
+    def drain(buf):
+        pltpu.make_async_copy(made.at[buf], made.at[buf], store_sem.at[buf]).wait()
+
+    buf = lax.rem(step, 2)
+
+    @pl.when(step == 0)
+    def _():
+        fetch(0, 0)
+        out_ref[...] = jnp.zeros_like(out_ref)
+        back_ref[...] = jnp.zeros_like(back_ref)
+
+    @pl.when(step + 1 < steps)
+    def _():
+        fetch(step + 1, 1 - buf)
+
+    pltpu.make_async_copy(held.at[buf], held.at[buf], load_sem.at[buf]).wait()
+
+    @pl.when(step >= 2)
+    def _():
+        drain(buf)
+
+    normed = normed_ref[...]
+    cot = cot_ref[...]
+    w_gate = held[buf, 0].reshape(rows, width)
+    w_up = held[buf, 1].reshape(rows, width)
+    w_down = held[buf, 2].reshape(rows, width)
+    nt = (((1,), (1,)), ((), ()))
+    nn = (((1,), (0,)), ((), ()))
+    tn = (((0,), (0,)), ((), ()))
+
+    def dot(a, b, dims):
+        return lax.dot_general(a, b, dims, preferred_element_type=jnp.float32)
+
+    gate = dot(normed, w_gate, nt)
+    up = dot(normed, w_up, nt)
+    hidden = dot(cot, w_down, nt)
+    sig = jax.nn.sigmoid(gate)
+    silu = gate * sig
+    act = (silu * up).astype(jnp.bfloat16)
+    g_gate = (hidden * up * sig * (1.0 + gate * (1.0 - sig))).astype(jnp.bfloat16)
+    g_up = (hidden * silu).astype(jnp.bfloat16)
+    out_ref[...] += dot(act, w_down, nn)
+    back_ref[...] += dot(g_gate, w_gate, nn) + dot(g_up, w_up, nn)
+    made[buf, 0] = dot(g_gate, normed, tn).astype(jnp.bfloat16).reshape(group, tile_rows, width)
+    made[buf, 1] = dot(g_up, normed, tn).astype(jnp.bfloat16).reshape(group, tile_rows, width)
+    made[buf, 2] = dot(act, cot, tn).astype(jnp.bfloat16).reshape(group, tile_rows, width)
+    for kind in range(3):
+        @pl.loop(0, group)
+        def _(t, kind=kind):
+            pltpu.make_async_copy(made.at[buf, kind, t], grads_ref.at[tables[kind][step * group + t]], store_sem.at[buf]).start()
+
+    @pl.when(step == steps - 1)
+    def _():
+        drain(1 - buf)
+        drain(buf)
+
+def ffn_call(gate_s, up_s, down_s, normed, cot, wall, group=16):
+    tokens, width = normed.shape
+    steps = gate_s.shape[0] // group
+    tr = wall.shape[1]
+    full = pl.BlockSpec((tokens, width), lambda i, *_: (0, 0))
+    return pl.pallas_call(
+        functools.partial(ffn_kernel, group),
+        grid_spec=pltpu.PrefetchScalarGridSpec(
+            num_scalar_prefetch=3, grid=(steps,),
+            in_specs=[full, full, pl.BlockSpec(memory_space=pl.ANY)],
+            out_specs=[full, full, pl.BlockSpec(memory_space=pl.ANY)],
+            scratch_shapes=[pltpu.VMEM((2, 3, group, tr, width), jnp.bfloat16), pltpu.VMEM((2, 3, group, tr, width), jnp.bfloat16),
+                pltpu.SemaphoreType.DMA((2,)), pltpu.SemaphoreType.DMA((2,))]),
+        out_shape=[jax.ShapeDtypeStruct((tokens, width), jnp.float32), jax.ShapeDtypeStruct((tokens, width), jnp.float32), jax.ShapeDtypeStruct(wall.shape, jnp.bfloat16)],
+        compiler_params=pltpu.CompilerParams(vmem_limit_bytes=56 << 20, dimension_semantics=("arbitrary",)),
+        name="ffn",
+    )(gate_s, up_s, down_s, normed, cot, wall)
+
+
+def gather_slots(low_tiles):
+    return lax.all_gather(low_tiles, ("dp", "fsdp"), axis=0, tiled=True)
+
+
+def scatter_slots(grads_wall, caps):
+    return lax.psum_scatter(
+        grads_wall, ("dp", "fsdp"), scatter_dimension=0, tiled=True
+    ).astype(jnp.float32)
 
 
 def piece_labels(positions, starts):
@@ -167,37 +282,26 @@
     gain_two,
 ):
     devices = lax.axis_size("dp") * lax.axis_size("fsdp")
-    tile_rows = master.shape[1]
-    model_width = master.shape[2]
+    caps, tile_rows, model_width = master.shape
     layout = section_layout(devices, tile_rows)
-    lookups = [tile_lookup(owners, entry[0], entry[1], entry[2], devices) for entry in layout]
-    weights_low = master.astype(jnp.bfloat16)
-    shard_qkv, shard_out, shard_ffn, shard_down = [
-        weights_low[entry[3] : entry[3] + entry[2]] for entry in layout
-    ]
-    map_qkv, map_out, map_ffn, map_down = lookups
-    cap_qkv, cap_out, cap_ffn, cap_down = [entry[2] for entry in layout]
-
-    def through_qkv(fold, start_value):
-        return fold(
-            start_value, lax.all_gather(shard_qkv, ("dp", "fsdp"), axis=0, tiled=True), jnp.int32(0)
+    slot_qkv, slot_out, slot_ffn, slot_down = slot_numbers(owners, layout, caps)
+    wall = gather_slots(master.astype(jnp.bfloat16))
+    slot_attn = jnp.concatenate([slot_qkv, slot_out])
+    attn_rows = pick_tiles(slot_attn, wall).reshape(-1, model_width)
+    w_qkv = attn_rows[: slot_qkv.shape[0] * tile_rows]
+    w_out = attn_rows[slot_qkv.shape[0] * tile_rows :]
+
+    def times(left, right):
+        return jnp.dot(left, right, preferred_element_type=jnp.float32)
+
+    def times_nt(left, right):
+        return lax.dot_general(
+            left, right, (((1,), (1,)), ((), ())), preferred_element_type=jnp.float32
         )
 
-    def through_out(fold, start_value):
-        return fold(
-            start_value, lax.all_gather(shard_out, ("dp", "fsdp"), axis=0, tiled=True), jnp.int32(0)
-        )
-
-    def through_ffn(fold, start_value):
-        return fold(
-            start_value, lax.all_gather(shard_ffn, ("dp", "fsdp"), axis=0, tiled=True), jnp.int32(0)
-        )
-
-    def through_down(fold, start_value):
-        return fold(
-            start_value,
-            lax.all_gather(shard_down, ("dp", "fsdp"), axis=0, tiled=True),
-            jnp.int32(0),
+    def times_tn(left, right):
+        return lax.dot_general(
+            left, right, (((0,), (0,)), ((), ())), preferred_element_type=jnp.float32
         )
 
     gains_low = lax.all_gather(
@@ -218,10 +322,7 @@
     cosine, sine = rope_tables(query_pos.astype(jnp.float32))
     inv_one = lax.rsqrt(jnp.mean(tokens * tokens, axis=1, keepdims=True) + norm_eps)
     normed = (tokens * inv_one * gain_attn).astype(jnp.bfloat16)
-    projected = through_qkv(
-        expand_fold(normed, map_qkv, tile_rows, qkv_width),
-        jnp.zeros((local_len, qkv_width), jnp.float32),
-    )
+    projected = times_nt(normed, w_qkv)
     queries = rope_apply(
         projected[:, :model_width].reshape(local_len, HEADS, HEAD), cosine, sine
     ).astype(jnp.bfloat16)
@@ -257,50 +358,16 @@
         "kgts,skh->tkgh", probs_low, values_all, preferred_element_type=jnp.float32
     )
     attended = attended.reshape(local_len, model_width).astype(jnp.bfloat16)
-    branch = through_out(
-        contract_fold(attended, map_out, tile_rows),
-        jnp.zeros((local_len, model_width), jnp.float32),
-    )
+    branch = times(attended, w_out)
     middle = tokens + branch
     inv_two = lax.rsqrt(jnp.mean(middle * middle, axis=1, keepdims=True) + norm_eps)
     normed_two = (middle * inv_two * gain_ffn).astype(jnp.bfloat16)
-    gate_up = through_ffn(
-        expand_fold(normed_two, map_ffn, tile_rows, 2 * FF),
-        jnp.zeros((local_len, 2 * FF), jnp.float32),
-    )
-    gate_part = gate_up[:, :FF]
-    up_part = gate_up[:, FF:]
-    sigmoid_gate = jax.nn.sigmoid(gate_part)
-    silu_gate = gate_part * sigmoid_gate
-    activated = (silu_gate * up_part).astype(jnp.bfloat16)
-    ffn_out = through_down(
-        contract_fold(activated, map_down, tile_rows),
-        jnp.zeros((local_len, model_width), jnp.float32),
+    half = slot_ffn.shape[0] // 2
+    ffn_out, grad_normed_two, grads_wall = ffn_call(
+        slot_ffn[:half], slot_ffn[half:], slot_down, normed_two, out_cotangent, wall
     )
     block_out = (middle + ffn_out).astype(jnp.bfloat16)
     grad_out = out_cotangent.astype(jnp.float32)
-    grad_hidden = through_down(
-        expand_fold(out_cotangent, map_down, tile_rows, FF), jnp.zeros((local_len, FF), jnp.float32)
-    )
-    down_grads = lax.psum_scatter(
-        grad_term(activated, out_cotangent, map_down, tile_rows),
-        ("dp", "fsdp"),
-        scatter_dimension=0,
-        tiled=True,
-    )
-    grad_gate = grad_hidden * up_part * sigmoid_gate * (1.0 + gate_part * (1.0 - sigmoid_gate))
-    grad_up = grad_hidden * silu_gate
-    grad_gate_up = jnp.concatenate([grad_gate, grad_up], axis=1).astype(jnp.bfloat16)
-    grad_normed_two = through_ffn(
-        contract_fold(grad_gate_up, map_ffn, tile_rows),
-        jnp.zeros((local_len, model_width), jnp.float32),
-    )
-    ffn_grads = lax.psum_scatter(
-        grad_term(grad_gate_up, normed_two, map_ffn, tile_rows),
-        ("dp", "fsdp"),
-        scatter_dimension=0,
-        tiled=True,
-    )
     scaled_two = grad_normed_two * gain_ffn
     grad_middle = (
         grad_out
@@ -309,16 +376,7 @@
     )
     gain_two_term = jnp.sum(grad_normed_two * middle * inv_two, axis=0)
     grad_branch = grad_middle.astype(jnp.bfloat16)
-    grad_attended = through_out(
-        expand_fold(grad_branch, map_out, tile_rows, model_width),
-        jnp.zeros((local_len, model_width), jnp.float32),
-    )
-    out_grads = lax.psum_scatter(
-        grad_term(attended, grad_branch, map_out, tile_rows),
-        ("dp", "fsdp"),
-        scatter_dimension=0,
-        tiled=True,
-    )
+    grad_attended = times_nt(grad_branch, w_out)
     grad_attn_low = grad_attended.astype(jnp.bfloat16).reshape(
         local_len, KV_HEADS, group_size, HEAD
     )
@@ -359,25 +417,16 @@
     grad_projected = jnp.concatenate([grad_query_pre, grad_key_pre, grad_values], axis=1).astype(
         jnp.bfloat16
     )
-    grad_normed = through_qkv(
-        contract_fold(grad_projected, map_qkv, tile_rows),
-        jnp.zeros((local_len, model_width), jnp.float32),
-    )
-    qkv_grads = lax.psum_scatter(
-        grad_term(grad_projected, normed, map_qkv, tile_rows),
-        ("dp", "fsdp"),
-        scatter_dimension=0,
-        tiled=True,
-    )
-    weight_grad = jnp.concatenate(
+    grad_normed = times(grad_projected, w_qkv)
+    attn_grads = jnp.concatenate(
         [
-            qkv_grads.reshape(cap_qkv, tile_rows, model_width),
-            out_grads.reshape(cap_out, tile_rows, model_width),
-            ffn_grads.reshape(cap_ffn, tile_rows, model_width),
-            down_grads.reshape(cap_down, tile_rows, model_width),
-        ],
-        axis=0,
-    )
+            times_tn(grad_projected, normed).astype(jnp.bfloat16),
+            times_tn(attended, grad_branch).astype(jnp.bfloat16),
+        ]
+    ).reshape(-1, tile_rows, model_width)
+    grads_wall = place_tiles(slot_attn, attn_grads, grads_wall)
+    keep_slot = filled_mask(owners, layout, lax.axis_index(("dp", "fsdp")))[:, None, None]
+    weight_grad = jnp.where(keep_slot, scatter_slots(grads_wall, caps), 0.0)
     scaled_one = grad_normed * gain_attn
     input_grad = (
         grad_middle
@@ -388,19 +437,10 @@
     gain_grad = lax.psum_scatter(
         jnp.stack([gain_one_term, gain_two_term]), ("dp", "fsdp"), scatter_dimension=1, tiled=True
     )
-    device = lax.axis_index(("dp", "fsdp"))
-    filled_slots = jnp.concatenate(
-        [
-            lax.dynamic_slice_in_dim(lookups[index], device * layout[index][2], layout[index][2])
-            >= 0
-            for index in range(4)
-        ]
-    )
     step = float(STEP)
     new_one, new_two, new_weights = adam_step(
         master, moment_one, moment_two, weight_grad, step, decay_rate, learn_rate
     )
-    keep_slot = filled_slots[:, None, None]
     new_one = jnp.where(keep_slot, new_one, 0.0)
     new_two = jnp.where(keep_slot, new_two, 0.0)
     new_weights = jnp.where(keep_slot, new_weights, 0.0)

time: 7050 us -> 5910 us (0.84)
  waiting for transfers between devices: 6030 us -> 4120 us
  Pallas kernels: 0 us -> 1390 us
  matrix products: 380 us -> 134 us
  other arithmetic: 364 us -> 130 us
  local copies, waits for them, and re-layouts: 183 us -> 36.2 us
    reduce_scatter x3 -> x0, waiting for transfers between devices: 1660 us -> none  [the longest x1 748 us: shards(): lax.psum_scatter(grad_term(activated, out_cotangent, map_down, tile_rows)...]
    pallas_call x0 -> x3, Pallas kernels: none -> 1390 us  [the longest x1 637 us: pick_tiles(): pl.pallas_call(pick_kernel, grid_spec=pltpu.PrefetchScalarGridSpec(num_sc...]
    unnamed x15 -> x9, waiting for transfers between devices: 3610 us -> 3330 us
    dot_general x12 -> x6, matrix products: 293 us -> 45.4 us  [the longest x2 16.7 us: times(): return jnp.dot(left, right, preferred_element_type=jnp.float32)]
    scatter-add x4 -> x0, other arithmetic: 223 us -> none  [fold(): return carry_sum.at[:, target].add(products, mode='drop')]
    gather x4 -> x0, local copies, waits for them, and re-layouts: 111 us -> none  [fold(): jnp.take(left_side, columns, axis=1)]
    all_gather x4 -> x1, waiting for transfers between devices: 697 us -> 722 us  [gather_slots(): return lax.all_gather(low_tiles, ('dp', 'fsdp'), axis=0, tiled=True)]
  transfers between devices with their start and end apart: 13 -> 7, of which waited for: 10 -> 6; matrix products, arithmetic and copies ran while one was open for 6% -> 2% of each run, Pallas kernels for 0% -> 11%
where the time goes in v1:
time: 5910 us; the launch traced here: 5900 us
  waiting for transfers between devices  4120 us (70%)
  Pallas kernels  1390 us (24%)
  matrix products  134 us (2%)
  other arithmetic  130 us (2%)
  blocking collectives  74 us (1%)
    unnamed x9, waiting for transfers between devices  3330 us
    all_gather x1, waiting for transfers between devices, gather_slots(): return lax.all_gather(low_tiles, ('dp', 'fsdp'), axis=0, tiled=True)  722 us
    pallas_call x1, Pallas kernels, pick_tiles(): pl.pallas_call(pick_kernel, grid_spec=pltpu.PrefetchScalarGridSpec(num_sc...  637 us
    pallas_call x1, Pallas kernels, place_tiles(): pl.pallas_call(place_kernel, grid_spec=pltpu.PrefetchScalarGridSpec(num_s...  637 us
  transfers between devices with their start and end apart: 7, of which 6 were waited for; matrix products, arithmetic and copies ran while one was open for 2% of the time, Pallas kernels for 11%

profile of v1, /device:TPU:0, one launch (start us, length us, event | category | flops | bytes accessed | tf_op | source)
XLA Modules:
  0.0 5899.5 jit_solution(16769806696806034933)
XLA Ops:
  7.2 6.9 convert_element_type.105
  14.2 0.6 copy-done.20
  15.0 74.0 %all-gather = bf16[32,64,2]{1,2,0:T(2,128)(2,1)S(1)} all-gather(bf16[1,64,2]{1,2,0:T(2,128)(2,1)S(1)} %convert_bitcast_fusion), channel_id=1, replica_groups=mesh['dp'=8,'fsdp'=4] {'dp','fsdp'}, dimensions={0}, use_global_device_ids=true | all-gather | bytes 8448 | tf_op jit(solution)/shard_map/all_gather | solution.py:307
  89.5 0.7 fusion.34
  90.2 0.7 fusion.33
  90.9 0.6 pad_add_fusion.table
  91.9 0.5 convert_reduce_fusion
  92.4 0.6 multiply_multiply_fusion.1
  93.2 0.6 fusion.41
  93.8 722.4 %all-gather.5.cloned.1.call-done.wall_ref = bf16[2432,16,2048]{2,1,0:T(8,128)(2,1)} async-done(((bf16[76,16,2048]{2,1,0:T(8,128)(2,1)}), bf16[2432,16,2048]{2,1,0:T(8,128)(2,1)}) %all-gather.5.cloned.1.call-update) | async-done | bytes 159383568 | tf_op jit(solution)/shard_map/all_gather | solution.py:209
  816.2 637.1 %pick.1 = bf16[320,16,2048]{2,1,0:T(8,128)(2,1)} custom-call(s32[320]{0:T(512)} %pad_add_fusion.table, bf16[2432,16,2048]{2,1,0:T(8,128)(2,1)} %all-gather.5.cloned.1.call-done.wall_ref), custom_call_target="tpu_custom_call" | custom-call | tf_op jit(solution)/shard_map/pick/pallas_call | solution.py:79
  1453.3 10.7 slice.98
  1464.0 6.5 fusion.26
  1470.5 1.7 copy-done.10
  1472.5 0.7 pad_maximum_fusion.8
  1473.7 0.8 convert_reduce_fusion.4
  1474.5 1.2 convert_reduce_fusion.5
  1476.1 8.6 slice.106
  1484.7 1.8 slice.137
  1486.5 3.2 slice.103
  1489.6 1.9 copy.66
  1491.6 1.3 subtract_convert_fusion.1
  1493.2 8.6 all-gather.9.cloned.1.call-done
  1501.8 14.9 fusion.43
  1516.6 13.1 fusion.3
  1529.8 0.4 all-gather.7.cloned.1.call-done
  1530.2 1.5 copy.64
  1531.7 14.0 fusion.19
  1545.7 6.2 multiply_reduce_fusion.2
  1552.0 1.2 multiply_convert_fusion.normed_ref
  1553.2 117.5 %ffn.1 = (f32[256,2048]{1,0:T(8,128)}, f32[256,2048]{1,0:T(8,128)}, bf16[2432,16,2048]{2,1,0:T(8,128)(2,1)}) custom-call(s32[512]{0:T(512)} %get-tuple-element.62.gate_s, s32[512]{0:T(512)} %get-tuple-element.63.up_s, s32[512]{0:T(512)} %get-tuple-element.46.down_s, bf16[256,2048]{1,0:T(8,128)(2,1)} %multiply_convert_fusion.normed_ref, ...), custom_call_target="tpu_custom_call" | custom-call | tf_op jit(solution)/shard_map/ffn/pallas_call | solution.py:194
  1670.8 2.3 multiply_reduce_fusion
  1673.1 0.5 copy-done.11
  1673.6 2.9 multiply_subtract_fusion
  1676.5 7.5 convolution_convert_fusion.2
  1684.0 2.3 copy.68
  1686.3 22.5 fusion
  1708.8 27.7 fusion.2
  1736.5 12.6 bitcast_multiply_fusion.1
  1749.1 15.3 fusion.5
  1764.5 0.4 reduce-scatter.14.cloned.1.call-start
  1765.0 9.2 convolution_multiply_fusion
  1774.2 0.3 add_convert_fusion.1
  1774.5 1.1 pad_maximum_fusion.3
  1775.6 5.7 convolution_convert_fusion.1
  1781.3 11.3 reduce-scatter.10.cloned.1.call-done
  1792.6 1.1 add_convert_fusion.3
  1793.7 44.9 reduce-scatter.12.cloned.1.call-done
  1838.7 1.1 convert.45
  1839.8 10.5 fusion.18
  1850.2 8.9 convolution_convert_fusion
  1859.2 1.3 copy.80
  1860.8 22.9 pad_maximum_fusion
  1883.7 637.1 %place.1 = bf16[2432,16,2048]{2,1,0:T(8,128)(2,1)} custom-call(s32[320]{0:T(512)} %pad_add_fusion.table, bf16[320,16,2048]{2,1,0:T(8,128)(2,1)} %bitcast.84, bf16[2432,16,2048]{2,1,0:T(8,128)(2,1)} %get-tuple-element.15.old_ref), custom_call_target="tpu_custom_call", output_to_operand_aliasing={{}: (2, {})} | custom-call | tf_op jit(solution)/shard_map/place/pallas_call | solution.py:104
  2520.9 0.8 iota_compare_fusion.7
  2521.7 0.7 iota_compare_fusion.8
  2522.5 0.6 iota_compare_fusion.5
  2523.1 0.7 iota_compare_fusion.6
  2523.9 3.5 fusion.15
  2527.4 0.8 copy.81
  2528.3 0.6 multiply_add_fusion.2
  2528.9 3329.9 %reduce-scatter.16.cloned.1.call-done = bf16[76,16,2048]{2,1,0:T(8,128)(2,1)} async-done(((bf16[2432,16,2048]{2,1,0:T(8,128)(2,1)}), bf16[76,16,2048]{2,1,0:T(8,128)(2,1)}) %reduce-scatter.16.cloned.1.call-update) | async-done | bytes 4980752
  5858.8 11.5 broadcast_select_fusion
  5870.4 22.1 broadcast_select_fusion.1
  (109 shorter events, 3.3 us)
Async XLA Ops:
  7.2 809.0 %all-gather.5.cloned.1.call-start = ((), (), s32[]{:S(2)}) async-start(), calls=%async_computation.4 | async-start | bytes 164364288 | tf_op jit(solution)/shard_map/all_gather | solution.py:209
  14.1 0.7 copy-start.20
  14.1 0.8 copy-start.27
  14.1 75.2 %slice-start = ((s32[1856]{0:T(1024)}), s32[192]{0:T(256)S(1)}, s32[]{:S(2)}) async-start(s32[1856]{0:T(1024)} %param.13), calls=%async_computation.11 | async-start | bytes 2048 | tf_op jit(solution)/shard_map/slice | solution.py:52
  14.1 77.4 %copy-start.26 = (s32[1,2]{1,0:T(1,128)S(1)}, s32[1,2]{1,0:T(1,128)}, u32[]{:S(2)}) copy-start(s32[1,2]{1,0:T(1,128)} %param.11) | copy-start | bytes 28
  14.1 77.5 %copy-start.3 = (bf16[256,2048]{1,0:T(8,128)(2,1)S(1)}, bf16[256,2048]{1,0:T(8,128)(2,1)}, u32[]{:S(2)}) copy-start(bf16[256,2048]{1,0:T(8,128)(2,1)} %param.10) | copy-start | bytes 3145732
  14.2 1487.6 %all-gather.9.cloned.1.call-start = ((), (), s32[]{:S(2)}) async-start(), calls=%async_computation.6 | async-start | bytes 1310720 | tf_op jit(solution)/shard_map/all_gather | solution.py:338
  93.0 1371.0 %copy-start.21 = (f32[256]{0:T(256)}, f32[256]{0:T(256)S(1)}, u32[]{:S(2)}) copy-start(f32[256]{0:T(256)S(1)} %get-tuple-element.52) | copy-start | bytes 3076
  93.2 1398.4 %copy-start.12 = (f32[256,32]{0,1:T(8,128)}, f32[256,32]{0,1:T(8,128)S(1)}, u32[]{:S(2)}) copy-start(f32[256,32]{0,1:T(8,128)S(1)} %get-tuple-element.49) | copy-start | bytes 98308
  93.2 1398.4 %copy-start.14 = (f32[256,32]{0,1:T(8,128)}, f32[256,32]{0,1:T(8,128)S(1)}, u32[]{:S(2)}) copy-start(f32[256,32]{0,1:T(8,128)S(1)} %get-tuple-element.50) | copy-start | bytes 98308
  93.8 1370.2 %copy-start.17 = (f32[1,2048]{1,0:T(1,128)}, f32[1,2048]{1,0:T(1,128)S(1)}, u32[]{:S(2)}) copy-start(f32[1,2048]{1,0:T(1,128)S(1)} %get-tuple-element.38) | copy-start | bytes 24580
  1470.5 1.7 copy-start.10
  1473.2 57.0 all-gather.7.cloned.1.call-start
  1492.9 299.7 %reduce-scatter.10.cloned.1.call-start = ((), (), s32[]{:S(2)}) async-start(), calls=%async_computation.7 | async-start | bytes 2621440 | tf_op jit(solution)/shard_map/reduce_scatter | solution.py:404
  1531.7 14.0 copy-start.8
  1545.7 6.2 copy-start.6
  1545.7 6.3 copy-start.16
  1670.8 2.3 copy-start.5
  1670.8 2.8 copy-start.11
  1676.5 99.0 %copy-start.1 = (f32[256,2048]{1,0:T(8,128)}, f32[256,2048]{1,0:T(8,128)S(1)}, u32[]{:S(2)}) copy-start(f32[256,2048]{1,0:T(8,128)S(1)} %get-tuple-element.31) | copy-start | bytes 6291460
  1749.1 89.6 %reduce-scatter.12.cloned.1.call-start = ((), (), s32[]{:S(2)}) async-start(), calls=%async_computation.8 | async-start | bytes 2621440 | tf_op jit(solution)/shard_map/reduce_scatter | solution.py:407
  1764.5 9.7 copy-start.13
  1764.5 9.7 copy-start.15
  1764.5 762.9 %reduce-scatter.14.cloned.1.call-start = ((), (), s32[]{:S(2)}) async-start(), calls=%async_computation.9 | async-start | bytes 1081344
  1774.1 1.4 copy-start.7
  1775.6 64.2 %copy-start.18 = (f32[1,2048]{1,0:T(1,128)S(1)}, f32[1,2048]{1,0:T(1,128)}, u32[]{:S(2)}) copy-start(f32[1,2048]{1,0:T(1,128)} %copy-done.17) | copy-start | bytes 24580
  1775.6 64.2 %copy-start.22 = (f32[256]{0:T(256)S(1)}, f32[256]{0:T(256)}, u32[]{:S(2)}) copy-start(f32[256]{0:T(256)} %copy-done.21) | copy-start | bytes 3076
  1839.7 10.5 copy-start.9
  1860.6 3998.2 %reduce-scatter.16.cloned.1.call-start = ((), (), s32[]{:S(2)}) async-start(), calls=%async_computation.10 | async-start | bytes 164364288
  2520.8 3.1 copy-start.31
  2520.8 3.1 copy-start.2
  2520.8 3.1 copy-start.4
  2520.8 3.1 copy-start.19
  2520.8 3.1 copy-start.23
  2520.8 3.1 copy-start.24
  2520.9 7.4 copy-start.28
  2520.9 7.4 copy-start.29
  2520.9 7.4 copy-start.30
  2528.3 3342.1 %copy-start.25 = (f32[2,64]{1,0:T(2,128)}, f32[2,64]{1,0:T(2,128)S(1)}, u32[]{:S(2)}) copy-start(f32[2,64]{1,0:T(2,128)S(1)} %copy.81) | copy-start | bytes 1540
  5870.4 22.1 copy-start
Sparse Core Ops, SparseCore 0:
  14.3 801.8 all-gather.4
  1473.4 28.3 all-gather.8
  1503.9 26.2 all-gather.6
  1749.2 43.3 reduce-scatter.9
  1795.4 43.1 reduce-scatter.11
  1860.7 135.0 reduce-scatter.13
  2521.0 3337.7 reduce-scatter.15

commit v2 on v1

--- a/solution.py
+++ b/solution.py
@@ -82,10 +82,11 @@
             num_scalar_prefetch=1,
             grid=(1,),
             in_specs=[pl.BlockSpec(memory_space=pl.ANY)],
-            out_specs=pl.BlockSpec(memory_space=pl.ANY),
+            out_specs=pl.BlockSpec((table.shape[0],) + wall.shape[1:], lambda i, *_: (0, 0, 0)),
             scratch_shapes=[pltpu.SemaphoreType.DMA],
         ),
         out_shape=jax.ShapeDtypeStruct((table.shape[0],) + wall.shape[1:], wall.dtype),
+        compiler_params=pltpu.CompilerParams(vmem_limit_bytes=50 << 20),
         name="pick",
     )(table, wall)
 
@@ -106,12 +107,16 @@
         grid_spec=pltpu.PrefetchScalarGridSpec(
             num_scalar_prefetch=1,
             grid=(1,),
-            in_specs=[pl.BlockSpec(memory_space=pl.ANY)] * 2,
+            in_specs=[
+                pl.BlockSpec(tiles.shape, lambda i, *_: (0, 0, 0)),
+                pl.BlockSpec(memory_space=pl.ANY),
+            ],
             out_specs=pl.BlockSpec(memory_space=pl.ANY),
             scratch_shapes=[pltpu.SemaphoreType.DMA],
         ),
         out_shape=jax.ShapeDtypeStruct(wall.shape, wall.dtype),
         input_output_aliases={2: 0},
+        compiler_params=pltpu.CompilerParams(vmem_limit_bytes=50 << 20),
         name="place",
     )(table, tiles, wall)
 
@@ -205,11 +210,330 @@
     )(gate_s, up_s, down_s, normed, cot, wall)
 
 
+MESH = pl.DeviceIdType.MESH
+EVERY = slice(None)
+GATHER_ROUTES = (
+    ("z1", "z2", "z3", "x", "y", "core"),
+    ("z1", "z2", "z3", "y", "x", "core"),
+    ("x", "z1", "z2", "z3", "y", "core"),
+    ("y", "z1", "z2", "z3", "x", "core"),
+)
+
+
+def position():
+    dp = lax.axis_index("dp")
+    return dp // 4, lax.rem(dp // 2, 2), lax.rem(dp, 2), lax.axis_index("fsdp")
+
+
+def target(hop):
+    y, x, c, z = position()
+    if hop == "x":
+        x = 1 - x
+    elif hop == "y":
+        y = 1 - y
+    elif hop == "core":
+        c = 1 - c
+    elif hop == "back":
+        z = lax.rem(z + 3, 4)
+    else:
+        z = lax.rem(z + 1, 4)
+    return (y * 4 + x * 2 + c, z)
+
+
+def enter(hops):
+    barrier = pltpu.get_barrier_semaphore()
+    for hop in hops:
+        pl.semaphore_signal(barrier, inc=1, device_id=target(hop), device_id_type=MESH)
+    pl.semaphore_wait(barrier, len(hops))
+
+
+def split_slots(caps):
+    small = caps // 6
+    third = (caps - 2 * small) // 2
+    counts = (small, small, third, caps - 2 * small - third)
+    starts = (0, small, 2 * small, 2 * small + third)
+    rounds = max(2 * small + 1, counts[2], counts[3])
+    return counts, starts, rounds
+
+
+def turn(route, at, counts):
+    if route < 2:
+        live = (at >= route) & (lax.rem(at + 64 - route, 2) == 0) & (at - route < 2 * counts[route])
+        return live, (at - route) // 2
+    return (at >= 0) & (at < counts[route]), at
+
+
+def gather_kernel(mine_ref, wall_ref, own_sem, send_sem, recv_sem):
+    y, x, c, z = position()
+    counts, starts, rounds = split_slots(mine_ref.shape[0])
+    own = pltpu.make_async_copy(mine_ref, wall_ref.at[y, x, c, z], own_sem)
+    own.start()
+    enter(("x", "y", "core", "z", "back"))
+    own.wait()
+
+    def region(route, stage):
+        hops = GATHER_ROUTES[route]
+        hop = hops[stage]
+        done = hops[:stage]
+        at_y = EVERY if "y" in done else y
+        at_x = EVERY if "x" in done else x
+        at_z = EVERY if "z3" in done else z
+        if hop in ("z1", "z2", "z3"):
+            at_z = lax.rem(z + 5 - int(hop[1]), 4)
+        return at_y, at_x, c, at_z
+
+    def copy(route, stage, index):
+        view = wall_ref.at[region(route, stage) + (starts[route] + index,)]
+        return pltpu.make_async_remote_copy(
+            src_ref=view,
+            dst_ref=view,
+            send_sem=send_sem.at[route, stage],
+            recv_sem=recv_sem.at[route, stage, index],
+            device_id=target(GATHER_ROUTES[route][stage]),
+            device_id_type=MESH,
+        )
+
+    stages = len(GATHER_ROUTES[0])
+
+    @pl.loop(0, rounds + stages)
+    def _(t):
+        for stage in range(stages + 1):
+            for route in range(4):
+                live, index = turn(route, t - stage, counts)
+
+                @pl.when(live)
+                def _(stage=stage, route=route, index=index):
+                    if stage > 0:
+                        copy(route, stage - 1, index).wait()
+                    if stage < stages:
+                        copy(route, stage, index).start()
+
+
 def gather_slots(low_tiles):
+    caps, rows, width = low_tiles.shape
+    counts, starts, rounds = split_slots(caps)
+    wall = pl.pallas_call(
+        gather_kernel,
+        out_shape=jax.ShapeDtypeStruct((2, 2, 2, 4, caps, rows, width), low_tiles.dtype),
+        in_specs=[pl.BlockSpec(memory_space=pltpu.VMEM)],
+        out_specs=pl.BlockSpec(memory_space=pl.ANY),
+        scratch_shapes=[
+            pltpu.SemaphoreType.DMA,
+            pltpu.SemaphoreType.DMA((4, 6)),
+            pltpu.SemaphoreType.DMA((4, 6, max(counts))),
+        ],
+        compiler_params=pltpu.CompilerParams(collective_id=0, has_side_effects=True, vmem_limit_bytes=24 << 20),
+        name="gather_slots",
+    )(low_tiles)
+    return wall.reshape(32 * caps, rows, width)
+
+
+SCATTER_ROUTES = (
+    ("core", "y", "x", "z1", "z2", "z3", "end"),
+    ("core", "x", "y", "z1", "z2", "z3", "end"),
+    ("core", "y", "z1", "z2", "z3", "x", "end"),
+    ("core", "x", "z1", "z2", "z3", "y", "end"),
+)
+
+
+def scatter_extent(route, stage):
+    hops = SCATTER_ROUTES[route]
+    done = hops[1 : stage + 1] if hops[stage] in ("x", "y") else hops[1:stage]
+    extent = []
+    if "x" not in done or "y" not in done:
+        extent.append(2)
+    if not any(hop[0] == "z" for hop in hops[: stage + 1]):
+        extent.append(4)
+    return tuple(extent)
+
+
+def scatter_terms(route, stage):
+    hops = SCATTER_ROUTES[route]
+    done = hops[1:stage]
+    return 2 + ("x" in done) + ("y" in done) + ("z1" in done)
+
+
+def scatter_kernel(look, wall_ref, out_ref, core_ref, first_ref, second_ref, ring_ref, last_ref, *scratch):
+    y, x, c, z = position()
+    caps, rows, width = out_ref.shape
+    counts, starts, rounds = split_slots(caps)
+    stages = len(SCATTER_ROUTES[0])
+    held = {}
+    made = {}
+    scratch = list(scratch)
+    for route in range(4):
+        for stage in range(1, stages):
+            held[route, stage] = scratch.pop(0)
+            if stage < stages - 1:
+                made[route, stage] = scratch.pop(0)
+    load_sem, send_sem, recv_sem = scratch
+    enter(("x", "y", "core", "z", "back"))
+
+    def pick(hop, mine, other):
+        return other if hop else mine
+
+    def landing(route, stage, slot):
+        hops = SCATTER_ROUTES[route]
+        hop = hops[stage]
+        if hop == "core":
+            return core_ref.at[:, :, :, slot]
+        if hop[0] == "z":
+            ring = ring_ref.at[int(hop[1]) - 1]
+            return ring.at[0, slot] if route < 2 else ring.at[:, slot]
+        if stage == 1:
+            return first_ref.at[:, :, slot]
+        if stage == 2:
+            return second_ref.at[:, slot]
+        return last_ref.at[slot]
+
+    def terms(route, stage, slot):
+        hops = SCATTER_ROUTES[route]
+        hop = hops[stage]
+        done = hops[1:stage]
+        at_y = 1 - y if hop == "y" else (y if "y" in done else EVERY)
+        at_x = 1 - x if hop == "x" else (x if "x" in done else EVERY)
+        at_z = EVERY
+        if hop[0] == "z":
+            at_z = lax.rem(z + 4 - int(hop[1]), 4)
+        elif "z3" in done:
+            at_z = z
+        views = [wall_ref.at[at_y, at_x, c, at_z, slot], core_ref.at[at_y, at_x, at_z, slot]]
+        other = at_x if hops[1] == "y" else at_y
+        if stage > 1:
+            views.append(first_ref.at[other, at_z, slot])
+        if route < 2 and stage > 2:
+            views.append(second_ref.at[at_z, slot])
+        if hop in ("z2", "z3"):
+            ring = ring_ref.at[int(hop[1]) - 2]
+            views.append(ring.at[0, slot] if route < 2 else ring.at[:, slot])
+        elif "z3" in done:
+            ring = ring_ref.at[2]
+            views.append(ring.at[0, slot] if route < 2 else ring.at[other, slot])
+        if route >= 2 and hop == "end":
+            views.append(last_ref.at[slot])
+        return views
+
+    def send(route, stage, index):
+        slot = starts[route] + index
+        if stage == 0:
+            source = wall_ref.at[:, :, 1 - c, :, slot]
+        else:
+            source = made[route, stage]
+        return pltpu.make_async_remote_copy(
+            src_ref=source,
+            dst_ref=landing(route, stage, slot),
+            send_sem=send_sem.at[route, stage],
+            recv_sem=recv_sem.at[route, stage, index],
+            device_id=target(SCATTER_ROUTES[route][stage]),
+            device_id_type=MESH,
+        )
+
+    def prepare(route, stage, index):
+        if stage > 0:
+            send(route, stage - 1, index).wait()
+            for k, view in enumerate(terms(route, stage, starts[route] + index)):
+                pltpu.make_async_copy(view, held[route, stage].at[k], load_sem.at[route, stage]).start()
+
+    def finish(route, stage, index):
+        if stage > 0:
+            buf = held[route, stage]
+            pltpu.make_async_copy(buf, buf, load_sem.at[route, stage]).wait()
+            number = buf.shape[0]
+            extent = buf.shape[1:-2]
+            blocks = 1
+            for size in extent:
+                blocks *= size
+            part = min(width, 512)
+
+            @pl.loop(0, blocks)
+            def _(block):
+                if len(extent) == 2:
+                    at = (block // extent[1], lax.rem(block, extent[1]))
+                elif len(extent) == 1:
+                    at = (block,)
+                else:
+                    at = ()
+                for left in range(0, width, part):
+                    cols = pl.ds(left, part)
+                    total = buf[(0,) + at + (EVERY, cols)].astype(jnp.float32)
+                    for k in range(1, number):
+                        total += buf[(k,) + at + (EVERY, cols)].astype(jnp.float32)
+                    if stage == stages - 1:
+                        out_ref[starts[route] + index, :, cols] = total
+                    else:
+                        made[route, stage][at + (EVERY, cols)] = total.astype(made[route, stage].dtype)
+
+        if stage < stages - 1:
+            send(route, stage, index).start()
+
+    @pl.loop(0, rounds + stages - 1)
+    def _(t):
+        items = [(stage, route) for stage in range(stages - 1, -1, -1) for route in range(4)]
+
+        def run(which, work):
+            stage, route = items[which]
+            live, index = turn(route, t - stage, counts)
+
+            @pl.when(live)
+            def _():
+                work(route, stage, index)
+
+        for which in range(len(items) + look):
+            if which < len(items):
+                run(which, prepare)
+            if which >= look:
+                run(which - look, finish)
+
+
+def scatter_slots(grads_wall, caps, look=3):
+    rows, width = grads_wall.shape[1:]
+    kind = grads_wall.dtype
+    wall = grads_wall.reshape(2, 2, 2, 4, caps, rows, width)
+    counts, starts, rounds = split_slots(caps)
+    stages = len(SCATTER_ROUTES[0])
+    scratch = []
+    for route in range(4):
+        for stage in range(1, stages):
+            extent = scatter_extent(route, stage)
+            scratch.append(pltpu.VMEM((scatter_terms(route, stage),) + extent + (rows, width), kind))
+            if stage < stages - 1:
+                scratch.append(pltpu.VMEM(extent + (rows, width), kind))
+    tile = (caps, rows, width)
+    out = pl.pallas_call(
+        functools.partial(scatter_kernel, look),
+        out_shape=[
+            jax.ShapeDtypeStruct(tile, jnp.float32),
+            jax.ShapeDtypeStruct((2, 2, 4) + tile, kind),
+            jax.ShapeDtypeStruct((2, 4) + tile, kind),
+            jax.ShapeDtypeStruct((4,) + tile, kind),
+            jax.ShapeDtypeStruct((3, 2) + tile, kind),
+            jax.ShapeDtypeStruct(tile, kind),
+        ],
+        in_specs=[pl.BlockSpec(memory_space=pl.ANY)],
+        out_specs=[pl.BlockSpec(memory_space=pltpu.VMEM)] + [pl.BlockSpec(memory_space=pl.ANY)] * 5,
+        scratch_shapes=scratch
+        + [
+            pltpu.SemaphoreType.DMA((4, stages)),
+            pltpu.SemaphoreType.DMA((4, stages)),
+            pltpu.SemaphoreType.DMA((4, stages, max(counts))),
+        ],
+        compiler_params=pltpu.CompilerParams(
+            collective_id=1, has_side_effects=True, vmem_limit_bytes=56 << 20
+        ),
+        name="scatter_slots",
+    )(wall)
+    return out[0]
+
+
+def gather_any(low_tiles):
+    if (lax.axis_size("dp"), lax.axis_size("fsdp")) == (8, 4):
+        return gather_slots(low_tiles)
     return lax.all_gather(low_tiles, ("dp", "fsdp"), axis=0, tiled=True)
 
 
-def scatter_slots(grads_wall, caps):
+def scatter_any(grads_wall, caps):
+    if (lax.axis_size("dp"), lax.axis_size("fsdp")) == (8, 4):
+        return scatter_slots(grads_wall, caps)
     return lax.psum_scatter(
         grads_wall, ("dp", "fsdp"), scatter_dimension=0, tiled=True
     ).astype(jnp.float32)
@@ -285,7 +609,7 @@
     caps, tile_rows, model_width = master.shape
     layout = section_layout(devices, tile_rows)
     slot_qkv, slot_out, slot_ffn, slot_down = slot_numbers(owners, layout, caps)
-    wall = gather_slots(master.astype(jnp.bfloat16))
+    wall = gather_any(master.astype(jnp.bfloat16))
     slot_attn = jnp.concatenate([slot_qkv, slot_out])
     attn_rows = pick_tiles(slot_attn, wall).reshape(-1, model_width)
     w_qkv = attn_rows[: slot_qkv.shape[0] * tile_rows]
@@ -426,7 +750,7 @@
     ).reshape(-1, tile_rows, model_width)
     grads_wall = place_tiles(slot_attn, attn_grads, grads_wall)
     keep_slot = filled_mask(owners, layout, lax.axis_index(("dp", "fsdp")))[:, None, None]
-    weight_grad = jnp.where(keep_slot, scatter_slots(grads_wall, caps), 0.0)
+    weight_grad = jnp.where(keep_slot, scatter_any(grads_wall, caps), 0.0)
     scaled_one = grad_normed * gain_attn
     input_grad = (
         grad_middle

time: 5910 us -> 1870 us (0.32)
  waiting for transfers between devices: 4120 us -> 65.2 us
    unnamed x9 -> x6, waiting for transfers between devices: 3330 us -> 0.08 us
    pallas_call x0 -> x2, Pallas kernels: none -> 1260 us  [the longest x1 683 us: scatter_slots(): pl.pallas_call(functools.partial(scatter_kernel, look), out_shape=[jax.Sh...]
    all_gather x1 -> x0, waiting for transfers between devices: 722 us -> none  [gather_slots(): return lax.all_gather(low_tiles, ('dp', 'fsdp'), axis=0, tiled=True)]
    pallas_call x1, Pallas kernels: 637 us -> 14.6 us  [pick_tiles(): pl.pallas_call(pick_kernel, grid_spec=pltpu.PrefetchScalarGridSpec(num_sc...]
    pallas_call x1, Pallas kernels: 637 us -> 14.7 us  [place_tiles(): pl.pallas_call(place_kernel, grid_spec=pltpu.PrefetchScalarGridSpec(num_s...]
  transfers between devices with their start and end apart: 7 -> 5, of which waited for: 6 -> 4; matrix products, arithmetic and copies ran while one was open for 2% -> 8% of each run, Pallas kernels for 11% -> 38%
where the time goes in v2:
time: 1870 us; the launch traced here: 1860 us
  Pallas kernels  1400 us (75%)
  matrix products  134 us (7%)
  other arithmetic  132 us (7%)
  blocking collectives  69.3 us (4%)
  waiting for transfers between devices  65.2 us (3%)
  local copies, waits for them, and re-layouts  34.7 us (2%)
    pallas_call x1, Pallas kernels, scatter_slots(): pl.pallas_call(functools.partial(scatter_kernel, look), out_shape=[jax.Sh...  683 us
    pallas_call x1, Pallas kernels, gather_slots(): pl.pallas_call(gather_kernel, out_shape=jax.ShapeDtypeStruct((2, 2, 2, 4,...  575 us
    pallas_call x1, Pallas kernels, ffn_call(): pl.pallas_call(functools.partial(ffn_kernel, group), grid_spec=pltpu.Pref...  118 us
    all_gather x1, blocking collectives, shards(): lax.all_gather(gain_master.astype(jnp.bfloat16), ('dp', 'fsdp'), axis=1,...  69.3 us
    reduce_scatter x1, waiting for transfers between devices, shards(): lax.psum_scatter(value_terms.reshape(seq_len, kv_width), 'fsdp', scatter_...  44.9 us
  transfers between devices with their start and end apart: 5, of which 4 were waited for; matrix products, arithmetic and copies ran while one was open for 8% of the time, Pallas kernels for 38%

profile of v2, /device:TPU:0, one launch (start us, length us, event | category | flops | bytes accessed | tf_op | source)
XLA Modules:
  0.0 1855.4 jit_solution(2355620909497241696)
XLA Ops:
  7.2 0.8 slice.76
  8.0 0.7 slice.75
  8.7 0.7 convert_bitcast_fusion
  9.6 1.5 fusion.11
  11.3 1.4 fusion.34
  12.7 1.3 fusion.33
  14.0 0.6 multiply_multiply_fusion.1
  14.6 69.3 %all-gather = bf16[32,64,2]{1,2,0:T(2,128)(2,1)S(1)} all-gather(bf16[1,64,2]{1,2,0:T(2,128)(2,1)S(1)} %convert_bitcast_fusion), channel_id=1, replica_groups=mesh['dp'=8,'fsdp'=4] {'dp','fsdp'}, dimensions={0}, use_global_device_ids=true | all-gather | bytes 8448 | tf_op jit(solution)/shard_map/all_gather | solution.py:631
  83.9 0.6 fusion.41
  84.5 4.6 convert_element_type.102.mine_ref
  89.2 574.7 %gather_slots.1 = bf16[2,2,2,4,76,16,2048]{6,5,4,3,2,1,0:T(8,128)(2,1)} custom-call(bf16[76,16,2048]{2,1,0:T(8,128)(2,1)S(1)} %convert_element_type.102.mine_ref), custom_call_target="tpu_custom_call" | custom-call | tf_op jit(solution)/shard_map/gather_slots/pallas_call | solution.py:315
  664.0 14.6 pick.1
  678.6 10.8 slice.98
  689.5 6.5 fusion.26
  696.0 1.7 copy-done.8
  698.2 0.7 pad_maximum_fusion.8
  699.0 1.8 slice.137
  701.7 8.6 slice.106
  710.6 0.5 convert_reduce_fusion
  711.1 0.7 convert_reduce_fusion.4
  711.8 1.8 copy.66
  713.6 1.9 subtract_convert_fusion.1
  715.6 1.5 convert_reduce_fusion.5
  717.4 11.4 all-gather.6.cloned.1.call-done
  728.7 14.8 fusion.43
  743.5 13.1 fusion.3
  757.2 1.5 copy.64
  758.7 14.0 fusion.19
  772.7 6.2 multiply_reduce_fusion.2
  778.9 1.2 multiply_convert_fusion.normed_ref
  780.2 117.7 %ffn.1 = (f32[256,2048]{1,0:T(8,128)}, f32[256,2048]{1,0:T(8,128)}, bf16[2432,16,2048]{2,1,0:T(8,128)(2,1)}) custom-call(s32[512]{0:T(512)} %get-tuple-element.64.gate_s, s32[512]{0:T(512)} %get-tuple-element.65.up_s, s32[512]{0:T(512)} %get-tuple-element.48.down_s, bf16[256,2048]{1,0:T(8,128)(2,1)} %multiply_convert_fusion.normed_ref, ...), custom_call_target="tpu_custom_call" | custom-call | tf_op jit(solution)/shard_map/ffn/pallas_call | solution.py:199
  897.8 2.1 multiply_reduce_fusion
  900.0 3.9 multiply_subtract_fusion
  903.9 7.5 convolution_convert_fusion.2
  911.3 2.3 copy.68
  913.6 22.5 %fusion = (f32[8,4,256]{2,1,0:T(4,128)S(1)}, f32[8,1024,256,4]{2,1,3,0:T(8,128)}) fusion(f32[8,4,256,1024]{2,3,1,0:T(8,128)} %get-tuple-element.58, f32[8,4,256]{2,1,0:T(4,128)S(1)} %bitcast.114, bf16[1024,8,64,1]{0,2,3,1:T(8,128)(2,1)} %bitcast.102, bf16[256,8,4,64]{0,3,2,1:T(8,128)(2,1)} %bitcast.91), kind=kOutput, calls=%fused_computation.2 | convolution fusion | flops 1098899456 | bytes 69271552 | tf_op jit(solution)/shard_map/tkgh,skh->kgts/dot_general | solution.py:708
  936.2 27.7 %fusion.2 = bf16[8,4,256,1024]{2,3,1,0:T(8,128)(2,1)} fusion(f32[8,1024,256,4]{2,1,3,0:T(8,128)} %get-tuple-element.62, f32[8,4,256,1024]{2,3,1,0:T(8,128)} %get-tuple-element.58, f32[8,4,256]{2,1,0:T(4,128)S(1)} %get-tuple-element.61, f32[8,4,256]{2,1,0:T(4,128)S(1)} %bitcast.115), kind=kLoop, calls=%fused_computation.4 | loop fusion | flops 33554432 | bytes 83951616 | tf_op jit(solution)/shard_map/convert_element_type | solution.py:712
  963.8 12.6 bitcast_multiply_fusion.1
  976.5 15.6 fusion.5
  992.1 0.7 iota_compare_fusion.7
  992.7 0.7 iota_compare_fusion.8
  993.4 0.6 iota_compare_fusion.5
  994.0 0.6 iota_compare_fusion.6
  994.6 0.6 pad_add_fusion.1
  995.2 9.2 convolution_multiply_fusion
  1004.8 1.1 pad_maximum_fusion.3
  1005.9 5.7 convolution_convert_fusion.1
  1011.6 8.3 reduce-scatter.6.cloned.1.call-done
  1019.9 1.1 add_convert_fusion.3
  1021.1 44.9 %reduce-scatter.8.cloned.1.call-done = f32[256,512]{0,1:T(8,128)} async-done(((f32[1024,512]{0,1:T(8,128)}), f32[256,512]{0,1:T(8,128)}) %reduce-scatter.8.cloned.1.call-update) | async-done | bytes 524304 | tf_op jit(solution)/shard_map/reduce_scatter | solution.py:731
  1066.0 1.1 convert.45
  1067.1 10.0 fusion.18
  1077.0 9.2 convolution_convert_fusion
  1086.3 0.6 broadcast_multiply_fusion
  1086.8 1.3 copy.80
  1088.2 22.9 %pad_maximum_fusion = bf16[5120,2048]{1,0:T(8,128)(2,1)} fusion(bf16[2048,2048]{1,0:T(8,128)(2,1)} %convolution_convert_fusion.1, bf16[3072,2048]{1,0:T(8,128)(2,1)} %convolution_convert_fusion), kind=kLoop, calls=%fused_computation.11 | loop fusion | flops 41943040 | bytes 41943040 | tf_op jit(solution)/shard_map/concatenate | solution.py:745
  1111.1 14.7 place.1
  1125.8 682.8 %scatter_slots.1 = (f32[76,16,2048]{2,1,0:T(8,128)}, bf16[2,2,4,76,16,2048]{5,4,3,2,1,0:T(8,128)(2,1)}, bf16[2,4,76,16,2048]{4,3,2,1,0:T(8,128)(2,1)}, bf16[4,76...) custom-call(bf16[2,2,2,4,76,16,2048]{6,5,4,3,2,1,0:T(8,128)(2,1)} %bitcast.46.wall_ref), custom_call_target="tpu_custom_call" | custom-call | tf_op jit(solution)/shard_map/scatter_slots/pallas_call | solution.py:502
  1808.7 17.9 broadcast_select_fusion
  1826.6 1.4 copy-done.3
  1828.1 16.9 broadcast_select_fusion.1
  1845.1 1.9 fusion.15
  1847.0 0.8 copy.81
  1847.8 0.6 multiply_add_fusion.2
  (115 shorter events, 3.8 us)
Async XLA Ops:
  7.2 721.6 %all-gather.6.cloned.1.call-start = ((), (), s32[]{:S(2)}) async-start(), calls=%async_computation.4 | async-start | bytes 1310720 | tf_op jit(solution)/shard_map/all_gather | solution.py:662
  14.6 674.9 %copy-start.26 = (f32[256]{0:T(256)}, f32[256]{0:T(256)S(1)}, u32[]{:S(2)}) copy-start(f32[256]{0:T(256)S(1)} %get-tuple-element.54) | copy-start | bytes 3076
  84.5 604.9 %copy-start.22 = (f32[1,2048]{1,0:T(1,128)}, f32[1,2048]{1,0:T(1,128)S(1)}, u32[]{:S(2)}) copy-start(f32[1,2048]{1,0:T(1,128)S(1)} %get-tuple-element.40) | copy-start | bytes 24580
  664.0 14.6 copy-start
  678.6 10.8 copy-start.6
  689.5 11.9 copy-start.33
  689.5 12.0 copy-start.25
  696.0 1.7 copy-start.8
  698.1 15.5 copy-start.17
  698.1 15.5 copy-start.19
  699.0 58.2 %all-gather.4.cloned.1.call-start = ((), (), s32[]{:S(2)}) async-start(), calls=%async_computation.3 | async-start | bytes 1310720 | tf_op jit(solution)/shard_map/all_gather | solution.py:663
  700.8 319.1 %reduce-scatter.6.cloned.1.call-start = ((), (), s32[]{:S(2)}) async-start(), calls=%async_computation.5 | async-start | bytes 2621440 | tf_op jit(solution)/shard_map/reduce_scatter | solution.py:728
  701.7 10.1 slice-start
  715.6 28.0 %copy-start.12 = (bf16[256,32,32]{0,2,1:T(8,128)(2,1)}, bf16[256,32,32]{0,2,1:T(8,128)(2,1)S(1)}, u32[]{:S(2)}) copy-start(bf16[256,32,32]{0,2,1:T(8,128)(2,1)S(1)} %get-tuple-element.31) | copy-start | bytes 1572868
  715.6 28.0 %copy-start.13 = (bf16[256,32,32]{0,2,1:T(8,128)(2,1)}, bf16[256,32,32]{0,2,1:T(8,128)(2,1)S(1)}, u32[]{:S(2)}) copy-start(bf16[256,32,32]{0,2,1:T(8,128)(2,1)S(1)} %get-tuple-element.32) | copy-start | bytes 1572868
  758.6 14.0 copy-start.11
  772.7 7.5 copy-start.9
  772.7 6.2 copy-start.21
  780.2 119.8 %copy-start.14 = (bf16[256,2048]{1,0:T(8,128)(2,1)S(1)}, bf16[256,2048]{1,0:T(8,128)(2,1)}, u32[]{:S(2)}) copy-start(bf16[256,2048]{1,0:T(8,128)(2,1)} %cot_ref.1) | copy-start | bytes 3145732
  903.9 102.0 %copy-start.4 = (f32[256,2048]{1,0:T(8,128)}, f32[256,2048]{1,0:T(8,128)S(1)}, u32[]{:S(2)}) copy-start(f32[256,2048]{1,0:T(8,128)S(1)} %get-tuple-element.33) | copy-start | bytes 6291460
  976.4 89.6 %reduce-scatter.8.cloned.1.call-start = ((), (), s32[]{:S(2)}) async-start(), calls=%async_computation.6 | async-start | bytes 2621440 | tf_op jit(solution)/shard_map/reduce_scatter | solution.py:731
  992.0 854.9 %reduce-scatter.10.cloned.1.call-start = ((), (), s32[]{:S(2)}) async-start(), calls=%async_computation.7 | async-start | bytes 1081344
  995.2 9.2 copy-start.18
  995.2 9.2 copy-start.20
  995.2 10.7 copy-start.10
  1005.9 61.2 %copy-start.23 = (f32[1,2048]{1,0:T(1,128)S(1)}, f32[1,2048]{1,0:T(1,128)}, u32[]{:S(2)}) copy-start(f32[1,2048]{1,0:T(1,128)} %copy-done.22) | copy-start | bytes 24580
  1005.9 61.2 %copy-start.27 = (f32[256]{0:T(256)S(1)}, f32[256]{0:T(256)}, u32[]{:S(2)}) copy-start(f32[256]{0:T(256)} %copy-done.26) | copy-start | bytes 3076
  1067.1 10.0 copy-start.15
  1088.2 22.9 %copy-start.1 = (s32[320]{0:T(512)S(1)}, s32[320]{0:T(512)}, u32[]{:S(2)}) copy-start(s32[320]{0:T(512)} %copy-done) | copy-start | bytes 3844
  1125.8 682.8 %copy-start.29 = (pred[76]{0:T(512)(128)(4,1)S(1)}, pred[76]{0:T(512)(128)(4,1)}, u32[]{:S(2)}) copy-start(pred[76]{0:T(512)(128)(4,1)} %pad_add_fusion.1) | copy-start | bytes 232
  1808.6 18.0 copy-start.2
  1808.7 19.4 %copy-start.3 = (f32[76,16,2048]{2,1,0:T(8,128)S(1)}, f32[76,16,2048]{2,1,0:T(8,128)}, u32[]{:S(2)}) copy-start(f32[76,16,2048]{2,1,0:T(8,128)} %param.16) | copy-start | bytes 29884420
  1828.0 17.0 copy-start.5
  1828.0 17.0 copy-start.7
  1828.0 17.0 copy-start.16
  1828.1 17.0 copy-start.24
  1828.1 17.0 copy-start.28
  1828.1 17.0 copy-start.30
  1828.1 17.0 copy-start.31
  1828.1 19.7 %copy-start.34 = (f32[2,64]{1,0:T(2,128)S(1)}, f32[2,64]{1,0:T(2,128)}, u32[]{:S(2)}) copy-start(f32[2,64]{1,0:T(2,128)} %param.17) | copy-start | bytes 1540
  1828.1 19.7 %copy-start.35 = (f32[2,64]{1,0:T(2,128)S(1)}, f32[2,64]{1,0:T(2,128)}, u32[]{:S(2)}) copy-start(f32[2,64]{1,0:T(2,128)} %param.18) | copy-start | bytes 1540
  1828.1 19.7 %copy-start.36 = (f32[2,64]{1,0:T(2,128)S(1)}, f32[2,64]{1,0:T(2,128)}, u32[]{:S(2)}) copy-start(f32[2,64]{1,0:T(2,128)} %param.19) | copy-start | bytes 1540
  1847.8 0.6 copy-start.32
Sparse Core Ops, SparseCore 0:
  699.1 29.6 all-gather.5
  730.9 26.2 all-gather.3
  976.5 43.3 reduce-scatter.5
  1022.8 43.1 reduce-scatter.7
  1088.3 137.5 reduce-scatter.9

commit v3 on v2

--- a/solution.py
+++ b/solution.py
@@ -1,5 +1,4 @@
 import functools
-import math
 
 import jax
 import jax.experimental.pallas as pl
@@ -46,6 +45,17 @@
     return layout
 
 
+def adam_step(weights, first_moment, second_moment, grads, step, decay, rate):
+    new_one = beta_one * first_moment + (1.0 - beta_one) * grads
+    new_two = beta_two * second_moment + (1.0 - beta_two) * grads * grads
+    correct_one = 1.0 - beta_one**step
+    correct_two = 1.0 - beta_two**step
+    update = -rate * (
+        new_one / correct_one / (jnp.sqrt(new_two / correct_two) + adam_eps) + decay * weights
+    )
+    return (new_one, new_two, weights + update)
+
+
 def slot_numbers(owners, layout, caps):
     placed = []
     for first_tile, number, capacity, first_slot in layout:
@@ -65,60 +75,440 @@
     return jnp.concatenate(masks)
 
 
-def pick_kernel(table, wall_ref, out_ref, sem):
-    number = out_ref.shape[0]
-
-    @pl.loop(0, number)
+def rope_tables(positions, block):
+    half_dim = HEAD // 2
+    inverse = rope_base ** (-(jnp.arange(half_dim, dtype=jnp.float32) * 2.0 / HEAD))
+    angles = positions[:, None] * inverse[None, :]
+    cosine = jnp.cos(angles)
+    sine = jnp.sin(angles)
+    return (
+        jnp.tile(jnp.concatenate([cosine, cosine], axis=1), (1, block // HEAD)),
+        jnp.tile(jnp.concatenate([-sine, sine], axis=1), (1, block // HEAD)),
+    )
+
+
+def turn_back(grads, cosine, sine):
+    tokens, width = grads.shape
+    half_dim = HEAD // 2
+    heads = grads.reshape(tokens, width // HEAD, 2, half_dim)
+    swapped = heads[:, :, ::-1].reshape(tokens, width)
+    times = width // cosine.shape[1]
+    return grads * jnp.tile(cosine, (1, times)) - swapped * jnp.tile(sine, (1, times))
+
+
+def tuned_mesh():
+    return (lax.axis_size("dp"), lax.axis_size("fsdp")) == (8, 4)
+
+
+def gather_any(low_tiles, low_gains):
+    if tuned_mesh():
+        return gather_slots(low_tiles, low_gains)
+    return (
+        lax.all_gather(low_tiles, ("dp", "fsdp"), axis=0, tiled=True),
+        lax.all_gather(low_gains, ("dp", "fsdp"), axis=1, tiled=True),
+    )
+
+
+def scatter_any(grads_wall, caps):
+    if tuned_mesh():
+        return scatter_slots(grads_wall, caps)
+    return lax.psum_scatter(
+        grads_wall, ("dp", "fsdp"), scatter_dimension=0, tiled=True
+    ).astype(jnp.float32)
+
+
+VMEM_ASK = 56 << 20
+NT = (((1,), (1,)), ((), ()))
+NN = (((1,), (0,)), ((), ()))
+TN = (((0,), (0,)), ((), ()))
+
+
+def dot(a, b, dims):
+    return lax.dot_general(a, b, dims, preferred_element_type=jnp.float32)
+
+
+def stream_tiles(table, wall_ref, held, sem, group):
+    step = pl.program_id(0)
+    steps = pl.num_programs(0)
+    depth = held.shape[0]
+    buf = lax.rem(step, depth)
+
+    def fetch(at):
+        into = lax.rem(at, depth)
+
+        @pl.loop(0, group, unroll=True)
+        def _(t):
+            pltpu.make_async_copy(
+                wall_ref.at[table[at * group + t]], held.at[into, t], sem.at[into]
+            ).start()
+
+    @pl.when(step == 0)
+    def _():
+        for ahead in range(depth - 1):
+
+            @pl.when(ahead < steps)
+            def _(ahead=ahead):
+                fetch(jnp.int32(ahead))
+
+    @pl.when(step + depth - 1 < steps)
+    def _():
+        fetch(step + depth - 1)
+
+    pltpu.make_async_copy(held.at[buf], held.at[buf], sem.at[buf]).wait()
+    rows = group * wall_ref.shape[1]
+    return held[buf].reshape(rows, wall_ref.shape[2])
+
+
+def store_tiles(table, grads_ref, made, sem, group, value):
+    step = pl.program_id(0)
+    steps = pl.num_programs(0)
+    buf = lax.rem(step, 2)
+
+    def drain(which):
+        pltpu.make_async_copy(made.at[which], made.at[which], sem.at[which]).wait()
+
+    @pl.when(step >= 2)
+    def _():
+        drain(buf)
+
+    made[buf] = value.astype(made.dtype).reshape(made.shape[1:])
+
+    @pl.loop(0, group, unroll=True)
     def _(t):
-        pltpu.make_async_copy(wall_ref.at[table[t]], out_ref.at[t], sem).start()
-
-    pltpu.make_async_copy(out_ref, out_ref, sem).wait()
-
-
-def pick_tiles(table, wall):
+        pltpu.make_async_copy(
+            made.at[buf, t], grads_ref.at[table[step * group + t]], sem.at[buf]
+        ).start()
+
+    @pl.when(step == steps - 1)
+    def _():
+        drain(1 - buf)
+        drain(buf)
+
+
+def swap_halves(u):
+    width = u.shape[1]
+    lane = lax.broadcasted_iota(jnp.int32, u.shape, 1)
+    first = lax.rem(lane, HEAD) < HEAD // 2
+    return jnp.where(
+        first, pltpu.roll(u, width - HEAD // 2, 1), pltpu.roll(u, HEAD // 2, 1)
+    )
+
+
+def project_kernel(group, turned, table, normed_ref, cos_ref, sin_ref, wall_ref, out_ref, held, sem):
+    weights = stream_tiles(table, wall_ref, held, sem, group)
+    u = dot(normed_ref[...], weights, NT)
+    if turned is None:
+        out_ref[...] = (u * cos_ref[...] + swap_halves(u) * sin_ref[...]).astype(out_ref.dtype)
+    else:
+
+        @pl.when(pl.program_id(0) < turned)
+        def _():
+            out_ref[...] = (u * cos_ref[...] + swap_halves(u) * sin_ref[...]).astype(out_ref.dtype)
+
+        @pl.when(pl.program_id(0) >= turned)
+        def _():
+            out_ref[...] = u.astype(out_ref.dtype)
+
+
+def full_spec(shape):
+    return pl.BlockSpec(shape, lambda i, *_: (0,) * len(shape))
+
+
+def any_spec():
+    return pl.BlockSpec(memory_space=pl.ANY)
+
+
+AHEAD = 4
+
+
+def held_tiles(depth, group, wall):
+    return pltpu.VMEM((depth, group) + wall.shape[1:], wall.dtype)
+
+
+def project(table, normed, cosine, sine, wall, turned=None, group=16):
+    tokens = normed.shape[0]
+    block = group * wall.shape[1]
+    steps = table.shape[0] // group
     return pl.pallas_call(
-        pick_kernel,
+        functools.partial(project_kernel, group, turned),
         grid_spec=pltpu.PrefetchScalarGridSpec(
             num_scalar_prefetch=1,
-            grid=(1,),
-            in_specs=[pl.BlockSpec(memory_space=pl.ANY)],
-            out_specs=pl.BlockSpec((table.shape[0],) + wall.shape[1:], lambda i, *_: (0, 0, 0)),
-            scratch_shapes=[pltpu.SemaphoreType.DMA],
+            grid=(steps,),
+            in_specs=[full_spec(normed.shape), full_spec(cosine.shape), full_spec(sine.shape), any_spec()],
+            out_specs=pl.BlockSpec((tokens, block), lambda i, *_: (0, i)),
+            scratch_shapes=[held_tiles(AHEAD, group, wall), pltpu.SemaphoreType.DMA((AHEAD,))],
         ),
-        out_shape=jax.ShapeDtypeStruct((table.shape[0],) + wall.shape[1:], wall.dtype),
-        compiler_params=pltpu.CompilerParams(vmem_limit_bytes=50 << 20),
-        name="pick",
-    )(table, wall)
-
-
-def place_kernel(table, tiles_ref, old_ref, out_ref, sem):
-    number = tiles_ref.shape[0]
-
-    @pl.loop(0, number)
-    def _(t):
-        pltpu.make_async_copy(tiles_ref.at[t], out_ref.at[table[t]], sem).start()
-
-    pltpu.make_async_copy(tiles_ref, tiles_ref, sem).wait()
-
-
-def place_tiles(table, tiles, wall):
+        out_shape=jax.ShapeDtypeStruct((tokens, steps * block), jnp.bfloat16),
+        compiler_params=pltpu.CompilerParams(vmem_limit_bytes=VMEM_ASK),
+        name="project",
+    )(table, normed, cosine, sine, wall)
+
+
+def mix_kernel(group, table, left_ref, hidden_ref, gain_ref, wall_ref, middle_ref, normed_ref, held, sem):
+    step = pl.program_id(0)
+    weights = stream_tiles(table, wall_ref, held, sem, group)
+
+    @pl.when(step == 0)
+    def _():
+        middle_ref[...] = hidden_ref[...].astype(jnp.float32)
+
+    middle_ref[...] += dot(left_ref[...], weights, NN)
+
+    @pl.when(step == pl.num_programs(0) - 1)
+    def _():
+        middle = middle_ref[...]
+        inv = lax.rsqrt(jnp.mean(middle * middle, axis=1, keepdims=True) + norm_eps)
+        normed_ref[...] = (middle * inv * gain_ref[...]).astype(normed_ref.dtype)
+
+
+def mix(table, left, hidden, gain, wall, group=16):
+    tokens, width = hidden.shape
+    block = group * wall.shape[1]
     return pl.pallas_call(
-        place_kernel,
+        functools.partial(mix_kernel, group),
         grid_spec=pltpu.PrefetchScalarGridSpec(
             num_scalar_prefetch=1,
-            grid=(1,),
+            grid=(table.shape[0] // group,),
             in_specs=[
-                pl.BlockSpec(tiles.shape, lambda i, *_: (0, 0, 0)),
-                pl.BlockSpec(memory_space=pl.ANY),
+                pl.BlockSpec((tokens, block), lambda i, *_: (0, i)),
+                full_spec(hidden.shape),
+                full_spec((1, width)),
+                any_spec(),
             ],
-            out_specs=pl.BlockSpec(memory_space=pl.ANY),
-            scratch_shapes=[pltpu.SemaphoreType.DMA],
+            out_specs=[full_spec(hidden.shape), full_spec(hidden.shape)],
+            scratch_shapes=[held_tiles(AHEAD, group, wall), pltpu.SemaphoreType.DMA((AHEAD,))],
         ),
-        out_shape=jax.ShapeDtypeStruct(wall.shape, wall.dtype),
-        input_output_aliases={2: 0},
-        compiler_params=pltpu.CompilerParams(vmem_limit_bytes=50 << 20),
-        name="place",
-    )(table, tiles, wall)
+        out_shape=[
+            jax.ShapeDtypeStruct(hidden.shape, jnp.float32),
+            jax.ShapeDtypeStruct(hidden.shape, jnp.bfloat16),
+        ],
+        compiler_params=pltpu.CompilerParams(vmem_limit_bytes=VMEM_ASK),
+        name="mix",
+    )(table, left, hidden, gain.reshape(1, width), wall)
+
+
+def mix_back_kernel(group, table, left_ref, right_ref, wall_ref, old_ref, out_ref, grads_ref, held, made, load_sem, store_sem):
+    weights = stream_tiles(table, wall_ref, held, load_sem, group)
+    right = right_ref[...]
+    out_ref[...] = dot(right, weights, NT).astype(out_ref.dtype)
+    store_tiles(table, grads_ref, made, store_sem, group, dot(left_ref[...], right, TN))
+
+
+def mix_back(table, left, right, wall, grads, group=16):
+    tokens, width = right.shape
+    block = group * wall.shape[1]
+    columns = pl.BlockSpec((tokens, block), lambda i, *_: (0, i))
+    return pl.pallas_call(
+        functools.partial(mix_back_kernel, group),
+        grid_spec=pltpu.PrefetchScalarGridSpec(
+            num_scalar_prefetch=1,
+            grid=(table.shape[0] // group,),
+            in_specs=[columns, full_spec(right.shape), any_spec(), any_spec()],
+            out_specs=[columns, any_spec()],
+            scratch_shapes=[
+                held_tiles(AHEAD, group, wall),
+                held_tiles(2, group, wall),
+                pltpu.SemaphoreType.DMA((AHEAD,)),
+                pltpu.SemaphoreType.DMA((2,)),
+            ],
+        ),
+        out_shape=[
+            jax.ShapeDtypeStruct(left.shape, jnp.bfloat16),
+            jax.ShapeDtypeStruct(grads.shape, grads.dtype),
+        ],
+        input_output_aliases={4: 1},
+        compiler_params=pltpu.CompilerParams(vmem_limit_bytes=VMEM_ASK),
+        name="mix_back",
+    )(table, left, right, wall, grads)
+
+
+def project_back_kernel(group, fresh, table, left_ref, right_ref, wall_ref, old_ref, start_ref, out_ref, grads_ref, held, made, load_sem, store_sem):
+    weights = stream_tiles(table, wall_ref, held, load_sem, group)
+
+    @pl.when(pl.program_id(0) == 0)
+    def _():
+        out_ref[...] = jnp.zeros_like(out_ref) if fresh else start_ref[...]
+
+    left = left_ref[...]
+    out_ref[...] += dot(left, weights, NN)
+    store_tiles(table, grads_ref, made, store_sem, group, dot(left, right_ref[...], TN))
+
+
+def project_back(table, left, right, start, wall, grads, group=16):
+    tokens, width = right.shape
+    block = group * wall.shape[1]
+    return pl.pallas_call(
+        functools.partial(project_back_kernel, group, start is None),
+        grid_spec=pltpu.PrefetchScalarGridSpec(
+            num_scalar_prefetch=1,
+            grid=(table.shape[0] // group,),
+            in_specs=[
+                pl.BlockSpec((tokens, block), lambda i, *_: (0, i)),
+                full_spec(right.shape),
+                any_spec(),
+                any_spec(),
+                any_spec() if start is None else full_spec(start.shape),
+            ],
+            out_specs=[full_spec(right.shape), any_spec()],
+            scratch_shapes=[
+                held_tiles(AHEAD, group, wall),
+                held_tiles(2, group, wall),
+                pltpu.SemaphoreType.DMA((AHEAD,)),
+                pltpu.SemaphoreType.DMA((2,)),
+            ],
+        ),
+        out_shape=[
+            jax.ShapeDtypeStruct(right.shape, jnp.float32),
+            jax.ShapeDtypeStruct(grads.shape, grads.dtype),
+        ],
+        input_output_aliases={4: 1},
+        compiler_params=pltpu.CompilerParams(vmem_limit_bytes=VMEM_ASK),
+        name="project_back",
+    )(table, left, right, wall, grads, table if start is None else start)
+
+
+def fill_mask(places, mask_ref):
+    shape = mask_ref.shape
+    query = lax.broadcasted_iota(jnp.int32, shape, 0) + places[0]
+    key = lax.broadcasted_iota(jnp.int32, shape, 1)
+    allowed = key <= query
+    for piece in range(places.shape[0] - 1):
+        low = places[1 + piece]
+        inside_query = (query >= low) & (query < low + PIECE)
+        inside_key = (key >= low) & (key < low + PIECE)
+        allowed = allowed | (inside_query & inside_key)
+    mask_ref[...] = jnp.where(allowed, 1.0, 0.0)
+
+
+PAIR = 2
+GROUP = HEADS // KV_HEADS
+
+
+def attend_kernel(places, q_ref, k_ref, v_ref, out_ref, lse_ref, mask_ref):
+    @pl.when(pl.program_id(0) == 0)
+    def _():
+        fill_mask(places, mask_ref)
+
+    mask = mask_ref[...] > 0.5
+    lane = lax.broadcasted_iota(jnp.int32, lse_ref.shape[1:], 1)
+    logs = jnp.zeros(lse_ref.shape[1:], jnp.float32)
+    scale = jnp.bfloat16(1.0 / HEAD**0.5)
+    for side in range(PAIR):
+        k = k_ref[:, side * HEAD : (side + 1) * HEAD]
+        v = v_ref[:, side * HEAD : (side + 1) * HEAD]
+        for h in range(GROUP):
+            head = side * GROUP + h
+            cols = slice(head * HEAD, (head + 1) * HEAD)
+            scores = jnp.where(mask, dot(q_ref[:, cols] * scale, k, NT), masked_score)
+            top = jnp.max(scores, axis=1, keepdims=True)
+            raised = jnp.exp(scores - top)
+            total = jnp.sum(raised, axis=1, keepdims=True)
+            probs = (raised * (1.0 / total)).astype(jnp.bfloat16)
+            out_ref[:, cols] = dot(probs, v, NN).astype(out_ref.dtype)
+            logs = jnp.where(lane == head, top + jnp.log(total), logs)
+    lse_ref[0] = logs
+
+
+def attend(places, queries, both):
+    tokens, width = queries.shape
+    length = both.shape[0]
+    steps = KV_HEADS // PAIR
+    wide = PAIR * GROUP * HEAD
+    narrow = PAIR * HEAD
+    return pl.pallas_call(
+        attend_kernel,
+        grid_spec=pltpu.PrefetchScalarGridSpec(
+            num_scalar_prefetch=1,
+            grid=(steps,),
+            in_specs=[
+                pl.BlockSpec((tokens, wide), lambda i, *_: (0, i)),
+                pl.BlockSpec((length, narrow), lambda i, *_: (0, i)),
+                pl.BlockSpec((length, narrow), lambda i, *_: (0, steps + i)),
+            ],
+            out_specs=[
+                pl.BlockSpec((tokens, wide), lambda i, *_: (0, i)),
+                pl.BlockSpec((1, tokens, 128), lambda i, *_: (i, 0, 0)),
+            ],
+            scratch_shapes=[pltpu.VMEM((tokens, length), jnp.float32)],
+        ),
+        out_shape=[
+            jax.ShapeDtypeStruct((tokens, width), jnp.bfloat16),
+            jax.ShapeDtypeStruct((steps, tokens, 128), jnp.float32),
+        ],
+        compiler_params=pltpu.CompilerParams(vmem_limit_bytes=VMEM_ASK),
+        name="attend",
+    )(places, queries, both, both)
+
+
+def attend_back_kernel(places, q_ref, k_ref, v_ref, grad_ref, lse_ref, cos_ref, sin_ref, out_ref, both_ref, mask_ref, turn_ref):
+    @pl.when(pl.program_id(0) == 0)
+    def _():
+        fill_mask(places, mask_ref)
+
+    mask = mask_ref[...] > 0.5
+    scale = jnp.bfloat16(1.0 / HEAD**0.5)
+    for side in range(PAIR):
+        here = slice(side * HEAD, (side + 1) * HEAD)
+        k = k_ref[:, here]
+        v = v_ref[:, here]
+        dk = None
+        dv = None
+        for h in range(GROUP):
+            head = side * GROUP + h
+            cols = slice(head * HEAD, (head + 1) * HEAD)
+            q = q_ref[:, cols] * scale
+            grad = grad_ref[:, cols]
+            scores = jnp.where(mask, dot(q, k, NT), masked_score)
+            probs = jnp.exp(scores - lse_ref[0, :, head : head + 1])
+            grad_probs = dot(grad, v, NT)
+            row_dot = jnp.sum(probs * grad_probs, axis=1, keepdims=True)
+            grad_scores = (probs * (grad_probs - row_dot)).astype(jnp.bfloat16)
+            turn_ref[:, cols] = dot(grad_scores, k, NN) * (1.0 / HEAD**0.5)
+            dk_part = dot(q, grad_scores, TN)
+            dv_part = dot(grad, probs.astype(jnp.bfloat16), TN)
+            dk = dk_part if dk is None else dk + dk_part
+            dv = dv_part if dv is None else dv + dv_part
+        there = slice((PAIR + side) * HEAD, (PAIR + side + 1) * HEAD)
+        both_ref[:, here] = dk.T.astype(both_ref.dtype)
+        both_ref[:, there] = dv.T.astype(both_ref.dtype)
+    wide = cos_ref.shape[1]
+    for left in range(0, turn_ref.shape[1], wide):
+        u = turn_ref[:, left : left + wide]
+        out_ref[:, left : left + wide] = (u * cos_ref[...] - swap_halves(u) * sin_ref[...]).astype(out_ref.dtype)
+
+
+def attend_back(places, queries, both, grad, lse, cosine, sine):
+    tokens, width = queries.shape
+    length = both.shape[0]
+    steps = KV_HEADS // PAIR
+    wide = PAIR * GROUP * HEAD
+    narrow = PAIR * HEAD
+    columns = pl.BlockSpec((tokens, wide), lambda i, *_: (0, i))
+    keys = pl.BlockSpec((length, narrow), lambda i, *_: (0, i))
+    return pl.pallas_call(
+        attend_back_kernel,
+        grid_spec=pltpu.PrefetchScalarGridSpec(
+            num_scalar_prefetch=1,
+            grid=(steps,),
+            in_specs=[
+                columns,
+                keys,
+                pl.BlockSpec((length, narrow), lambda i, *_: (0, steps + i)),
+                columns,
+                pl.BlockSpec((1, tokens, 128), lambda i, *_: (i, 0, 0)),
+                full_spec(cosine.shape),
+                full_spec(sine.shape),
+            ],
+            out_specs=[columns, pl.BlockSpec((length, 2 * narrow), lambda i, *_: (0, i))],
+            scratch_shapes=[pltpu.VMEM((tokens, length), jnp.float32), pltpu.VMEM((tokens, wide), jnp.float32)],
+        ),
+        out_shape=[
+            jax.ShapeDtypeStruct((tokens, width), jnp.bfloat16),
+            jax.ShapeDtypeStruct((length, 2 * KV_HEADS * HEAD), jnp.bfloat16),
+        ],
+        compiler_params=pltpu.CompilerParams(vmem_limit_bytes=VMEM_ASK),
+        name="attend_back",
+    )(places, queries, both, both, grad, lse, cosine, sine)
 
 
 def ffn_kernel(group, gate_s, up_s, down_s, normed_ref, cot_ref, wall_ref, out_ref, back_ref, grads_ref, held, made, load_sem, store_sem):
@@ -131,7 +521,7 @@
 
     def fetch(at, buf):
         for kind in range(3):
-            @pl.loop(0, group)
+            @pl.loop(0, group, unroll=True)
             def _(t, kind=kind):
                 pltpu.make_async_copy(wall_ref.at[tables[kind][at * group + t]], held.at[buf, kind, t], load_sem.at[buf]).start()
 
@@ -182,7 +572,7 @@
     made[buf, 1] = dot(g_up, normed, tn).astype(jnp.bfloat16).reshape(group, tile_rows, width)
     made[buf, 2] = dot(act, cot, tn).astype(jnp.bfloat16).reshape(group, tile_rows, width)
     for kind in range(3):
-        @pl.loop(0, group)
+        @pl.loop(0, group, unroll=True)
         def _(t, kind=kind):
             pltpu.make_async_copy(made.at[buf, kind, t], grads_ref.at[tables[kind][step * group + t]], store_sem.at[buf]).start()
 
@@ -252,27 +642,42 @@
     third = (caps - 2 * small) // 2
     counts = (small, small, third, caps - 2 * small - third)
     starts = (0, small, 2 * small, 2 * small + third)
-    rounds = max(2 * small + 1, counts[2], counts[3])
-    return counts, starts, rounds
-
-
-def turn(route, at, counts):
+    return counts, starts
+
+
+GATHER_DELAYS = (0, 1, 0, 0)
+SCATTER_DELAYS = (4, 4, 0, 0)
+
+
+def round_count(counts, delays):
+    return max(
+        delay + (2 * count - 1 if route < 2 else count)
+        for route, (count, delay) in enumerate(zip(counts, delays))
+    )
+
+
+def turn(route, at, counts, delays):
+    at = at - delays[route]
     if route < 2:
-        live = (at >= route) & (lax.rem(at + 64 - route, 2) == 0) & (at - route < 2 * counts[route])
-        return live, (at - route) // 2
+        live = (at >= 0) & (lax.rem(at + 64, 2) == 0) & (at < 2 * counts[route])
+        return live, at // 2
     return (at >= 0) & (at < counts[route]), at
 
 
-def gather_kernel(mine_ref, wall_ref, own_sem, send_sem, recv_sem):
+def gather_kernel(mine_ref, gain_ref, wall_ref, gains_ref, own_sem, send_sem, recv_sem):
     y, x, c, z = position()
-    counts, starts, rounds = split_slots(mine_ref.shape[0])
-    own = pltpu.make_async_copy(mine_ref, wall_ref.at[y, x, c, z], own_sem)
+    counts, starts = split_slots(mine_ref.shape[0])
+    rounds = round_count(counts, GATHER_DELAYS)
+    own = pltpu.make_async_copy(mine_ref, wall_ref.at[y, x, c, z], own_sem.at[0])
+    own_gain = pltpu.make_async_copy(gain_ref, gains_ref.at[y, x, c, z], own_sem.at[1])
     own.start()
+    own_gain.start()
     enter(("x", "y", "core", "z", "back"))
     own.wait()
+    own_gain.wait()
 
     def region(route, stage):
-        hops = GATHER_ROUTES[route]
+        hops = GATHER_ROUTES[route % 4]
         hop = hops[stage]
         done = hops[:stage]
         at_y = EVERY if "y" in done else y
@@ -283,13 +688,16 @@
         return at_y, at_x, c, at_z
 
     def copy(route, stage, index):
-        view = wall_ref.at[region(route, stage) + (starts[route] + index,)]
+        if route == 4:
+            view = gains_ref.at[region(route, stage)]
+        else:
+            view = wall_ref.at[region(route, stage) + (starts[route] + index,)]
         return pltpu.make_async_remote_copy(
             src_ref=view,
             dst_ref=view,
             send_sem=send_sem.at[route, stage],
             recv_sem=recv_sem.at[route, stage, index],
-            device_id=target(GATHER_ROUTES[route][stage]),
+            device_id=target(GATHER_ROUTES[route % 4][stage]),
             device_id_type=MESH,
         )
 
@@ -298,8 +706,11 @@
     @pl.loop(0, rounds + stages)
     def _(t):
         for stage in range(stages + 1):
-            for route in range(4):
-                live, index = turn(route, t - stage, counts)
+            for route in range(5):
+                if route == 4:
+                    live, index = t == stage, 0
+                else:
+                    live, index = turn(route, t - stage, counts, GATHER_DELAYS)
 
                 @pl.when(live)
                 def _(stage=stage, route=route, index=index):
@@ -309,23 +720,33 @@
                         copy(route, stage, index).start()
 
 
-def gather_slots(low_tiles):
+def gather_slots(low_tiles, low_gains):
     caps, rows, width = low_tiles.shape
-    counts, starts, rounds = split_slots(caps)
-    wall = pl.pallas_call(
+    counts, starts = split_slots(caps)
+    kind = low_tiles.dtype
+    vmem = pl.BlockSpec(memory_space=pltpu.VMEM)
+    padded = jnp.pad(low_gains, ((0, 16 - low_gains.shape[0]), (0, 128 - low_gains.shape[1])))
+    wall, gains = pl.pallas_call(
         gather_kernel,
-        out_shape=jax.ShapeDtypeStruct((2, 2, 2, 4, caps, rows, width), low_tiles.dtype),
-        in_specs=[pl.BlockSpec(memory_space=pltpu.VMEM)],
-        out_specs=pl.BlockSpec(memory_space=pl.ANY),
+        out_shape=[
+            jax.ShapeDtypeStruct((2, 2, 2, 4, caps, rows, width), kind),
+            jax.ShapeDtypeStruct((2, 2, 2, 4) + padded.shape, kind),
+        ],
+        in_specs=[vmem, vmem],
+        out_specs=[pl.BlockSpec(memory_space=pl.ANY)] * 2,
         scratch_shapes=[
-            pltpu.SemaphoreType.DMA,
-            pltpu.SemaphoreType.DMA((4, 6)),
-            pltpu.SemaphoreType.DMA((4, 6, max(counts))),
+            pltpu.SemaphoreType.DMA((2,)),
+            pltpu.SemaphoreType.DMA((5, 6)),
+            pltpu.SemaphoreType.DMA((5, 6, max(counts))),
         ],
-        compiler_params=pltpu.CompilerParams(collective_id=0, has_side_effects=True, vmem_limit_bytes=24 << 20),
+        compiler_params=pltpu.CompilerParams(
+            collective_id=0, has_side_effects=True, vmem_limit_bytes=24 << 20
+        ),
         name="gather_slots",
-    )(low_tiles)
-    return wall.reshape(32 * caps, rows, width)
+    )(low_tiles, padded)
+    gains = gains.reshape((32,) + padded.shape)[:, : low_gains.shape[0], : low_gains.shape[1]]
+    gains = gains.transpose(1, 0, 2).reshape(low_gains.shape[0], -1)
+    return wall.reshape(32 * caps, rows, width), gains
 
 
 SCATTER_ROUTES = (
@@ -356,7 +777,8 @@
 def scatter_kernel(look, wall_ref, out_ref, core_ref, first_ref, second_ref, ring_ref, last_ref, *scratch):
     y, x, c, z = position()
     caps, rows, width = out_ref.shape
-    counts, starts, rounds = split_slots(caps)
+    counts, starts = split_slots(caps)
+    rounds = round_count(counts, SCATTER_DELAYS)
     stages = len(SCATTER_ROUTES[0])
     held = {}
     made = {}
@@ -428,11 +850,17 @@
             device_id_type=MESH,
         )
 
-    def prepare(route, stage, index):
+    def early(route, stage, index):
+        if stage > 0:
+            for k, view in enumerate(terms(route, stage, starts[route] + index)[:-1]):
+                pltpu.make_async_copy(view, held[route, stage].at[k], load_sem.at[route, stage]).start()
+
+    def late(route, stage, index):
         if stage > 0:
             send(route, stage - 1, index).wait()
-            for k, view in enumerate(terms(route, stage, starts[route] + index)):
-                pltpu.make_async_copy(view, held[route, stage].at[k], load_sem.at[route, stage]).start()
+            view = terms(route, stage, starts[route] + index)[-1]
+            last = held[route, stage].shape[0] - 1
+            pltpu.make_async_copy(view, held[route, stage].at[last], load_sem.at[route, stage]).start()
 
     def finish(route, stage, index):
         if stage > 0:
@@ -472,24 +900,27 @@
 
         def run(which, work):
             stage, route = items[which]
-            live, index = turn(route, t - stage, counts)
+            live, index = turn(route, t - stage, counts, SCATTER_DELAYS)
 
             @pl.when(live)
             def _():
                 work(route, stage, index)
 
-        for which in range(len(items) + look):
+        far, near = look
+        for which in range(len(items) + far):
             if which < len(items):
-                run(which, prepare)
-            if which >= look:
-                run(which - look, finish)
-
-
-def scatter_slots(grads_wall, caps, look=3):
+                run(which, early)
+            if far - near <= which < len(items) + far - near:
+                run(which - far + near, late)
+            if which >= far:
+                run(which - far, finish)
+
+
+def scatter_slots(grads_wall, caps, look=(4, 1)):
     rows, width = grads_wall.shape[1:]
     kind = grads_wall.dtype
     wall = grads_wall.reshape(2, 2, 2, 4, caps, rows, width)
-    counts, starts, rounds = split_slots(caps)
+    counts, starts = split_slots(caps)
     stages = len(SCATTER_ROUTES[0])
     scratch = []
     for route in range(4):
@@ -525,74 +956,6 @@
     return out[0]
 
 
-def gather_any(low_tiles):
-    if (lax.axis_size("dp"), lax.axis_size("fsdp")) == (8, 4):
-        return gather_slots(low_tiles)
-    return lax.all_gather(low_tiles, ("dp", "fsdp"), axis=0, tiled=True)
-
-
-def scatter_any(grads_wall, caps):
-    if (lax.axis_size("dp"), lax.axis_size("fsdp")) == (8, 4):
-        return scatter_slots(grads_wall, caps)
-    return lax.psum_scatter(
-        grads_wall, ("dp", "fsdp"), scatter_dimension=0, tiled=True
-    ).astype(jnp.float32)
-
-
-def piece_labels(positions, starts):
-    inside = (positions[:, None] >= starts[None, :]) & (
-        positions[:, None] < starts[None, :] + PIECE
-    )
-    labels = jnp.arange(1, starts.shape[0] + 1, dtype=jnp.int32)
-    return jnp.sum(jnp.where(inside, labels[None, :], 0), axis=1) - 1
-
-
-def attention_mask(query_pos, key_pos, starts):
-    query_label = piece_labels(query_pos, starts)
-    key_label = piece_labels(key_pos, starts)
-    causal = key_pos[None, :] <= query_pos[:, None]
-    shared = (query_label[:, None] == key_label[None, :]) & (query_label[:, None] >= 0)
-    return causal | shared
-
-
-def rope_tables(positions):
-    half_dim = HEAD // 2
-    inverse = rope_base ** (-(jnp.arange(half_dim, dtype=jnp.float32) * 2.0 / HEAD))
-    angles = positions[:, None] * inverse[None, :]
-    return (jnp.cos(angles)[:, None, :], jnp.sin(angles)[:, None, :])
-
-
-def rope_apply(values, cosine, sine):
-    half_dim = HEAD // 2
-    first_half = values[..., :half_dim]
-    second_half = values[..., half_dim:]
-    return jnp.concatenate(
-        [first_half * cosine - second_half * sine, second_half * cosine + first_half * sine],
-        axis=-1,
-    )
-
-
-def rope_back(grads, cosine, sine):
-    half_dim = HEAD // 2
-    first_half = grads[..., :half_dim]
-    second_half = grads[..., half_dim:]
-    return jnp.concatenate(
-        [first_half * cosine + second_half * sine, second_half * cosine - first_half * sine],
-        axis=-1,
-    )
-
-
-def adam_step(weights, first_moment, second_moment, grads, step, decay, rate):
-    new_one = beta_one * first_moment + (1.0 - beta_one) * grads
-    new_two = beta_two * second_moment + (1.0 - beta_two) * grads * grads
-    correct_one = 1.0 - beta_one**step
-    correct_two = 1.0 - beta_two**step
-    update = -rate * (
-        new_one / correct_one / (jnp.sqrt(new_two / correct_two) + adam_eps) + decay * weights
-    )
-    return (new_one, new_two, weights + update)
-
-
 def shards(
     hidden_in,
     piece_starts,
@@ -609,146 +972,57 @@
     caps, tile_rows, model_width = master.shape
     layout = section_layout(devices, tile_rows)
     slot_qkv, slot_out, slot_ffn, slot_down = slot_numbers(owners, layout, caps)
-    wall = gather_any(master.astype(jnp.bfloat16))
-    slot_attn = jnp.concatenate([slot_qkv, slot_out])
-    attn_rows = pick_tiles(slot_attn, wall).reshape(-1, model_width)
-    w_qkv = attn_rows[: slot_qkv.shape[0] * tile_rows]
-    w_out = attn_rows[slot_qkv.shape[0] * tile_rows :]
-
-    def times(left, right):
-        return jnp.dot(left, right, preferred_element_type=jnp.float32)
-
-    def times_nt(left, right):
-        return lax.dot_general(
-            left, right, (((1,), (1,)), ((), ())), preferred_element_type=jnp.float32
-        )
-
-    def times_tn(left, right):
-        return lax.dot_general(
-            left, right, (((0,), (0,)), ((), ())), preferred_element_type=jnp.float32
-        )
-
-    gains_low = lax.all_gather(
-        gain_master.astype(jnp.bfloat16), ("dp", "fsdp"), axis=1, tiled=True
-    ).astype(jnp.float32)
+    query_tiles = model_width // tile_rows
+    slot_query, slot_both = slot_qkv[:query_tiles], slot_qkv[query_tiles:]
+    half = slot_ffn.shape[0] // 2
+    wall, gains_low = gather_any(
+        master.astype(jnp.bfloat16), gain_master.astype(jnp.bfloat16)
+    )
+    gains_low = gains_low.astype(jnp.float32)
     gain_attn = gains_low[0]
     gain_ffn = gains_low[1]
     tokens = hidden_in.astype(jnp.float32)
     local_len = tokens.shape[0]
-    seq_len = local_len * lax.axis_size("fsdp")
-    group_size = HEADS // KV_HEADS
     kv_width = KV_HEADS * HEAD
-    qkv_width = model_width + 2 * kv_width
-    score_scale = 1.0 / math.sqrt(HEAD)
-    query_pos = lax.axis_index("fsdp") * local_len + jnp.arange(local_len, dtype=jnp.int32)
-    key_pos = jnp.arange(seq_len, dtype=jnp.int32)
-    allowed = attention_mask(query_pos, key_pos, piece_starts[0])
-    cosine, sine = rope_tables(query_pos.astype(jnp.float32))
+    first = lax.axis_index("fsdp") * local_len
+    positions = first + jnp.arange(local_len, dtype=jnp.int32)
+    places = jnp.concatenate([first[None].astype(jnp.int32), piece_starts[0]])
+    cosine, sine = rope_tables(positions.astype(jnp.float32), 16 * tile_rows)
     inv_one = lax.rsqrt(jnp.mean(tokens * tokens, axis=1, keepdims=True) + norm_eps)
     normed = (tokens * inv_one * gain_attn).astype(jnp.bfloat16)
-    projected = times_nt(normed, w_qkv)
-    queries = rope_apply(
-        projected[:, :model_width].reshape(local_len, HEADS, HEAD), cosine, sine
-    ).astype(jnp.bfloat16)
-    queries = queries.reshape(local_len, KV_HEADS, group_size, HEAD)
-    keys_local = rope_apply(
-        projected[:, model_width : model_width + kv_width].reshape(local_len, KV_HEADS, HEAD),
-        cosine,
-        sine,
-    )
-    keys_local = keys_local.astype(jnp.bfloat16).reshape(local_len, kv_width)
-    values_local = projected[:, model_width + kv_width :].astype(jnp.bfloat16)
-    keys_all, values_all = (
-        lax.all_gather(keys_local, "fsdp", axis=0, tiled=True),
-        lax.all_gather(values_local, "fsdp", axis=0, tiled=True),
-    )
-    keys_all = keys_all.reshape(seq_len, KV_HEADS, HEAD)
-    values_all = values_all.reshape(seq_len, KV_HEADS, HEAD)
-
-    def masked_scores():
-        raw = (
-            jnp.einsum("tkgh,skh->kgts", queries, keys_all, preferred_element_type=jnp.float32)
-            * score_scale
-        )
-        return jnp.where(allowed[None, None], raw, masked_score)
-
-    scores = masked_scores()
-    row_top = jnp.max(scores, axis=-1, keepdims=True)
-    shifted = jnp.exp(scores - row_top)
-    row_total = jnp.sum(shifted, axis=-1, keepdims=True)
-    log_total = row_top + jnp.log(row_total)
-    probs_low = (shifted / row_total).astype(jnp.bfloat16)
-    attended = jnp.einsum(
-        "kgts,skh->tkgh", probs_low, values_all, preferred_element_type=jnp.float32
-    )
-    attended = attended.reshape(local_len, model_width).astype(jnp.bfloat16)
-    branch = times(attended, w_out)
-    middle = tokens + branch
+    both_local = project(slot_both, normed, cosine, sine, wall, turned=kv_width // (16 * tile_rows))
+    both = lax.all_gather(both_local, "fsdp", axis=0, tiled=True)
+    queries = project(slot_query, normed, cosine, sine, wall)
+    attended, lse = attend(places, queries, both)
+    middle, normed_two = mix(slot_out, attended, hidden_in, gain_ffn, wall)
     inv_two = lax.rsqrt(jnp.mean(middle * middle, axis=1, keepdims=True) + norm_eps)
-    normed_two = (middle * inv_two * gain_ffn).astype(jnp.bfloat16)
-    half = slot_ffn.shape[0] // 2
     ffn_out, grad_normed_two, grads_wall = ffn_call(
         slot_ffn[:half], slot_ffn[half:], slot_down, normed_two, out_cotangent, wall
     )
     block_out = (middle + ffn_out).astype(jnp.bfloat16)
-    grad_out = out_cotangent.astype(jnp.float32)
     scaled_two = grad_normed_two * gain_ffn
     grad_middle = (
-        grad_out
+        out_cotangent.astype(jnp.float32)
         + inv_two * scaled_two
         - middle * inv_two**3 * jnp.mean(scaled_two * middle, axis=1, keepdims=True)
     )
     gain_two_term = jnp.sum(grad_normed_two * middle * inv_two, axis=0)
     grad_branch = grad_middle.astype(jnp.bfloat16)
-    grad_attended = times_nt(grad_branch, w_out)
-    grad_attn_low = grad_attended.astype(jnp.bfloat16).reshape(
-        local_len, KV_HEADS, group_size, HEAD
-    )
-    probs_again = jnp.exp(masked_scores() - log_total)
-    grad_probs = jnp.einsum(
-        "tkgh,skh->kgts", grad_attn_low, values_all, preferred_element_type=jnp.float32
-    )
-    row_dot = jnp.sum(probs_again * grad_probs, axis=-1, keepdims=True)
-    grad_scores = (probs_again * (grad_probs - row_dot)).astype(jnp.bfloat16)
-    grad_queries = (
-        jnp.einsum("kgts,skh->tkgh", grad_scores, keys_all, preferred_element_type=jnp.float32)
-        * score_scale
-    )
-    key_terms = (
-        jnp.einsum("kgts,tkgh->skh", grad_scores, queries, preferred_element_type=jnp.float32)
-        * score_scale
-    )
-    value_terms = jnp.einsum(
-        "kgts,tkgh->skh",
-        probs_again.astype(jnp.bfloat16),
-        grad_attn_low,
-        preferred_element_type=jnp.float32,
-    )
-    grad_keys, grad_values = (
-        lax.psum_scatter(
-            key_terms.reshape(seq_len, kv_width), "fsdp", scatter_dimension=0, tiled=True
-        ),
-        lax.psum_scatter(
-            value_terms.reshape(seq_len, kv_width), "fsdp", scatter_dimension=0, tiled=True
-        ),
-    )
-    grad_query_pre = rope_back(grad_queries.reshape(local_len, HEADS, HEAD), cosine, sine).reshape(
-        local_len, model_width
-    )
-    grad_key_pre = rope_back(grad_keys.reshape(local_len, KV_HEADS, HEAD), cosine, sine).reshape(
-        local_len, kv_width
-    )
-    grad_projected = jnp.concatenate([grad_query_pre, grad_key_pre, grad_values], axis=1).astype(
-        jnp.bfloat16
-    )
-    grad_normed = times(grad_projected, w_qkv)
-    attn_grads = jnp.concatenate(
-        [
-            times_tn(grad_projected, normed).astype(jnp.bfloat16),
-            times_tn(attended, grad_branch).astype(jnp.bfloat16),
-        ]
-    ).reshape(-1, tile_rows, model_width)
-    grads_wall = place_tiles(slot_attn, attn_grads, grads_wall)
+    grad_attended, grads_wall = mix_back(slot_out, attended, grad_branch, wall, grads_wall)
+    grad_query, both_terms = attend_back(
+        places, queries, both, grad_attended, lse, cosine, sine
+    )
+    both_sum = lax.psum_scatter(both_terms, "fsdp", scatter_dimension=0, tiled=True).astype(
+        jnp.float32
+    )
+    grad_normed, grads_wall = project_back(slot_query, grad_query, normed, None, wall, grads_wall)
+    both_sum = both_sum.reshape(local_len, KV_HEADS // PAIR, 2, PAIR * HEAD)
+    grad_key = turn_back(both_sum[:, :, 0].reshape(local_len, kv_width), cosine, sine)
+    grad_value = both_sum[:, :, 1].reshape(local_len, kv_width)
+    grad_both = jnp.concatenate([grad_key, grad_value], axis=1).astype(jnp.bfloat16)
+    grad_normed, grads_wall = project_back(
+        slot_both, grad_both, normed, grad_normed, wall, grads_wall
+    )
     keep_slot = filled_mask(owners, layout, lax.axis_index(("dp", "fsdp")))[:, None, None]
     weight_grad = jnp.where(keep_slot, scatter_any(grads_wall, caps), 0.0)
     scaled_one = grad_normed * gain_attn

time: 1870 us -> 1660 us (0.89)
  matrix products: 134 us -> 0 us
  waiting for transfers between devices: 65.2 us -> 150 us
  blocking collectives: 69.3 us -> 0 us
  other arithmetic: 132 us -> 66.5 us
  local copies, waits for them, and re-layouts: 34.7 us -> 12.1 us
    dot_general x12 -> x0, matrix products: 134 us -> none  [the longest x1 22.5 us: shards(): jnp.einsum('tkgh,skh->kgts', grad_attn_low, values_all, preferred_element...]
    pallas_call x3 -> x9, Pallas kernels: 604 us -> 708 us  [the longest x1 584 us: gather_slots(): pl.pallas_call(gather_kernel, out_shape=[jax.ShapeDtypeStruct((2, 2, 2, 4...]
    unnamed x6 -> x4, waiting for transfers between devices: 0.08 us -> 97.4 us
    pallas_call x1, Pallas kernels: 683 us -> 590 us  [scatter_slots(): pl.pallas_call(functools.partial(scatter_kernel, look), out_shape=[jax.Sh...]
    all_gather x1 -> x0, blocking collectives: 69.3 us -> none  [shards(): lax.all_gather(gain_master.astype(jnp.bfloat16), ('dp', 'fsdp'), axis=1,...]
    reduce_scatter x2 -> x1, waiting for transfers between devices: 53.2 us -> 25.2 us  [shards(): lax.psum_scatter(both_terms, 'fsdp', scatter_dimension=0, tiled=True)]
    concatenate x5 -> x3, other arithmetic: 24.8 us -> 1.54 us  [the longest x1 0.86 us: shards(): jnp.concatenate([grad_key, grad_value], axis=1).astype(jnp.bfloat16)]
    convert_element_type x5 -> x6, other arithmetic: 33.5 us -> 10.2 us  [the longest x1 4.6 us: shards(): master.astype(jnp.bfloat16)]
  transfers between devices with their start and end apart: 5 -> 3, of which waited for: 4 -> 3; matrix products, arithmetic and copies ran while one was open for 8% -> 3% of each run, Pallas kernels for 38% -> 1%
where the time goes in v3:
time: 1660 us; the launch traced here: 1640 us
  Pallas kernels  1400 us (84%)
  waiting for transfers between devices  150 us (9%)
  other arithmetic  66.5 us (4%)
    pallas_call x1, Pallas kernels, scatter_slots(): pl.pallas_call(functools.partial(scatter_kernel, look), out_shape=[jax.Sh...  590 us
    pallas_call x1, Pallas kernels, gather_slots(): pl.pallas_call(gather_kernel, out_shape=[jax.ShapeDtypeStruct((2, 2, 2, 4...  584 us
    pallas_call x1, Pallas kernels, ffn_call(): pl.pallas_call(functools.partial(ffn_kernel, group), grid_spec=pltpu.Pref...  102 us
    unnamed x4, waiting for transfers between devices  97.4 us
    pallas_call x1, Pallas kernels, attend_back(): pl.pallas_call(attend_back_kernel, grid_spec=pltpu.PrefetchScalarGridSpec...  35.8 us
  transfers between devices with their start and end apart: 3, of which 3 were waited for; matrix products, arithmetic and copies ran while one was open for 3% of the time, Pallas kernels for 1%

profile of v3, /device:TPU:0, one launch (start us, length us, event | category | flops | bytes accessed | tf_op | source)
XLA Modules:
  0.0 1644.2 jit_solution(4326533131367016462)
XLA Ops:
  7.2 0.7 slice.52
  7.9 0.2 convert_reduce_fusion.2
  8.1 4.6 convert_element_type.66.mine_ref
  12.8 584.2 %gather_slots.1 = (bf16[2,2,2,4,76,16,2048]{6,5,4,3,2,1,0:T(8,128)(2,1)}, bf16[2,2,2,4,16,128]{5,4,3,2,1,0:T(8,128)(2,1)S(1)}) custom-call(bf16[76,16,2048]{2,1,0:T(8,128)(2,1)S(1)} %convert_element_type.66.mine_ref, bf16[16,128]{1,0:T(8,128)(2,1)S(1)} %pad.4.gain_ref), custom_call_target="tpu_custom_call" | custom-call | tf_op jit(solution)/shard_map/gather_slots/pallas_call | solution.py:729
  597.1 0.3 fusion.2
  597.4 0.6 multiply_multiply_fusion.1
  598.0 0.2 fusion.13
  598.2 0.8 copy.53.cos_ref
  599.1 0.8 copy.54.sin_ref
  599.9 0.6 fusion.15
  600.6 0.6 slice.56.table
  601.2 1.3 fusion.4.normed_ref.right_ref
  602.4 6.5 project.3
  609.0 0.2 reduce-scatter.5.cloned.1.call-start
  609.2 0.1 slice.62
  609.3 0.1 slice.59
  609.4 0.1 slice.51
  609.5 0.5 slice.53.table.start_ref
  610.0 0.7 slice.58.gain_ref
  610.6 0.1 mul.232
  610.7 9.5 project.2.q_ref
  620.2 0.7 pad_add_fusion.1.places
  620.9 0.2 convert_reduce_fusion.3
  621.0 0.3 convert_reduce_fusion.1
  621.3 0.5 convert_reduce_fusion
  621.8 1.4 fusion.16
  623.2 0.7 convert_reduce_fusion.4
  623.9 1.3 convert_reduce_fusion.5
  625.2 27.3 %all-gather.2.cloned.1.call-done.k_ref.v_ref = bf16[1024,1024]{1,0:T(8,128)(2,1)} async-done(((bf16[256,1024]{1,0:T(8,128)(2,1)}), bf16[1024,1024]{1,0:T(8,128)(2,1)}) %all-gather.2.cloned.1.call-update) | async-done | bytes 2097168 | tf_op jit(solution)/shard_map/all_gather | solution.py:994
  652.5 24.9 %attend.1 = (bf16[256,2048]{1,0:T(8,128)(2,1)}, f32[4,256,128]{2,1,0:T(8,128)}) custom-call(s32[3]{0:T(128)} %pad_add_fusion.1.places, bf16[256,2048]{1,0:T(8,128)(2,1)} %project.2.q_ref, bf16[1024,1024]{1,0:T(8,128)(2,1)} %all-gather.2.cloned.1.call-done.k_ref.v_ref, bf16[1024,1024]{1,0:T(8,128)(2,1)} %all-gather.2.cloned.1.call-done.k_ref.v_ref), custom_call_target="tpu_custom_call" | custom-call | tf_op jit(solution)/shard_map/attend/pallas_call | solution.py:418
  677.4 10.7 mix.1
  688.2 1.8 multiply_reduce_fusion.2
  690.0 102.5 %ffn.1 = (f32[256,2048]{1,0:T(8,128)}, f32[256,2048]{1,0:T(8,128)}, bf16[2432,16,2048]{2,1,0:T(8,128)(2,1)}) custom-call(s32[512]{0:T(512)} %get-tuple-element.83.gate_s, s32[512]{0:T(512)} %get-tuple-element.84.up_s, s32[512]{0:T(512)} %get-tuple-element.71.down_s, bf16[256,2048]{1,0:T(8,128)(2,1)} %get-tuple-element.32.normed_ref, ...), custom_call_target="tpu_custom_call" | custom-call | tf_op jit(solution)/shard_map/ffn/pallas_call | solution.py:589
  792.5 2.9 multiply_reduce_fusion
  795.4 4.4 fusion.18
  799.8 12.7 mix_back.1
  812.4 35.8 %attend_back.1 = (bf16[256,2048]{1,0:T(8,128)(2,1)}, bf16[1024,1024]{1,0:T(8,128)(2,1)}) custom-call(s32[3]{0:T(128)} %pad_add_fusion.1.places, bf16[256,2048]{1,0:T(8,128)(2,1)} %project.2.q_ref, bf16[1024,1024]{1,0:T(8,128)(2,1)} %all-gather.2.cloned.1.call-done.k_ref.v_ref, bf16[1024,1024]{1,0:T(8,128)(2,1)} %all-gather.2.cloned.1.call-done.k_ref.v_ref, ...), custom_call_target="tpu_custom_call" | custom-call | tf_op jit(solution)/shard_map/attend_back/pallas_call | solution.py:488
  848.3 0.2 tile.40
  848.6 0.6 copy-done.7
  849.2 0.2 tile.38
  849.4 0.7 iota_compare_fusion.4
  850.1 0.7 iota_compare_fusion.5
  850.7 0.6 iota_compare_fusion.6
  851.4 0.6 iota_compare_fusion.7
  852.0 0.6 pad_add_fusion
  852.6 13.6 project_back.2
  866.2 25.2 %reduce-scatter.5.cloned.1.call-done = bf16[256,1024]{1,0:T(8,128)(2,1)} async-done(((bf16[1024,1024]{1,0:T(8,128)(2,1)}), bf16[256,1024]{1,0:T(8,128)(2,1)}) %reduce-scatter.5.cloned.1.call-update) | async-done | bytes 524304 | tf_op jit(solution)/shard_map/reduce_scatter | solution.py:1015
  891.4 1.4 reshape.120
  892.8 1.9 fusion.19
  894.7 0.5 copy.69
  895.3 0.2 copy.63
  895.5 0.2 copy.67
  895.7 0.3 subtract_convert_fusion
  896.0 0.9 pad_maximum_fusion.left_ref
  896.9 10.2 project_back.3
  907.1 2.1 fusion.9
  909.2 590.0 %scatter_slots.1 = (f32[76,16,2048]{2,1,0:T(8,128)}, bf16[2,2,4,76,16,2048]{5,4,3,2,1,0:T(8,128)(2,1)}, bf16[2,4,76,16,2048]{4,3,2,1,0:T(8,128)(2,1)}, bf16[4,76...) custom-call(bf16[2,2,2,4,76,16,2048]{6,5,4,3,2,1,0:T(8,128)(2,1)} %bitcast.12.wall_ref), custom_call_target="tpu_custom_call" | custom-call | tf_op jit(solution)/shard_map/scatter_slots/pallas_call | solution.py:933
  1499.3 1.3 copy.65
  1500.7 13.1 broadcast_select_fusion
  1513.9 22.6 %broadcast_select_fusion.1 = (f32[76,16,2048]{2,1,0:T(8,128)}, f32[76,16,2048]{2,1,0:T(8,128)}) fusion(pred[76]{0:T(512)(128)(4,1)S(1)} %copy-done.16, f32[76,16,2048]{2,1,0:T(8,128)S(1)} %get-tuple-element.54, f32[76,16,2048]{2,1,0:T(8,128)} %param.15, f32[76,16,2048]{2,1,0:T(8,128)} %param.14, f32[76,16,2048]{2,1,0:T(8,128)} %param.16), kind=kLoop, calls=%fused_computation.5 | loop fusion | flops 39845888 | bytes 59768908 | tf_op jit(solution)/shard_map/jit(_where)/select_n | solution.py:1042
  1536.5 1.9 fusion.6
  1538.4 97.3 %reduce-scatter.7.cloned.1.call-done = f32[64,2]{1,0:T(8,128)} async-done(((f32[2048,2]{1,0:T(8,128)}), f32[64,2]{1,0:T(8,128)}) %reduce-scatter.7.cloned.1.call-update) | async-done | bytes 528
  1635.7 0.8 copy.66
  1636.6 0.6 multiply_add_fusion.2
  (72 shorter events, 0.6 us)
Async XLA Ops:
  7.2 645.3 %all-gather.2.cloned.1.call-start = ((), (), s32[]{:S(2)}) async-start(), calls=%async_computation.2 | async-start | bytes 2621440 | tf_op jit(solution)/shard_map/all_gather | solution.py:994
  8.1 4.6 copy-start.19
  12.8 584.3 %copy-start.1 = (bf16[256,2048]{1,0:T(8,128)(2,1)S(1)}, bf16[256,2048]{1,0:T(8,128)(2,1)}, u32[]{:S(2)}) copy-start(bf16[256,2048]{1,0:T(8,128)(2,1)} %hidden_ref.1) | copy-start | bytes 3145732
  597.0 3.0 copy-start.13
  597.1 5.3 copy-start.10
  598.0 11.0 copy-start.14
  609.0 282.4 %reduce-scatter.5.cloned.1.call-start = ((), (), s32[]{:S(2)}) async-start(), calls=%async_computation.3 | async-start | bytes 2621440 | tf_op jit(solution)/shard_map/reduce_scatter | solution.py:1015
  610.7 9.5 copy-start.23
  690.0 102.5 %copy-start.3 = (f32[256,2048]{1,0:T(8,128)S(1)}, f32[256,2048]{1,0:T(8,128)}, u32[]{:S(2)}) copy-start(f32[256,2048]{1,0:T(8,128)} %get-tuple-element.31) | copy-start | bytes 6291460
  792.5 2.9 copy-start.6
  792.5 2.9 copy-start.9
  812.4 35.9 %copy-start.8 = (f32[256,256]{1,0:T(8,128)S(1)}, f32[256,256]{1,0:T(8,128)}, u32[]{:S(2)}) copy-start(f32[256,256]{1,0:T(8,128)} %copy.54.sin_ref) | copy-start | bytes 786436
  848.2 0.9 copy-start.7
  848.3 787.4 %reduce-scatter.7.cloned.1.call-start = ((), (), s32[]{:S(2)}) async-start(), calls=%async_computation.4 | async-start | bytes 1081344
  896.8 10.2 copy-start.2
  896.8 10.2 copy-start.11
  896.8 10.2 copy-start.15
  909.2 590.1 %copy-start.12 = (f32[2048]{0:T(1024)S(1)}, f32[2048]{0:T(1024)}, u32[]{:S(2)}) copy-start(f32[2048]{0:T(1024)} %get-tuple-element.46) | copy-start | bytes 24580
  909.2 591.5 %copy-start.16 = (pred[76]{0:T(512)(128)(4,1)S(1)}, pred[76]{0:T(512)(128)(4,1)}, u32[]{:S(2)}) copy-start(pred[76]{0:T(512)(128)(4,1)} %pad_add_fusion) | copy-start | bytes 232
  1513.8 22.6 %copy-start = (f32[76,16,2048]{2,1,0:T(8,128)}, f32[76,16,2048]{2,1,0:T(8,128)S(1)}, u32[]{:S(2)}) copy-start(f32[76,16,2048]{2,1,0:T(8,128)S(1)} %get-tuple-element.54) | copy-start | bytes 29884420
  1513.8 22.6 %copy-start.4 = (f32[256,2048]{1,0:T(8,128)S(1)}, f32[256,2048]{1,0:T(8,128)}, u32[]{:S(2)}) copy-start(f32[256,2048]{1,0:T(8,128)} %get-tuple-element.43) | copy-start | bytes 6291460
  1513.8 22.6 %copy-start.5 = (f32[256,2048]{1,0:T(8,128)S(1)}, f32[256,2048]{1,0:T(8,128)}, u32[]{:S(2)}) copy-start(f32[256,2048]{1,0:T(8,128)} %get-tuple-element.56) | copy-start | bytes 6291460
  1513.8 22.6 %copy-start.17 = (f32[256]{0:T(256)S(1)}, f32[256]{0:T(256)}, u32[]{:S(2)}) copy-start(f32[256]{0:T(256)} %get-tuple-element.77) | copy-start | bytes 3076
  1536.5 100.1 %copy-start.20 = (f32[2,64]{1,0:T(2,128)S(1)}, f32[2,64]{1,0:T(2,128)}, u32[]{:S(2)}) copy-start(f32[2,64]{1,0:T(2,128)} %param.17) | copy-start | bytes 1540
  1536.5 100.1 %copy-start.21 = (f32[2,64]{1,0:T(2,128)S(1)}, f32[2,64]{1,0:T(2,128)}, u32[]{:S(2)}) copy-start(f32[2,64]{1,0:T(2,128)} %param.18) | copy-start | bytes 1540
  1536.5 100.1 %copy-start.22 = (f32[2,64]{1,0:T(2,128)S(1)}, f32[2,64]{1,0:T(2,128)}, u32[]{:S(2)}) copy-start(f32[2,64]{1,0:T(2,128)} %param.19) | copy-start | bytes 1540
  1636.6 0.6 copy-start.18
Sparse Core Ops, SparseCore 0:
  609.1 43.3 all-gather.1
  848.4 42.9 reduce-scatter.4
  1500.8 134.8 reduce-scatter.6

commit v4 on v3

--- a/solution.py
+++ b/solution.py
@@ -109,12 +109,17 @@
     )
 
 
-def scatter_any(grads_wall, caps):
+def scatter_any(grads_wall, gain_terms, caps):
+    number = gain_terms.shape[0]
     if tuned_mesh():
-        return scatter_slots(grads_wall, caps)
-    return lax.psum_scatter(
-        grads_wall, ("dp", "fsdp"), scatter_dimension=0, tiled=True
-    ).astype(jnp.float32)
+        padded = jnp.pad(gain_terms, ((0, 8 - number), (0, 0)))
+        grads, total = scatter_slots(grads_wall, padded, caps)
+        width = gain_terms.shape[1] // 32
+        device = lax.axis_index(("dp", "fsdp"))
+        return grads, lax.dynamic_slice_in_dim(total[:number], device * width, width, 1)
+    grads = lax.psum_scatter(grads_wall, ("dp", "fsdp"), scatter_dimension=0, tiled=True)
+    gain_grad = lax.psum_scatter(gain_terms, ("dp", "fsdp"), scatter_dimension=1, tiled=True)
+    return grads.astype(jnp.float32), gain_grad
 
 
 VMEM_ASK = 56 << 20
@@ -757,6 +762,10 @@
 )
 
 
+SUM_HOPS = ("core", "x", "y", "z1", "z2", "z3")
+SUM_START = 2
+
+
 def scatter_extent(route, stage):
     hops = SCATTER_ROUTES[route]
     done = hops[1 : stage + 1] if hops[stage] in ("x", "y") else hops[1:stage]
@@ -774,7 +783,7 @@
     return 2 + ("x" in done) + ("y" in done) + ("z1" in done)
 
 
-def scatter_kernel(look, wall_ref, out_ref, core_ref, first_ref, second_ref, ring_ref, last_ref, *scratch):
+def scatter_kernel(look, wall_ref, gain_ref, out_ref, total_ref, core_ref, first_ref, second_ref, ring_ref, last_ref, *scratch):
     y, x, c, z = position()
     caps, rows, width = out_ref.shape
     counts, starts = split_slots(caps)
@@ -788,7 +797,7 @@
             held[route, stage] = scratch.pop(0)
             if stage < stages - 1:
                 made[route, stage] = scratch.pop(0)
-    load_sem, send_sem, recv_sem = scratch
+    load_sem, send_sem, recv_sem, sums, landed, sum_send, sum_recv = scratch
     enter(("x", "y", "core", "z", "back"))
 
     def pick(hop, mine, other):
@@ -894,8 +903,36 @@
         if stage < stages - 1:
             send(route, stage, index).start()
 
+    def pass_sum(hop):
+        return pltpu.make_async_remote_copy(
+            src_ref=sums.at[hop] if hop < 4 else landed.at[hop - 1],
+            dst_ref=landed.at[hop],
+            send_sem=sum_send.at[hop],
+            recv_sem=sum_recv.at[hop],
+            device_id=target(SUM_HOPS[hop]),
+            device_id_type=MESH,
+        )
+
+    def add_sums(step):
+        if step > 0:
+            pass_sum(step - 1).wait()
+        if step == 0:
+            sums[0] = gain_ref[...]
+        elif step < 4:
+            sums[step] = sums[step - 1] + landed[step - 1]
+        elif step == len(SUM_HOPS):
+            total_ref[...] = (sums[3] + landed[3]) + (landed[4] + landed[5])
+        if step < len(SUM_HOPS):
+            pass_sum(step).start()
+
     @pl.loop(0, rounds + stages - 1)
     def _(t):
+        for step in range(len(SUM_HOPS) + 1):
+
+            @pl.when(t == SUM_START + step)
+            def _(step=step):
+                add_sums(step)
+
         items = [(stage, route) for stage in range(stages - 1, -1, -1) for route in range(4)]
 
         def run(which, work):
@@ -916,7 +953,7 @@
                 run(which - far, finish)
 
 
-def scatter_slots(grads_wall, caps, look=(4, 1)):
+def scatter_slots(grads_wall, gain_terms, caps, look=(4, 1)):
     rows, width = grads_wall.shape[1:]
     kind = grads_wall.dtype
     wall = grads_wall.reshape(2, 2, 2, 4, caps, rows, width)
@@ -934,26 +971,31 @@
         functools.partial(scatter_kernel, look),
         out_shape=[
             jax.ShapeDtypeStruct(tile, jnp.float32),
+            jax.ShapeDtypeStruct(gain_terms.shape, jnp.float32),
             jax.ShapeDtypeStruct((2, 2, 4) + tile, kind),
             jax.ShapeDtypeStruct((2, 4) + tile, kind),
             jax.ShapeDtypeStruct((4,) + tile, kind),
             jax.ShapeDtypeStruct((3, 2) + tile, kind),
             jax.ShapeDtypeStruct(tile, kind),
         ],
-        in_specs=[pl.BlockSpec(memory_space=pl.ANY)],
-        out_specs=[pl.BlockSpec(memory_space=pltpu.VMEM)] + [pl.BlockSpec(memory_space=pl.ANY)] * 5,
+        in_specs=[pl.BlockSpec(memory_space=pl.ANY), pl.BlockSpec(memory_space=pltpu.VMEM)],
+        out_specs=[pl.BlockSpec(memory_space=pltpu.VMEM)] * 2 + [pl.BlockSpec(memory_space=pl.ANY)] * 5,
         scratch_shapes=scratch
         + [
             pltpu.SemaphoreType.DMA((4, stages)),
             pltpu.SemaphoreType.DMA((4, stages)),
             pltpu.SemaphoreType.DMA((4, stages, max(counts))),
+            pltpu.VMEM((4,) + gain_terms.shape, jnp.float32),
+            pltpu.VMEM((6,) + gain_terms.shape, jnp.float32),
+            pltpu.SemaphoreType.DMA((6,)),
+            pltpu.SemaphoreType.DMA((6,)),
         ],
         compiler_params=pltpu.CompilerParams(
             collective_id=1, has_side_effects=True, vmem_limit_bytes=56 << 20
         ),
         name="scatter_slots",
-    )(wall)
-    return out[0]
+    )(wall, gain_terms)
+    return out[0], out[1]
 
 
 def shards(
@@ -1024,16 +1066,16 @@
         slot_both, grad_both, normed, grad_normed, wall, grads_wall
     )
     keep_slot = filled_mask(owners, layout, lax.axis_index(("dp", "fsdp")))[:, None, None]
-    weight_grad = jnp.where(keep_slot, scatter_any(grads_wall, caps), 0.0)
+    gain_one_term = jnp.sum(grad_normed * tokens * inv_one, axis=0)
+    weight_grad, gain_grad = scatter_any(
+        grads_wall, jnp.stack([gain_one_term, gain_two_term]), caps
+    )
+    weight_grad = jnp.where(keep_slot, weight_grad, 0.0)
     scaled_one = grad_normed * gain_attn
     input_grad = (
         grad_middle
         + inv_one * scaled_one
         - tokens * inv_one**3 * jnp.mean(scaled_one * tokens, axis=1, keepdims=True)
-    )
-    gain_one_term = jnp.sum(grad_normed * tokens * inv_one, axis=0)
-    gain_grad = lax.psum_scatter(
-        jnp.stack([gain_one_term, gain_two_term]), ("dp", "fsdp"), scatter_dimension=1, tiled=True
     )
     step = float(STEP)
     new_one, new_two, new_weights = adam_step(

time: 1660 us -> 1560 us (0.940)
  waiting for transfers between devices: 150 us -> 52.7 us
    unnamed x4 -> x2, waiting for transfers between devices: 97.4 us -> 0.03 us
  transfers between devices with their start and end apart: 3 -> 2, of which waited for: 3 -> 2; matrix products, arithmetic and copies ran while one was open for 3% -> 1% of each run, Pallas kernels for 1% -> 1%
where the time goes in v4:
time: 1560 us; the launch traced here: 1550 us
  Pallas kernels  1400 us (90%)
  other arithmetic  66.7 us (4%)
  waiting for transfers between devices  52.7 us (3%)
    pallas_call x1, Pallas kernels, scatter_slots(): pl.pallas_call(functools.partial(scatter_kernel, look), out_shape=[jax.Sh...  591 us
    pallas_call x1, Pallas kernels, gather_slots(): pl.pallas_call(gather_kernel, out_shape=[jax.ShapeDtypeStruct((2, 2, 2, 4...  584 us
    pallas_call x1, Pallas kernels, ffn_call(): pl.pallas_call(functools.partial(ffn_kernel, group), grid_spec=pltpu.Pref...  103 us
    pallas_call x1, Pallas kernels, attend_back(): pl.pallas_call(attend_back_kernel, grid_spec=pltpu.PrefetchScalarGridSpec...  35.8 us
  transfers between devices with their start and end apart: 2, of which 2 were waited for; matrix products, arithmetic and copies ran while one was open for 1% of the time, Pallas kernels for 1%

profile of v4, /device:TPU:0, one launch (start us, length us, event | category | flops | bytes accessed | tf_op | source)
XLA Modules:
  0.0 1547.5 jit_solution(13855836894297496556)
XLA Ops:
  7.2 0.7 slice.55
  7.9 0.2 convert_reduce_fusion.2
  8.1 4.6 convert_element_type.68.mine_ref
  12.8 584.1 %gather_slots.1 = (bf16[2,2,2,4,76,16,2048]{6,5,4,3,2,1,0:T(8,128)(2,1)}, bf16[2,2,2,4,16,128]{5,4,3,2,1,0:T(8,128)(2,1)S(1)}) custom-call(bf16[76,16,2048]{2,1,0:T(8,128)(2,1)S(1)} %convert_element_type.68.mine_ref, bf16[16,128]{1,0:T(8,128)(2,1)S(1)} %pad.8.gain_ref), custom_call_target="tpu_custom_call" | custom-call | tf_op jit(solution)/shard_map/gather_slots/pallas_call | solution.py:734
  597.0 0.1 mul.224
  597.1 0.3 fusion.2
  597.4 0.6 multiply_multiply_fusion.1
  597.9 0.2 fusion.13
  598.2 0.8 copy.40.cos_ref
  599.1 0.8 copy.41.sin_ref
  599.9 0.6 fusion.15
  600.5 0.6 slice.59.table
  601.1 1.3 fusion.4.normed_ref.right_ref
  602.4 6.5 project.3
  609.0 0.2 reduce-scatter.2.cloned.1.call-start
  609.2 0.1 slice.65
  609.3 0.1 slice.62
  609.3 0.1 slice.54
  609.4 0.5 slice.56.table.start_ref
  609.9 0.7 slice.61.gain_ref
  610.6 0.1 mul.236
  610.7 9.5 project.2.q_ref
  620.2 0.7 pad_add_fusion.1.places
  620.8 0.2 convert_reduce_fusion.3
  621.0 0.3 convert_reduce_fusion.1
  621.3 0.5 convert_reduce_fusion
  621.8 1.4 fusion.16
  623.2 0.7 convert_reduce_fusion.4
  623.9 1.3 convert_reduce_fusion.5
  625.1 27.3 %all-gather.2.cloned.1.call-done.k_ref.v_ref = bf16[1024,1024]{1,0:T(8,128)(2,1)} async-done(((bf16[256,1024]{1,0:T(8,128)(2,1)}), bf16[1024,1024]{1,0:T(8,128)(2,1)}) %all-gather.2.cloned.1.call-update) | async-done | bytes 2097168 | tf_op jit(solution)/shard_map/all_gather | solution.py:1036
  652.4 24.9 %attend.1 = (bf16[256,2048]{1,0:T(8,128)(2,1)}, f32[4,256,128]{2,1,0:T(8,128)}) custom-call(s32[3]{0:T(128)} %pad_add_fusion.1.places, bf16[256,2048]{1,0:T(8,128)(2,1)} %project.2.q_ref, bf16[1024,1024]{1,0:T(8,128)(2,1)} %all-gather.2.cloned.1.call-done.k_ref.v_ref, bf16[1024,1024]{1,0:T(8,128)(2,1)} %all-gather.2.cloned.1.call-done.k_ref.v_ref), custom_call_target="tpu_custom_call" | custom-call | tf_op jit(solution)/shard_map/attend/pallas_call | solution.py:423
  677.4 10.7 mix.1
  688.1 1.8 multiply_reduce_fusion.2
  690.0 102.6 %ffn.1 = (f32[256,2048]{1,0:T(8,128)}, f32[256,2048]{1,0:T(8,128)}, bf16[2432,16,2048]{2,1,0:T(8,128)(2,1)}) custom-call(s32[512]{0:T(512)} %get-tuple-element.86.gate_s, s32[512]{0:T(512)} %get-tuple-element.87.up_s, s32[512]{0:T(512)} %get-tuple-element.74.down_s, bf16[256,2048]{1,0:T(8,128)(2,1)} %get-tuple-element.33.normed_ref, ...), custom_call_target="tpu_custom_call" | custom-call | tf_op jit(solution)/shard_map/ffn/pallas_call | solution.py:594
  792.6 2.9 multiply_reduce_fusion
  795.5 4.4 fusion.18
  799.9 12.7 mix_back.1
  812.6 35.8 %attend_back.1 = (bf16[256,2048]{1,0:T(8,128)(2,1)}, bf16[1024,1024]{1,0:T(8,128)(2,1)}) custom-call(s32[3]{0:T(128)} %pad_add_fusion.1.places, bf16[256,2048]{1,0:T(8,128)(2,1)} %project.2.q_ref, bf16[1024,1024]{1,0:T(8,128)(2,1)} %all-gather.2.cloned.1.call-done.k_ref.v_ref, bf16[1024,1024]{1,0:T(8,128)(2,1)} %all-gather.2.cloned.1.call-done.k_ref.v_ref, ...), custom_call_target="tpu_custom_call" | custom-call | tf_op jit(solution)/shard_map/attend_back/pallas_call | solution.py:493
  848.5 0.2 tile.40
  848.7 0.7 copy-done.7
  849.4 0.2 tile.38
  849.6 0.7 iota_compare_fusion.5
  850.3 0.7 iota_compare_fusion.6
  850.9 0.6 iota_compare_fusion.7
  851.6 0.6 iota_compare_fusion.8
  852.2 0.6 pad_add_fusion
  852.8 13.6 project_back.2
  866.4 25.3 %reduce-scatter.2.cloned.1.call-done = bf16[256,1024]{1,0:T(8,128)(2,1)} async-done(((bf16[1024,1024]{1,0:T(8,128)(2,1)}), bf16[256,1024]{1,0:T(8,128)(2,1)}) %reduce-scatter.2.cloned.1.call-update) | async-done | bytes 524304 | tf_op jit(solution)/shard_map/reduce_scatter | solution.py:1057
  891.7 1.4 reshape.120
  893.1 1.9 fusion.19
  895.0 0.5 copy.54
  895.6 0.2 copy.50
  895.8 0.2 copy.52
  896.0 0.3 subtract_convert_fusion
  896.3 0.9 pad_maximum_fusion.left_ref
  897.1 10.2 project_back.3
  907.4 2.1 fusion.9
  909.6 0.7 select_maximum_fusion.gain_ref
  910.2 591.2 %scatter_slots.1 = (f32[76,16,2048]{2,1,0:T(8,128)}, f32[8,2048]{1,0:T(8,128)}, bf16[2,2,4,76,16,2048]{5,4,3,2,1,0:T(8,128)(2,1)}, bf16[2,4,76,16,2048]{4,3,2,1,...) custom-call(bf16[2,2,2,4,76,16,2048]{6,5,4,3,2,1,0:T(8,128)(2,1)} %b, ...), custom_call_target="tpu_custom_call" | custom-call | tf_op jit(solution)/shard_map/scatter_slots/pallas_call | solution.py:970
  1501.4 0.8 slice.69
  1502.3 13.1 broadcast_select_fusion
  1515.4 22.2 %broadcast_select_fusion.1 = (f32[76,16,2048]{2,1,0:T(8,128)}, f32[76,16,2048]{2,1,0:T(8,128)}) fusion(pred[76]{0:T(512)(128)(4,1)S(1)} %copy-done.16, f32[76,16,2048]{2,1,0:T(8,128)S(1)} %get-tuple-element.57, f32[76,16,2048]{2,1,0:T(8,128)} %param.15, f32[76,16,2048]{2,1,0:T(8,128)} %param.14, f32[76,16,2048]{2,1,0:T(8,128)} %param.16), kind=kLoop, calls=%fused_computation.5 | loop fusion | flops 39845888 | bytes 59768908 | tf_op jit(solution)/shard_map/jit(_where)/select_n | solution.py:1084
  1537.7 1.9 fusion.6
  1539.6 0.7 multiply_add_fusion.2
  (66 shorter events, 0.5 us)
Async XLA Ops:
  7.2 645.3 %all-gather.2.cloned.1.call-start = ((), (), s32[]{:S(2)}) async-start(), calls=%async_computation.1 | async-start | bytes 2621440 | tf_op jit(solution)/shard_map/all_gather | solution.py:1036
  8.1 4.6 copy-start.18
  12.8 584.3 %copy-start.1 = (bf16[256,2048]{1,0:T(8,128)(2,1)S(1)}, bf16[256,2048]{1,0:T(8,128)(2,1)}, u32[]{:S(2)}) copy-start(bf16[256,2048]{1,0:T(8,128)(2,1)} %hidden_ref.1) | copy-start | bytes 3145732
  596.9 3.0 copy-start.13
  597.1 5.3 copy-start.10
  597.9 11.0 copy-start.14
  609.0 282.7 %reduce-scatter.2.cloned.1.call-start = ((), (), s32[]{:S(2)}) async-start(), calls=%async_computation.2 | async-start | bytes 2621440 | tf_op jit(solution)/shard_map/reduce_scatter | solution.py:1057
  610.7 9.5 copy-start.22
  690.0 102.7 %copy-start.3 = (f32[256,2048]{1,0:T(8,128)S(1)}, f32[256,2048]{1,0:T(8,128)}, u32[]{:S(2)}) copy-start(f32[256,2048]{1,0:T(8,128)} %get-tuple-element.32) | copy-start | bytes 6291460
  792.6 2.9 copy-start.6
  792.6 2.9 copy-start.9
  812.6 35.8 %copy-start.8 = (f32[256,256]{1,0:T(8,128)S(1)}, f32[256,256]{1,0:T(8,128)}, u32[]{:S(2)}) copy-start(f32[256,256]{1,0:T(8,128)} %copy.41.sin_ref) | copy-start | bytes 786436
  848.4 0.9 copy-start.7
  897.1 10.3 copy-start.2
  897.1 10.3 copy-start.11
  897.1 10.3 copy-start.15
  907.4 2.2 copy-start.12
  910.2 592.1 %copy-start.16 = (pred[76]{0:T(512)(128)(4,1)S(1)}, pred[76]{0:T(512)(128)(4,1)}, u32[]{:S(2)}) copy-start(pred[76]{0:T(512)(128)(4,1)} %pad_add_fusion) | copy-start | bytes 232
  1515.4 22.2 %copy-start = (f32[76,16,2048]{2,1,0:T(8,128)}, f32[76,16,2048]{2,1,0:T(8,128)S(1)}, u32[]{:S(2)}) copy-start(f32[76,16,2048]{2,1,0:T(8,128)S(1)} %get-tuple-element.57) | copy-start | bytes 29884420
  1515.4 22.2 %copy-start.4 = (f32[256,2048]{1,0:T(8,128)S(1)}, f32[256,2048]{1,0:T(8,128)}, u32[]{:S(2)}) copy-start(f32[256,2048]{1,0:T(8,128)} %get-tuple-element.44) | copy-start | bytes 6291460
  1515.4 22.2 %copy-start.5 = (f32[256,2048]{1,0:T(8,128)S(1)}, f32[256,2048]{1,0:T(8,128)}, u32[]{:S(2)}) copy-start(f32[256,2048]{1,0:T(8,128)} %get-tuple-element.59) | copy-start | bytes 6291460
  1515.4 22.2 %copy-start.17 = (f32[256]{0:T(256)S(1)}, f32[256]{0:T(256)}, u32[]{:S(2)}) copy-start(f32[256]{0:T(256)} %get-tuple-element.80) | copy-start | bytes 3076
  1537.6 1.9 copy-start.19
  1537.6 1.9 copy-start.20
  1537.6 1.9 copy-start.21
Sparse Core Ops, SparseCore 0:
  609.1 43.2 all-gather.1
  848.6 43.0 reduce-scatter.1

commit v5 on v4

--- a/solution.py
+++ b/solution.py
@@ -100,13 +100,28 @@
     return (lax.axis_size("dp"), lax.axis_size("fsdp")) == (8, 4)
 
 
-def gather_any(low_tiles, low_gains):
+def forward_attention(low_tiles, low_gains, slots, places, hidden_in, cosine, sine, lead):
+    caps, tile_rows, width = low_tiles.shape
+    slot_query, slot_both, slot_out = slots
     if tuned_mesh():
-        return gather_slots(low_tiles, low_gains)
-    return (
-        lax.all_gather(low_tiles, ("dp", "fsdp"), axis=0, tiled=True),
-        lax.all_gather(low_gains, ("dp", "fsdp"), axis=1, tiled=True),
-    )
+        table = jnp.concatenate(slots)
+        table = table // caps * lead + lax.rem(table, caps)
+        (wall, weights, both, gains, normed, queries, attended, lse, middle, normed_two) = (
+            gather_slots(low_tiles, low_gains, table, places, hidden_in, cosine, sine, lead)
+        )
+        return wall, gains, both, normed, queries, attended, lse, middle, normed_two
+    wall = lax.all_gather(low_tiles, ("dp", "fsdp"), axis=0, tiled=True)
+    gains = lax.all_gather(low_gains, ("dp", "fsdp"), axis=1, tiled=True).astype(jnp.float32)
+    tokens = hidden_in.astype(jnp.float32)
+    inv_one = lax.rsqrt(jnp.mean(tokens * tokens, axis=1, keepdims=True) + norm_eps)
+    normed = (tokens * inv_one * gains[0]).astype(jnp.bfloat16)
+    turned = KV_HEADS * HEAD // cosine.shape[1]
+    both_local = project(slot_both, normed, cosine, sine, wall, turned=turned)
+    both = lax.all_gather(both_local, "fsdp", axis=0, tiled=True)
+    queries = project(slot_query, normed, cosine, sine, wall)
+    attended, lse = attend(places, queries, both)
+    middle, normed_two = mix(slot_out, attended, hidden_in, gains[1], wall)
+    return wall, gains, both, normed, queries, attended, lse, middle, normed_two
 
 
 def scatter_any(grads_wall, gain_terms, caps):
@@ -669,7 +684,71 @@
     return (at >= 0) & (at < counts[route]), at
 
 
-def gather_kernel(mine_ref, gain_ref, wall_ref, gains_ref, own_sem, send_sem, recv_sem):
+def slot_of(route, index, counts, starts, lead, early):
+    if route < 2:
+        return 2 * lead + starts[route] + index
+    here = 2 * lead + starts[route] - (route - 2) * lead
+    count = counts[route]
+    if early:
+        later = (index + count - lead) // count
+        return (route - 2) * lead + index + later * (here - route * lead + lead)
+    final = index // (count - lead)
+    return here + index - final * (here + count - lead - (route - 2) * lead)
+
+
+def attend_side(side, q, k_pair, v_pair, mask, out_ref, logs):
+    lane = lax.broadcasted_iota(jnp.int32, (q.shape[0], 128), 1)
+    scale = jnp.bfloat16(1.0 / HEAD**0.5)
+    k = k_pair[:, side * HEAD : (side + 1) * HEAD]
+    v = v_pair[:, side * HEAD : (side + 1) * HEAD]
+    for h in range(GROUP):
+        cols = slice(h * HEAD, (h + 1) * HEAD)
+        scores = jnp.where(mask, dot(q[:, cols] * scale, k, NT), masked_score)
+        top = jnp.max(scores, axis=1, keepdims=True)
+        raised = jnp.exp(scores - top)
+        total = jnp.sum(raised, axis=1, keepdims=True)
+        probs = (raised * (1.0 / total)).astype(jnp.bfloat16)
+        out_ref[:, cols] = dot(probs, v, NN).astype(out_ref.dtype)
+        logs = jnp.where(lane == side * GROUP + h, top + jnp.log(total), logs)
+    return logs
+
+
+GATHER_HOPS = ("z1", "z2", "z3")
+
+
+def gather_kernel(
+    lead,
+    mine_ref,
+    gain_ref,
+    table,
+    places,
+    hidden_ref,
+    cos_ref,
+    sin_ref,
+    wall_ref,
+    gains_ref,
+    weights_ref,
+    both_ref,
+    all_gains_ref,
+    normed_ref,
+    q_ref,
+    att_ref,
+    lse_ref,
+    middle_ref,
+    normed_two_ref,
+    own_sem,
+    send_sem,
+    recv_sem,
+    tiles,
+    block,
+    gain_tiles,
+    keys,
+    mask_ref,
+    pair_ref,
+    side_sem,
+    hop_send,
+    hop_recv,
+):
     y, x, c, z = position()
     counts, starts = split_slots(mine_ref.shape[0])
     rounds = round_count(counts, GATHER_DELAYS)
@@ -696,7 +775,8 @@
         if route == 4:
             view = gains_ref.at[region(route, stage)]
         else:
-            view = wall_ref.at[region(route, stage) + (starts[route] + index,)]
+            slot = slot_of(route, index, counts, starts, lead // 2, True)
+            view = wall_ref.at[region(route, stage) + (slot,)]
         return pltpu.make_async_remote_copy(
             src_ref=view,
             dst_ref=view,
@@ -707,6 +787,120 @@
         )
 
     stages = len(GATHER_ROUTES[0])
+    tokens, width = hidden_ref.shape
+    number = block.shape[0]
+    rows = number * block.shape[1]
+    query_blocks = q_ref.shape[1] // rows
+    key_blocks = keys.shape[1] // rows
+
+    def take(at):
+        @pl.loop(0, number, unroll=True)
+        def _(t):
+            block[t] = tiles[table[at * number + t]]
+
+        pltpu.make_async_copy(
+            block, weights_ref.at[pl.ds(at * number, number)], side_sem.at[1]
+        ).start()
+        return block[...].reshape(rows, width)
+
+    def taken(at):
+        pltpu.make_async_copy(
+            block, weights_ref.at[pl.ds(at * number, number)], side_sem.at[1]
+        ).wait()
+
+    def load_tiles(d):
+        return pltpu.make_async_copy(
+            wall_ref.at[d // 16, lax.rem(d // 8, 2), lax.rem(d // 4, 2), lax.rem(d, 4), pl.ds(0, lead)],
+            tiles.at[pl.ds(d * lead, lead)],
+            side_sem.at[0],
+        )
+
+    load_gains = pltpu.make_async_copy(gains_ref, gain_tiles, side_sem.at[2])
+
+    def pass_keys(part):
+        hop = part // 2
+        at = lax.rem(z + 4 - hop, 4)
+        cols = KV_HEADS * HEAD
+        view = keys.at[
+            pl.ds(pl.multiple_of(at * tokens, tokens), tokens),
+            pl.ds(part % 2 * cols, cols),
+        ]
+        return pltpu.make_async_remote_copy(
+            src_ref=view,
+            dst_ref=view,
+            send_sem=hop_send.at[part],
+            recv_sem=hop_recv.at[part],
+            device_id=target(GATHER_HOPS[hop]),
+            device_id_type=MESH,
+        )
+
+    def begin():
+        @pl.loop(0, 32)
+        def _(d):
+            load_tiles(d).start()
+
+        load_gains.start()
+
+    def norm():
+        load_gains.wait()
+        lane = lax.broadcasted_iota(jnp.int32, (8, 128), 1)
+        parts = []
+        for d in range(0, 32, 2):
+            even = gain_tiles[d // 16, (d // 8) % 2, (d // 4) % 2, d % 4].astype(jnp.float32)[:8]
+            odd = gain_tiles[d // 16, (d // 8) % 2, (d // 4) % 2, d % 4 + 1].astype(jnp.float32)[:8]
+            parts.append(jnp.where(lane < 64, even, pltpu.roll(odd, 64, 1)))
+        all_gains_ref[...] = jnp.concatenate(parts, axis=1)
+        hidden = hidden_ref[...].astype(jnp.float32)
+        inv = lax.rsqrt(jnp.mean(hidden * hidden, axis=1, keepdims=True) + norm_eps)
+        normed_ref[...] = (hidden * inv * all_gains_ref[0:1, :]).astype(normed_ref.dtype)
+        fill_mask(places, mask_ref)
+
+    def project_keys():
+        pltpu.make_async_copy(tiles, tiles, side_sem.at[0]).wait()
+        own_rows = pl.ds(pl.multiple_of(z * tokens, tokens), tokens)
+
+        for b in range(key_blocks):
+            at = query_blocks + b
+            u = dot(normed_ref[...], take(at), NT)
+            if b < key_blocks // 2:
+                u = u * cos_ref[...] + swap_halves(u) * sin_ref[...]
+            keys[own_rows, b * rows : (b + 1) * rows] = u.astype(keys.dtype)
+            taken(at)
+
+    def project_queries(low, high):
+        @pl.loop(low, high)
+        def _(b):
+            u = dot(normed_ref[...], take(b), NT)
+            u = u * cos_ref[...] + swap_halves(u) * sin_ref[...]
+            q_ref[:, pl.ds(pl.multiple_of(b * rows, rows), rows)] = u.astype(q_ref.dtype)
+            taken(b)
+
+    def attend_step(pair, side):
+        wide = GROUP * HEAD
+        narrow = PAIR * HEAD
+        here = pl.ds(pl.multiple_of((pair * PAIR + side) * wide, wide), wide)
+        k_pair = keys[:, pl.ds(pl.multiple_of(pair * narrow, narrow), narrow)]
+        v_pair = keys[:, pl.ds(pl.multiple_of(KV_HEADS * HEAD + pair * narrow, narrow), narrow)]
+        logs = lse_ref[pair] if side else jnp.zeros((tokens, 128), jnp.float32)
+        mask = mask_ref[...] > 0.5
+        lse_ref[pair] = attend_side(side, q_ref[:, here], k_pair, v_pair, mask, pair_ref, logs)
+        att_ref[:, here] = pair_ref[...]
+
+    def mix_blocks(low):
+        for more in range(4):
+            b = low + more
+            at = query_blocks + key_blocks + b
+            left = att_ref[:, pl.ds(pl.multiple_of(b * rows, rows), rows)]
+            middle_ref[...] += dot(left, take(at), NN)
+            taken(at)
+
+    def mix_end():
+        middle = middle_ref[...]
+        inv = lax.rsqrt(jnp.mean(middle * middle, axis=1, keepdims=True) + norm_eps)
+        normed_two_ref[...] = (middle * inv * all_gains_ref[1:2, :]).astype(normed_two_ref.dtype)
+
+    start = GATHER_DELAYS[3] + lead // 2 - 1 + stages
+    keep_both = pltpu.make_async_copy(keys, both_ref, side_sem.at[3])
 
     @pl.loop(0, rounds + stages)
     def _(t):
@@ -724,34 +918,106 @@
                     if stage < stages:
                         copy(route, stage, index).start()
 
-
-def gather_slots(low_tiles, low_gains):
+        @pl.when(t == start)
+        def _():
+            begin()
+            norm()
+
+        @pl.when(t == start + 1)
+        def _():
+            project_keys()
+
+        parts = 2 * len(GATHER_HOPS)
+        for part in range(parts + 1):
+
+            @pl.when(t == start + 1 + part)
+            def _(part=part):
+                if part > 0:
+                    pass_keys(part - 1).wait()
+                if part < parts:
+                    pass_keys(part).start()
+
+        for third in range(4):
+
+            @pl.when(t == start + 2 + third)
+            def _(third=third):
+                project_queries(third * query_blocks // 4, (third + 1) * query_blocks // 4)
+
+        attending = start + 1 + parts
+
+        @pl.when(t == attending)
+        def _():
+            keep_both.start()
+            middle_ref[...] = hidden_ref[...].astype(jnp.float32)
+
+        for side in range(PAIR):
+            since = t - attending
+
+            @pl.when((since >= 0) & (since < KV_HEADS) & (lax.rem(since + 64, 2) == side))
+            def _(side=side, since=since):
+                attend_step(since // 2, side)
+
+        mixing = attending + KV_HEADS
+
+        @pl.when((t >= mixing) & (t < mixing + query_blocks // 4))
+        def _():
+            mix_blocks((t - mixing) * 4)
+
+        @pl.when(t == mixing + query_blocks // 4)
+        def _():
+            mix_end()
+            keep_both.wait()
+
+
+def gather_slots(low_tiles, low_gains, table, places, hidden, cosine, sine, lead):
     caps, rows, width = low_tiles.shape
+    tokens = hidden.shape[0]
+    length = tokens * 4
     counts, starts = split_slots(caps)
     kind = low_tiles.dtype
     vmem = pl.BlockSpec(memory_space=pltpu.VMEM)
+    smem = pl.BlockSpec(memory_space=pltpu.SMEM)
+    anyw = pl.BlockSpec(memory_space=pl.ANY)
     padded = jnp.pad(low_gains, ((0, 16 - low_gains.shape[0]), (0, 128 - low_gains.shape[1])))
-    wall, gains = pl.pallas_call(
-        gather_kernel,
+    number = cosine.shape[1] // rows
+    pairs = KV_HEADS // PAIR
+    outs = pl.pallas_call(
+        functools.partial(gather_kernel, lead),
         out_shape=[
             jax.ShapeDtypeStruct((2, 2, 2, 4, caps, rows, width), kind),
             jax.ShapeDtypeStruct((2, 2, 2, 4) + padded.shape, kind),
+            jax.ShapeDtypeStruct((table.shape[0], rows, width), kind),
+            jax.ShapeDtypeStruct((length, 2 * KV_HEADS * HEAD), kind),
+            jax.ShapeDtypeStruct((8, width), jnp.float32),
+            jax.ShapeDtypeStruct((tokens, width), kind),
+            jax.ShapeDtypeStruct((tokens, width), kind),
+            jax.ShapeDtypeStruct((tokens, width), kind),
+            jax.ShapeDtypeStruct((pairs, tokens, 128), jnp.float32),
+            jax.ShapeDtypeStruct((tokens, width), jnp.float32),
+            jax.ShapeDtypeStruct((tokens, width), kind),
         ],
-        in_specs=[vmem, vmem],
-        out_specs=[pl.BlockSpec(memory_space=pl.ANY)] * 2,
+        in_specs=[vmem, vmem, smem, smem, vmem, vmem, vmem],
+        out_specs=[anyw] * 4 + [vmem] * 7,
         scratch_shapes=[
             pltpu.SemaphoreType.DMA((2,)),
             pltpu.SemaphoreType.DMA((5, 6)),
             pltpu.SemaphoreType.DMA((5, 6, max(counts))),
+            pltpu.VMEM((32 * lead, rows, width), kind),
+            pltpu.VMEM((number, rows, width), kind),
+            pltpu.VMEM((2, 2, 2, 4) + padded.shape, kind),
+            pltpu.VMEM((length, 2 * KV_HEADS * HEAD), kind),
+            pltpu.VMEM((tokens, length), jnp.float32),
+            pltpu.VMEM((tokens, GROUP * HEAD), kind),
+            pltpu.SemaphoreType.DMA((4,)),
+            pltpu.SemaphoreType.DMA((6,)),
+            pltpu.SemaphoreType.DMA((6,)),
         ],
         compiler_params=pltpu.CompilerParams(
-            collective_id=0, has_side_effects=True, vmem_limit_bytes=24 << 20
+            collective_id=0, has_side_effects=True, vmem_limit_bytes=62 << 20
         ),
         name="gather_slots",
-    )(low_tiles, padded)
-    gains = gains.reshape((32,) + padded.shape)[:, : low_gains.shape[0], : low_gains.shape[1]]
-    gains = gains.transpose(1, 0, 2).reshape(low_gains.shape[0], -1)
-    return wall.reshape(32 * caps, rows, width), gains
+    )(low_tiles, padded, table, places, hidden, cosine, sine)
+    return [outs[0].reshape(32 * caps, rows, width)] + list(outs[2:])
 
 
 SCATTER_ROUTES = (
@@ -1017,12 +1283,7 @@
     query_tiles = model_width // tile_rows
     slot_query, slot_both = slot_qkv[:query_tiles], slot_qkv[query_tiles:]
     half = slot_ffn.shape[0] // 2
-    wall, gains_low = gather_any(
-        master.astype(jnp.bfloat16), gain_master.astype(jnp.bfloat16)
-    )
-    gains_low = gains_low.astype(jnp.float32)
-    gain_attn = gains_low[0]
-    gain_ffn = gains_low[1]
+    lead = layout[2][3]
     tokens = hidden_in.astype(jnp.float32)
     local_len = tokens.shape[0]
     kv_width = KV_HEADS * HEAD
@@ -1030,13 +1291,19 @@
     positions = first + jnp.arange(local_len, dtype=jnp.int32)
     places = jnp.concatenate([first[None].astype(jnp.int32), piece_starts[0]])
     cosine, sine = rope_tables(positions.astype(jnp.float32), 16 * tile_rows)
+    wall, gains_low, both, normed, queries, attended, lse, middle, normed_two = forward_attention(
+        master.astype(jnp.bfloat16),
+        gain_master.astype(jnp.bfloat16),
+        (slot_query, slot_both, slot_out),
+        places,
+        hidden_in,
+        cosine,
+        sine,
+        lead,
+    )
+    gain_attn = gains_low[0]
+    gain_ffn = gains_low[1]
     inv_one = lax.rsqrt(jnp.mean(tokens * tokens, axis=1, keepdims=True) + norm_eps)
-    normed = (tokens * inv_one * gain_attn).astype(jnp.bfloat16)
-    both_local = project(slot_both, normed, cosine, sine, wall, turned=kv_width // (16 * tile_rows))
-    both = lax.all_gather(both_local, "fsdp", axis=0, tiled=True)
-    queries = project(slot_query, normed, cosine, sine, wall)
-    attended, lse = attend(places, queries, both)
-    middle, normed_two = mix(slot_out, attended, hidden_in, gain_ffn, wall)
     inv_two = lax.rsqrt(jnp.mean(middle * middle, axis=1, keepdims=True) + norm_eps)
     ffn_out, grad_normed_two, grads_wall = ffn_call(
         slot_ffn[:half], slot_ffn[half:], slot_down, normed_two, out_cotangent, wall

time: 1560 us -> 1520 us (0.974)
  waiting for transfers between devices: 52.7 us -> 22.8 us
    all_gather x1 -> x0, waiting for transfers between devices: 27.3 us -> none  [shards(): both = lax.all_gather(both_local, 'fsdp', axis=0, tiled=True)]
    pallas_call x5 -> x1, Pallas kernels: 636 us -> 624 us  [gather_slots(): pl.pallas_call(functools.partial(gather_kernel, lead), out_shape=[jax.Sha...]
  transfers between devices with their start and end apart: 2 -> 1, of which waited for: 2 -> 1; matrix products, arithmetic and copies ran while one was open for 1% -> 0% of each run, Pallas kernels for 1% -> 1%
where the time goes in v5:
time: 1520 us; the launch traced here: 1510 us
  Pallas kernels  1390 us (91%)
  other arithmetic  69.6 us (5%)
  waiting for transfers between devices  22.8 us (2%)
  local copies, waits for them, and re-layouts  16.1 us (1%)
    pallas_call x1, Pallas kernels, gather_slots(): pl.pallas_call(functools.partial(gather_kernel, lead), out_shape=[jax.Sha...  624 us
    pallas_call x1, Pallas kernels, scatter_slots(): pl.pallas_call(functools.partial(scatter_kernel, look), out_shape=[jax.Sh...  591 us
    pallas_call x1, Pallas kernels, ffn_call(): pl.pallas_call(functools.partial(ffn_kernel, group), grid_spec=pltpu.Pref...  102 us
    pallas_call x1, Pallas kernels, attend_back(): pl.pallas_call(attend_back_kernel, grid_spec=pltpu.PrefetchScalarGridSpec...  36.2 us
  transfers between devices with their start and end apart: 1, of which 1 were waited for; matrix products, arithmetic and copies ran while one was open for 0% of the time, Pallas kernels for 1%

profile of v5, /device:TPU:0, one launch (start us, length us, event | category | flops | bytes accessed | tf_op | source)
XLA Modules:
  0.0 1513.0 jit_solution(2856537262318222406)
XLA Ops:
  7.2 0.0 reduce-scatter.2.cloned.1.call-start
  7.2 0.7 slice.48
  7.9 0.8 slice.49
  8.7 0.8 slice.50
  9.5 0.8 slice.53
  10.2 0.2 convert_reduce_fusion.2
  10.4 0.2 convert_reduce_fusion.3
  10.6 1.3 fusion.14
  11.9 1.4 fusion.15
  13.3 0.2 fusion.11
  13.6 0.8 copy.35.cos_ref
  14.4 0.8 copy.36.sin_ref
  15.3 6.9 convert_element_type.55.mine_ref
  22.2 0.5 convert_reduce_fusion
  22.7 0.7 convert_reduce_fusion.4
  23.4 0.2 convert_reduce_fusion.1
  23.7 0.7 multiply_add_fusion.1.table
  24.4 0.6 pad_add_fusion.2.places
  24.9 0.6 pad.8.gain_ref
  25.5 624.0 %gather_slots.1 = (bf16[2,2,2,4,76,16,2048]{6,5,4,3,2,1,0:T(8,128)(2,1)}, bf16[2,2,2,4,16,128]{5,4,3,2,1,0:T(8,128)(2,1)}, bf16[320,16,2048]{2,1,0:T(8,128)(2,1)...) custom-call(bf16[76,16,2048]{2,1,0:T(8,128)(2,1)} %convert_element_t, ...), custom_call_target="tpu_custom_call" | custom-call | tf_op jit(solution)/shard_map/gather_slots/pallas_call | solution.py:984
  649.5 1.8 multiply_reduce_fusion.2
  651.3 1.5 fusion.19
  652.8 1.3 convert_reduce_fusion.5
  654.1 102.3 %ffn.1 = (f32[256,2048]{1,0:T(8,128)}, f32[256,2048]{1,0:T(8,128)}, bf16[2432,16,2048]{2,1,0:T(8,128)(2,1)}) custom-call(s32[512]{0:T(512)} %get-tuple-element.92.gate_s, s32[512]{0:T(512)} %get-tuple-element.93.up_s, s32[512]{0:T(512)} %get-tuple-element.80.down_s, bf16[256,2048]{1,0:T(8,128)(2,1)} %get-tuple-element.33.normed_ref, ...), custom_call_target="tpu_custom_call" | custom-call | tf_op jit(solution)/shard_map/ffn/pallas_call | solution.py:609
  756.5 0.0 copy-start.5
  756.5 0.0 copy-start.6
  756.5 2.9 multiply_reduce_fusion
  759.4 4.4 fusion.17
  763.8 12.5 mix_back.1
  776.3 0.0 copy-start.7
  776.3 36.2 %attend_back.1 = (bf16[256,2048]{1,0:T(8,128)(2,1)}, bf16[1024,1024]{1,0:T(8,128)(2,1)}) custom-call(s32[3]{0:T(128)} %pad_add_fusion.2.places, bf16[256,2048]{1,0:T(8,128)(2,1)} %get-tuple-element.38.q_ref, bf16[1024,1024]{1,0:T(8,128)(2,1)} %get-tuple-element.39.k_ref.v_ref, bf16[1024,1024]{1,0:T(8,128)(2,1)} %get-tuple-element.39.k_ref.v_ref, ...), custom_call_target="tpu_custom_call" | custom-call | tf_op jit(solution)/shard_map/attend_back/pallas_call | solution.py:508
  812.5 0.0 reduce-scatter.2.cloned.1.call-update
  812.5 0.5 slice.59.table.start_ref
  813.0 0.6 slice.55.table
  813.6 0.2 tile.38
  813.9 0.2 tile.40
  814.1 0.0 copy-start.2
  814.1 13.5 project_back.2
  827.6 0.7 iota_compare_fusion.5
  828.3 0.7 iota_compare_fusion.6
  828.9 0.7 iota_compare_fusion.8
  829.6 0.7 iota_compare_fusion.7
  830.3 0.1 pad_add_fusion.1
  830.3 0.3 fusion.2
  830.6 0.6 multiply_multiply_fusion.1
  831.2 22.8 %reduce-scatter.2.cloned.1.call-done = bf16[256,1024]{1,0:T(8,128)(2,1)} async-done(((bf16[1024,1024]{1,0:T(8,128)(2,1)}), bf16[256,1024]{1,0:T(8,128)(2,1)}) %reduce-scatter.2.cloned.1.call-update) | async-done | bytes 524304 | tf_op jit(solution)/shard_map/reduce_scatter | solution.py:1324
  854.0 1.4 reshape.110
  855.4 2.6 fusion.18
  858.0 0.6 copy.46
  858.7 1.0 copy.43
  859.7 0.2 copy.45
  859.9 1.0 copy.52
  860.9 1.2 subtract_convert_fusion
  862.1 0.9 pad_maximum_fusion.left_ref
  863.0 10.2 project_back.3
  873.2 2.1 fusion.7
  875.3 0.6 select_maximum_fusion.gain_ref
  876.0 591.2 %scatter_slots.1 = (f32[76,16,2048]{2,1,0:T(8,128)}, f32[8,2048]{1,0:T(8,128)}, bf16[2,2,4,76,16,2048]{5,4,3,2,1,0:T(8,128)(2,1)}, bf16[2,4,76,16,2048]{4,3,2,1,...) custom-call(bf16[2,2,2,4,76,16,2048]{6,5,4,3,2,1,0:T(8,128)(2,1)} %b, ...), custom_call_target="tpu_custom_call" | custom-call | tf_op jit(solution)/shard_map/scatter_slots/pallas_call | solution.py:1236
  1467.2 0.8 slice.61
  1468.0 13.1 broadcast_select_fusion
  1481.1 0.0 copy-start.13
  1481.2 22.2 %broadcast_select_fusion.1 = (f32[76,16,2048]{2,1,0:T(8,128)}, f32[76,16,2048]{2,1,0:T(8,128)}) fusion(pred[76]{0:T(512)(128)(4,1)S(1)} %pad_add_fusion.1, f32[76,16,2048]{2,1,0:T(8,128)S(1)} %get-tuple-element.63, f32[76,16,2048]{2,1,0:T(8,128)} %param.15, f32[76,16,2048]{2,1,0:T(8,128)} %param.14, f32[76,16,2048]{2,1,0:T(8,128)} %param.16), kind=kLoop, calls=%fused_computation.5 | loop fusion | flops 39845888 | bytes 59768908 | tf_op jit(solution)/shard_map/jit(_where)/select_n | solution.py:1351
  1503.4 1.9 fusion.4
  1505.3 0.7 multiply_add_fusion.3
  (46 shorter events, 0.3 us)
Async XLA Ops:
  7.2 846.8 %reduce-scatter.2.cloned.1.call-start = ((), (), s32[]{:S(2)}) async-start(), calls=%async_computation.1 | async-start | bytes 2621440 | tf_op jit(solution)/shard_map/reduce_scatter | solution.py:1324
  13.3 10.4 copy-start.12
  15.3 6.9 copy-start.14
  15.3 7.5 copy-start.11
  15.3 9.1 copy-start.18
  654.1 102.4 %copy-start.1 = (f32[256,2048]{1,0:T(8,128)S(1)}, f32[256,2048]{1,0:T(8,128)}, u32[]{:S(2)}) copy-start(f32[256,2048]{1,0:T(8,128)} %get-tuple-element.32) | copy-start | bytes 6291460
  756.5 2.9 copy-start.5
  756.5 2.9 copy-start.6
  776.3 37.3 %copy-start.7 = (f32[256,256]{1,0:T(8,128)S(1)}, f32[256,256]{1,0:T(8,128)}, u32[]{:S(2)}) copy-start(f32[256,256]{1,0:T(8,128)} %copy.35.cos_ref) | copy-start | bytes 786436
  776.3 37.5 %copy-start.8 = (f32[256,256]{1,0:T(8,128)S(1)}, f32[256,256]{1,0:T(8,128)}, u32[]{:S(2)}) copy-start(f32[256,256]{1,0:T(8,128)} %copy.36.sin_ref) | copy-start | bytes 786436
  814.1 16.3 %copy-start.2 = (bf16[256,2048]{1,0:T(8,128)(2,1)S(1)}, bf16[256,2048]{1,0:T(8,128)(2,1)}, u32[]{:S(2)}) copy-start(bf16[256,2048]{1,0:T(8,128)(2,1)} %hidden_ref.1) | copy-start | bytes 3145732
  863.0 10.2 copy-start.9
  863.0 12.3 copy-start.10
  1481.1 22.2 %copy-start = (f32[76,16,2048]{2,1,0:T(8,128)}, f32[76,16,2048]{2,1,0:T(8,128)S(1)}, u32[]{:S(2)}) copy-start(f32[76,16,2048]{2,1,0:T(8,128)S(1)} %get-tuple-element.63) | copy-start | bytes 29884420
  1481.1 22.2 %copy-start.3 = (f32[256,2048]{1,0:T(8,128)S(1)}, f32[256,2048]{1,0:T(8,128)}, u32[]{:S(2)}) copy-start(f32[256,2048]{1,0:T(8,128)} %get-tuple-element.50) | copy-start | bytes 6291460
  1481.1 22.2 %copy-start.4 = (f32[256,2048]{1,0:T(8,128)S(1)}, f32[256,2048]{1,0:T(8,128)}, u32[]{:S(2)}) copy-start(f32[256,2048]{1,0:T(8,128)} %get-tuple-element.65) | copy-start | bytes 6291460
  1481.1 22.2 %copy-start.13 = (f32[256]{0:T(256)S(1)}, f32[256]{0:T(256)}, u32[]{:S(2)}) copy-start(f32[256]{0:T(256)} %get-tuple-element.86) | copy-start | bytes 3076
  1503.3 2.0 copy-start.15
  1503.3 2.0 copy-start.16
  1503.3 2.0 copy-start.17
Sparse Core Ops, SparseCore 0:
  812.7 41.2 reduce-scatter.1

commit v6 on v5

--- a/solution.py
+++ b/solution.py
@@ -109,7 +109,7 @@
         (wall, weights, both, gains, normed, queries, attended, lse, middle, normed_two) = (
             gather_slots(low_tiles, low_gains, table, places, hidden_in, cosine, sine, lead)
         )
-        return wall, gains, both, normed, queries, attended, lse, middle, normed_two
+        return wall, weights, gains, both, normed, queries, attended, lse, middle, normed_two
     wall = lax.all_gather(low_tiles, ("dp", "fsdp"), axis=0, tiled=True)
     gains = lax.all_gather(low_gains, ("dp", "fsdp"), axis=1, tiled=True).astype(jnp.float32)
     tokens = hidden_in.astype(jnp.float32)
@@ -121,20 +121,82 @@
     queries = project(slot_query, normed, cosine, sine, wall)
     attended, lse = attend(places, queries, both)
     middle, normed_two = mix(slot_out, attended, hidden_in, gains[1], wall)
-    return wall, gains, both, normed, queries, attended, lse, middle, normed_two
-
-
-def scatter_any(grads_wall, gain_terms, caps):
-    number = gain_terms.shape[0]
+    return wall, wall, gains, both, normed, queries, attended, lse, middle, normed_two
+
+
+def backward_attention(
+    grads_wall,
+    gain_two_term,
+    weights,
+    slots,
+    places,
+    branch,
+    attended,
+    queries,
+    both,
+    lse,
+    normed,
+    hidden_in,
+    cosine,
+    sine,
+    layout,
+    caps,
+):
+    slot_query, slot_both, slot_out = slots
+    local_len, width = normed.shape
+    kv_width = KV_HEADS * HEAD
     if tuned_mesh():
-        padded = jnp.pad(gain_terms, ((0, 8 - number), (0, 0)))
-        grads, total = scatter_slots(grads_wall, padded, caps)
-        width = gain_terms.shape[1] // 32
+        lead = layout[2][3]
+        table = jnp.concatenate(slots)
+        table = table // caps * lead + lax.rem(table, caps)
+        order = jnp.arange(table.shape[0], dtype=jnp.int32)
+        here = jnp.arange(32 * lead, dtype=jnp.int32)
+        tile_at = jnp.sum(jnp.where(table[None, :] == here[:, None], order[None, :], 0), axis=1)
+        terms = jnp.pad(gain_two_term[None, :], ((1, 6), (0, 0)))
+        grads, total, grad_normed = scatter_slots(
+            grads_wall,
+            terms,
+            weights,
+            tile_at,
+            places,
+            branch,
+            attended,
+            queries,
+            both,
+            lse,
+            normed,
+            hidden_in,
+            cosine,
+            sine,
+            lead,
+            layout[0][2],
+            caps,
+        )
+        part = width // 32
         device = lax.axis_index(("dp", "fsdp"))
-        return grads, lax.dynamic_slice_in_dim(total[:number], device * width, width, 1)
+        return grads, lax.dynamic_slice_in_dim(total[:2], device * part, part, 1), grad_normed
+    grad_attended, grads_wall = mix_back(slot_out, attended, branch, weights, grads_wall)
+    grad_query, both_terms = attend_back(
+        places, queries, both, grad_attended, lse, cosine, sine
+    )
+    both_sum = lax.psum_scatter(both_terms, "fsdp", scatter_dimension=0, tiled=True).astype(
+        jnp.float32
+    )
+    grad_normed, grads_wall = project_back(slot_query, grad_query, normed, None, weights, grads_wall)
+    both_sum = both_sum.reshape(local_len, KV_HEADS // PAIR, 2, PAIR * HEAD)
+    grad_key = turn_back(both_sum[:, :, 0].reshape(local_len, kv_width), cosine, sine)
+    grad_value = both_sum[:, :, 1].reshape(local_len, kv_width)
+    grad_both = jnp.concatenate([grad_key, grad_value], axis=1).astype(jnp.bfloat16)
+    grad_normed, grads_wall = project_back(
+        slot_both, grad_both, normed, grad_normed, weights, grads_wall
+    )
+    tokens = hidden_in.astype(jnp.float32)
+    inv_one = lax.rsqrt(jnp.mean(tokens * tokens, axis=1, keepdims=True) + norm_eps)
+    gain_one_term = jnp.sum(grad_normed * tokens * inv_one, axis=0)
+    gain_terms = jnp.stack([gain_one_term, gain_two_term])
     grads = lax.psum_scatter(grads_wall, ("dp", "fsdp"), scatter_dimension=0, tiled=True)
     gain_grad = lax.psum_scatter(gain_terms, ("dp", "fsdp"), scatter_dimension=1, tiled=True)
-    return grads.astype(jnp.float32), gain_grad
+    return grads.astype(jnp.float32), gain_grad, grad_normed
 
 
 VMEM_ASK = 56 << 20
@@ -1049,7 +1111,60 @@
     return 2 + ("x" in done) + ("y" in done) + ("z1" in done)
 
 
-def scatter_kernel(look, wall_ref, gain_ref, out_ref, total_ref, core_ref, first_ref, second_ref, ring_ref, last_ref, *scratch):
+def attend_back_side(side, q, k_pair, v_pair, grad, mask, logs, turn_ref, k_out, v_out):
+    scale = jnp.bfloat16(1.0 / HEAD**0.5)
+    here = slice(side * HEAD, (side + 1) * HEAD)
+    k = k_pair[:, here]
+    v = v_pair[:, here]
+    dk = None
+    dv = None
+    for h in range(GROUP):
+        cols = slice(h * HEAD, (h + 1) * HEAD)
+        head = side * GROUP + h
+        q_head = q[:, cols] * scale
+        scores = jnp.where(mask, dot(q_head, k, NT), masked_score)
+        probs = jnp.exp(scores - logs[:, head : head + 1])
+        grad_probs = dot(grad[:, cols], v, NT)
+        row_dot = jnp.sum(probs * grad_probs, axis=1, keepdims=True)
+        grad_scores = (probs * (grad_probs - row_dot)).astype(jnp.bfloat16)
+        turn_ref[:, cols] = dot(grad_scores, k, NN) * (1.0 / HEAD**0.5)
+        dk_part = dot(q_head, grad_scores, TN)
+        dv_part = dot(grad[:, cols], probs.astype(jnp.bfloat16), TN)
+        dk = dk_part if dk is None else dk + dk_part
+        dv = dv_part if dv is None else dv + dv_part
+    k_out[:, here] = dk.T.astype(k_out.dtype)
+    v_out[:, here] = dv.T.astype(v_out.dtype)
+
+
+def scatter_kernel(
+    look,
+    lead,
+    first_group,
+    old_ref,
+    gain_ref,
+    weights_ref,
+    table,
+    places,
+    branch_ref,
+    att_ref,
+    q_ref,
+    both_ref,
+    lse_ref,
+    normed_ref,
+    hidden_ref,
+    cos_ref,
+    sin_ref,
+    wall_ref,
+    out_ref,
+    total_ref,
+    back_ref,
+    core_ref,
+    first_ref,
+    second_ref,
+    ring_ref,
+    last_ref,
+    *scratch,
+):
     y, x, c, z = position()
     caps, rows, width = out_ref.shape
     counts, starts = split_slots(caps)
@@ -1061,13 +1176,29 @@
     for route in range(4):
         for stage in range(1, stages):
             held[route, stage] = scratch.pop(0)
-            if stage < stages - 1:
-                made[route, stage] = scratch.pop(0)
-    load_sem, send_sem, recv_sem, sums, landed, sum_send, sum_recv = scratch
+            made[route, stage] = scratch.pop(0)
+    load_sem, send_sem, recv_sem, out_sem, sums, landed, sum_send, sum_recv = scratch[:8]
+    (
+        streamed,
+        grad_att,
+        grad_q,
+        grad_kv,
+        grad_both,
+        k_pair_ref,
+        v_pair_ref,
+        turn_ref,
+        hop_out,
+        hop_in,
+        turned,
+        left_ref,
+        built,
+        mask_ref,
+        stream_sem,
+        hop_send,
+        hop_recv,
+        built_sem,
+    ) = scratch[8:]
     enter(("x", "y", "core", "z", "back"))
-
-    def pick(hop, mine, other):
-        return other if hop else mine
 
     def landing(route, stage, slot):
         hops = SCATTER_ROUTES[route]
@@ -1110,8 +1241,11 @@
             views.append(last_ref.at[slot])
         return views
 
+    def slot_at(route, index):
+        return slot_of(route, index, counts, starts, lead // 2, False)
+
     def send(route, stage, index):
-        slot = starts[route] + index
+        slot = slot_at(route, index)
         if stage == 0:
             source = wall_ref.at[:, :, 1 - c, :, slot]
         else:
@@ -1125,15 +1259,20 @@
             device_id_type=MESH,
         )
 
+    def keep(route, index):
+        return pltpu.make_async_copy(
+            made[route, stages - 1], out_ref.at[slot_at(route, index)], out_sem.at[route]
+        )
+
     def early(route, stage, index):
         if stage > 0:
-            for k, view in enumerate(terms(route, stage, starts[route] + index)[:-1]):
+            for k, view in enumerate(terms(route, stage, slot_at(route, index))[:-1]):
                 pltpu.make_async_copy(view, held[route, stage].at[k], load_sem.at[route, stage]).start()
 
     def late(route, stage, index):
         if stage > 0:
             send(route, stage - 1, index).wait()
-            view = terms(route, stage, starts[route] + index)[-1]
+            view = terms(route, stage, slot_at(route, index))[-1]
             last = held[route, stage].shape[0] - 1
             pltpu.make_async_copy(view, held[route, stage].at[last], load_sem.at[route, stage]).start()
 
@@ -1147,6 +1286,11 @@
             for size in extent:
                 blocks *= size
             part = min(width, 512)
+            if stage == stages - 1:
+
+                @pl.when(index > 0)
+                def _():
+                    keep(route, index - 1).wait()
 
             @pl.loop(0, blocks)
             def _(block):
@@ -1161,13 +1305,12 @@
                     total = buf[(0,) + at + (EVERY, cols)].astype(jnp.float32)
                     for k in range(1, number):
                         total += buf[(k,) + at + (EVERY, cols)].astype(jnp.float32)
-                    if stage == stages - 1:
-                        out_ref[starts[route] + index, :, cols] = total
-                    else:
-                        made[route, stage][at + (EVERY, cols)] = total.astype(made[route, stage].dtype)
+                    made[route, stage][at + (EVERY, cols)] = total.astype(made[route, stage].dtype)
 
         if stage < stages - 1:
             send(route, stage, index).start()
+        else:
+            keep(route, index).start()
 
     def pass_sum(hop):
         return pltpu.make_async_remote_copy(
@@ -1183,7 +1326,11 @@
         if step > 0:
             pass_sum(step - 1).wait()
         if step == 0:
-            sums[0] = gain_ref[...]
+            hidden = hidden_ref[...].astype(jnp.float32)
+            inv = lax.rsqrt(jnp.mean(hidden * hidden, axis=1, keepdims=True) + norm_eps)
+            term = jnp.sum(back_ref[...] * hidden * inv, axis=0, keepdims=True)
+            line = lax.broadcasted_iota(jnp.int32, gain_ref.shape, 0)
+            sums[0] = jnp.where(line == 0, term, gain_ref[...])
         elif step < 4:
             sums[step] = sums[step - 1] + landed[step - 1]
         elif step == len(SUM_HOPS):
@@ -1191,11 +1338,199 @@
         if step < len(SUM_HOPS):
             pass_sum(step).start()
 
+    tokens = hidden_ref.shape[0]
+    number = cos_ref.shape[1] // rows
+    block = number * rows
+    query_blocks = q_ref.shape[1] // block
+    key_blocks = both_ref.shape[1] // block
+    out_blocks = att_ref.shape[1] // block
+    all_blocks = query_blocks + key_blocks + out_blocks
+    kv_width = KV_HEADS * HEAD
+
+    def stream(n):
+        at = lax.rem(n + query_blocks + key_blocks, all_blocks)
+        return pltpu.make_async_copy(
+            weights_ref.at[pl.ds(at * number, number)],
+            streamed.at[lax.rem(n, 2)],
+            stream_sem.at[lax.rem(n, 2)],
+        )
+
+    def streamed_block(n):
+        stream(n).wait()
+
+        @pl.when(n + 1 < all_blocks)
+        def _():
+            stream(n + 1).start()
+
+        return streamed[lax.rem(n, 2)].reshape(block, width)
+
+    def column(b):
+        return pl.ds(pl.multiple_of(b * block, block), block)
+
+    def turn_tiles(at, value):
+        flipped = value.astype(jnp.float32).T.astype(turned.dtype)
+        turned[pl.ds(at * number, number)] = flipped.reshape(number, rows, tokens)
+
+    def out_back(low, high):
+        @pl.loop(low, high)
+        def _(b):
+            grad_att[:, column(b)] = dot(branch_ref[...], streamed_block(b), NT).astype(
+                grad_att.dtype
+            )
+            turn_tiles(query_blocks + key_blocks + b, att_ref[:, column(b)])
+
+    def query_back(low, high):
+        @pl.loop(low, high)
+        def _(b):
+            left = grad_q[:, column(b)]
+            back_ref[...] += dot(left, streamed_block(out_blocks + b), NN)
+            turn_tiles(b, left)
+
+    def key_back():
+        @pl.loop(0, key_blocks)
+        def _(b):
+            left = grad_both[:, column(b)]
+            back_ref[...] += dot(left, streamed_block(out_blocks + query_blocks + b), NN)
+            turn_tiles(query_blocks + b, left)
+
+    def attend_back_step(pair, side):
+        wide = GROUP * HEAD
+        narrow = PAIR * HEAD
+        here = pl.ds(pl.multiple_of((pair * PAIR + side) * wide, wide), wide)
+        k_cols = pl.ds(pl.multiple_of(pair * narrow, narrow), narrow)
+        v_cols = pl.ds(pl.multiple_of(kv_width + pair * narrow, narrow), narrow)
+        attend_back_side(
+            side,
+            q_ref[:, here],
+            both_ref[:, k_cols],
+            both_ref[:, v_cols],
+            grad_att[:, here],
+            mask_ref[...] > 0.5,
+            lse_ref[pair],
+            turn_ref,
+            k_pair_ref,
+            v_pair_ref,
+        )
+        u = turn_ref[...]
+        grad_q[:, here] = (u * cos_ref[...] - swap_halves(u) * sin_ref[...]).astype(grad_q.dtype)
+        if side == PAIR - 1:
+            grad_kv[:, k_cols] = k_pair_ref[...]
+            grad_kv[:, v_cols] = v_pair_ref[...]
+
+    def key_rows(far):
+        at = lax.rem(z + 4 - far, 4)
+        return pl.ds(pl.multiple_of(at * tokens, tokens), tokens)
+
+    def pass_terms(hop):
+        return pltpu.make_async_remote_copy(
+            src_ref=hop_out.at[hop],
+            dst_ref=hop_in.at[hop],
+            send_sem=hop_send.at[hop],
+            recv_sem=hop_recv.at[hop],
+            device_id=target("z1"),
+            device_id_type=MESH,
+        )
+
+    def key_terms(hop):
+        if hop > 0:
+            pass_terms(hop - 1).wait()
+        if hop < 3:
+            own = grad_kv[key_rows(hop + 1), :]
+            if hop > 0:
+                own = (own.astype(jnp.float32) + hop_in[hop - 1].astype(jnp.float32)).astype(own.dtype)
+            hop_out[hop] = own
+            pass_terms(hop).start()
+        else:
+            own = grad_kv[key_rows(0), :].astype(jnp.float32) + hop_in[2].astype(jnp.float32)
+            for b in range(key_blocks):
+                u = own[:, b * block : (b + 1) * block]
+                if b < key_blocks // 2:
+                    u = u * cos_ref[...] - swap_halves(u) * sin_ref[...]
+                grad_both[:, b * block : (b + 1) * block] = u.astype(grad_both.dtype)
+
+    def built_copy(which, j, d):
+        return pltpu.make_async_copy(
+            built.at[which, d],
+            wall_ref.at[d // 16, lax.rem(d // 8, 2), lax.rem(d // 4, 2), lax.rem(d, 4), j],
+            built_sem.at[which],
+        )
+
+    def build(which, j, right_ref):
+        @pl.loop(0, 32, unroll=True)
+        def _(d):
+            left_ref[d] = turned[table[d * lead + j]]
+
+        for part in range(4):
+            left = left_ref[part * 8 : (part + 1) * 8].reshape(8 * rows, tokens)
+            value = dot(left, right_ref[...], NN).astype(built.dtype)
+            built[which, part * 8 : (part + 1) * 8] = value.reshape(8, rows, width)
+
+        @pl.loop(0, 32)
+        def _(d):
+            built_copy(which, j, d).start()
+
+    def finish_built(which):
+        pltpu.make_async_copy(built.at[which], built.at[which], built_sem.at[which]).wait()
+
+    half = lead // 2
+    attending = 2
+    passing = attending + KV_HEADS
+    building = passing + 5
+    stream(0).start()
+
     @pl.loop(0, rounds + stages - 1)
     def _(t):
+        for step in range(2):
+
+            @pl.when(t == step)
+            def _(step=step):
+                if step == 0:
+                    fill_mask(places, mask_ref)
+                    back_ref[...] = jnp.zeros_like(back_ref)
+                out_back(step * out_blocks // 2, (step + 1) * out_blocks // 2)
+
+        for side in range(PAIR):
+            since = t - attending
+
+            @pl.when((since >= 0) & (since < KV_HEADS) & (lax.rem(since + 64, 2) == side))
+            def _(side=side, since=since):
+                attend_back_step(since // 2, side)
+
+        for hop in range(4):
+
+            @pl.when(t == passing + hop)
+            def _(hop=hop):
+                key_terms(hop)
+                query_back(hop * query_blocks // 4, (hop + 1) * query_blocks // 4)
+
+        @pl.when(t == passing + 4)
+        def _():
+            key_back()
+
+        pair = t - building
+
+        @pl.when((pair >= 1) & (pair <= half))
+        def _():
+            finish_built(0)
+            finish_built(1)
+
+        @pl.when((pair >= 0) & (pair < half))
+        def _():
+            build(0, pair, normed_ref)
+
+        split = first_group - half
+
+        @pl.when((pair >= 0) & (pair < split))
+        def _():
+            build(1, half + pair, normed_ref)
+
+        @pl.when((pair >= split) & (pair < half))
+        def _():
+            build(1, half + pair, branch_ref)
+
         for step in range(len(SUM_HOPS) + 1):
 
-            @pl.when(t == SUM_START + step)
+            @pl.when(t == building + step)
             def _(step=step):
                 add_sums(step)
 
@@ -1218,8 +1553,30 @@
             if which >= far:
                 run(which - far, finish)
 
-
-def scatter_slots(grads_wall, gain_terms, caps, look=(4, 1)):
+    for route in range(4):
+        keep(route, counts[route] - 1).wait()
+
+
+def scatter_slots(
+    grads_wall,
+    gain_terms,
+    weights,
+    table,
+    places,
+    branch,
+    attended,
+    queries,
+    both,
+    lse,
+    normed,
+    hidden,
+    cosine,
+    sine,
+    lead,
+    first_group,
+    caps,
+    look=(4, 1),
+):
     rows, width = grads_wall.shape[1:]
     kind = grads_wall.dtype
     wall = grads_wall.reshape(2, 2, 2, 4, caps, rows, width)
@@ -1230,38 +1587,70 @@
         for stage in range(1, stages):
             extent = scatter_extent(route, stage)
             scratch.append(pltpu.VMEM((scatter_terms(route, stage),) + extent + (rows, width), kind))
-            if stage < stages - 1:
-                scratch.append(pltpu.VMEM(extent + (rows, width), kind))
+            last = stage == stages - 1
+            scratch.append(pltpu.VMEM(extent + (rows, width), jnp.float32 if last else kind))
     tile = (caps, rows, width)
+    tokens = hidden.shape[0]
+    number = cosine.shape[1] // rows
+    length, both_width = both.shape
+    dma = pltpu.SemaphoreType.DMA
+    scratch += [
+        dma((4, stages)),
+        dma((4, stages)),
+        dma((4, stages, max(counts))),
+        dma((4,)),
+        pltpu.VMEM((4,) + gain_terms.shape, jnp.float32),
+        pltpu.VMEM((6,) + gain_terms.shape, jnp.float32),
+        dma((6,)),
+        dma((6,)),
+        pltpu.VMEM((2, number, rows, width), kind),
+        pltpu.VMEM((tokens, width), kind),
+        pltpu.VMEM((tokens, width), kind),
+        pltpu.VMEM((length, both_width), kind),
+        pltpu.VMEM((tokens, both_width), kind),
+        pltpu.VMEM((length, PAIR * HEAD), kind),
+        pltpu.VMEM((length, PAIR * HEAD), kind),
+        pltpu.VMEM((tokens, GROUP * HEAD), jnp.float32),
+        pltpu.VMEM((3, tokens, both_width), kind),
+        pltpu.VMEM((3, tokens, both_width), kind),
+        pltpu.VMEM((weights.shape[0], rows, tokens), kind),
+        pltpu.VMEM((32, rows, tokens), kind),
+        pltpu.VMEM((2, 32, rows, width), kind),
+        pltpu.VMEM((tokens, length), jnp.float32),
+        dma((2,)),
+        dma((3,)),
+        dma((3,)),
+        dma((2,)),
+    ]
+    vmem = pl.BlockSpec(memory_space=pltpu.VMEM)
+    smem = pl.BlockSpec(memory_space=pltpu.SMEM)
+    anyw = pl.BlockSpec(memory_space=pl.ANY)
     out = pl.pallas_call(
-        functools.partial(scatter_kernel, look),
+        functools.partial(scatter_kernel, look, lead, first_group),
         out_shape=[
+            jax.ShapeDtypeStruct(wall.shape, kind),
             jax.ShapeDtypeStruct(tile, jnp.float32),
             jax.ShapeDtypeStruct(gain_terms.shape, jnp.float32),
+            jax.ShapeDtypeStruct((tokens, width), jnp.float32),
             jax.ShapeDtypeStruct((2, 2, 4) + tile, kind),
             jax.ShapeDtypeStruct((2, 4) + tile, kind),
             jax.ShapeDtypeStruct((4,) + tile, kind),
             jax.ShapeDtypeStruct((3, 2) + tile, kind),
             jax.ShapeDtypeStruct(tile, kind),
         ],
-        in_specs=[pl.BlockSpec(memory_space=pl.ANY), pl.BlockSpec(memory_space=pltpu.VMEM)],
-        out_specs=[pl.BlockSpec(memory_space=pltpu.VMEM)] * 2 + [pl.BlockSpec(memory_space=pl.ANY)] * 5,
-        scratch_shapes=scratch
-        + [
-            pltpu.SemaphoreType.DMA((4, stages)),
-            pltpu.SemaphoreType.DMA((4, stages)),
-            pltpu.SemaphoreType.DMA((4, stages, max(counts))),
-            pltpu.VMEM((4,) + gain_terms.shape, jnp.float32),
-            pltpu.VMEM((6,) + gain_terms.shape, jnp.float32),
-            pltpu.SemaphoreType.DMA((6,)),
-            pltpu.SemaphoreType.DMA((6,)),
-        ],
+        in_specs=[anyw, vmem, anyw, smem, smem] + [vmem] * 9,
+        out_specs=[anyw, anyw, vmem, vmem] + [anyw] * 5,
+        scratch_shapes=scratch,
+        input_output_aliases={0: 0},
         compiler_params=pltpu.CompilerParams(
-            collective_id=1, has_side_effects=True, vmem_limit_bytes=56 << 20
+            collective_id=1, has_side_effects=True, vmem_limit_bytes=62 << 20
         ),
         name="scatter_slots",
-    )(wall, gain_terms)
-    return out[0], out[1]
+    )(
+        wall, gain_terms, weights, table, places, branch, attended, queries, both, lse, normed,
+        hidden, cosine, sine,
+    )
+    return out[1], out[2], out[3]
 
 
 def shards(
@@ -1286,12 +1675,13 @@
     lead = layout[2][3]
     tokens = hidden_in.astype(jnp.float32)
     local_len = tokens.shape[0]
-    kv_width = KV_HEADS * HEAD
     first = lax.axis_index("fsdp") * local_len
     positions = first + jnp.arange(local_len, dtype=jnp.int32)
     places = jnp.concatenate([first[None].astype(jnp.int32), piece_starts[0]])
     cosine, sine = rope_tables(positions.astype(jnp.float32), 16 * tile_rows)
-    wall, gains_low, both, normed, queries, attended, lse, middle, normed_two = forward_attention(
+    (
+        wall, weights, gains_low, both, normed, queries, attended, lse, middle, normed_two
+    ) = forward_attention(
         master.astype(jnp.bfloat16),
         gain_master.astype(jnp.bfloat16),
         (slot_query, slot_both, slot_out),
@@ -1317,26 +1707,25 @@
     )
     gain_two_term = jnp.sum(grad_normed_two * middle * inv_two, axis=0)
     grad_branch = grad_middle.astype(jnp.bfloat16)
-    grad_attended, grads_wall = mix_back(slot_out, attended, grad_branch, wall, grads_wall)
-    grad_query, both_terms = attend_back(
-        places, queries, both, grad_attended, lse, cosine, sine
-    )
-    both_sum = lax.psum_scatter(both_terms, "fsdp", scatter_dimension=0, tiled=True).astype(
-        jnp.float32
-    )
-    grad_normed, grads_wall = project_back(slot_query, grad_query, normed, None, wall, grads_wall)
-    both_sum = both_sum.reshape(local_len, KV_HEADS // PAIR, 2, PAIR * HEAD)
-    grad_key = turn_back(both_sum[:, :, 0].reshape(local_len, kv_width), cosine, sine)
-    grad_value = both_sum[:, :, 1].reshape(local_len, kv_width)
-    grad_both = jnp.concatenate([grad_key, grad_value], axis=1).astype(jnp.bfloat16)
-    grad_normed, grads_wall = project_back(
-        slot_both, grad_both, normed, grad_normed, wall, grads_wall
+    weight_grad, gain_grad, grad_normed = backward_attention(
+        grads_wall,
+        gain_two_term,
+        weights,
+        (slot_query, slot_both, slot_out),
+        places,
+        grad_branch,
+        attended,
+        queries,
+        both,
+        lse,
+        normed,
+        hidden_in,
+        cosine,
+        sine,
+        layout,
+        caps,
     )
     keep_slot = filled_mask(owners, layout, lax.axis_index(("dp", "fsdp")))[:, None, None]
-    gain_one_term = jnp.sum(grad_normed * tokens * inv_one, axis=0)
-    weight_grad, gain_grad = scatter_any(
-        grads_wall, jnp.stack([gain_one_term, gain_two_term]), caps
-    )
     weight_grad = jnp.where(keep_slot, weight_grad, 0.0)
     scaled_one = grad_normed * gain_attn
     input_grad = (

time: 1520 us -> 1460 us (0.961)
  waiting for transfers between devices: 22.8 us -> 0 us
  Pallas kernels: 1390 us -> 1370 us
    pallas_call x5 -> x1, Pallas kernels: 664 us -> 640 us  [scatter_slots(): pl.pallas_call(functools.partial(scatter_kernel, look, lead, first_group)...]
    reduce_scatter x1 -> x0, waiting for transfers between devices: 22.8 us -> none  [shards(): lax.psum_scatter(both_terms, 'fsdp', scatter_dimension=0, tiled=True)]
  transfers between devices with their start and end apart: 1 -> 0, of which waited for: 1 -> 0; matrix products, arithmetic and copies ran while one was open for 0% -> 0% of each run, Pallas kernels for 1% -> 0%
where the time goes in v6:
time: 1460 us; the launch traced here: 1450 us
  Pallas kernels  1370 us (94%)
  other arithmetic  69.4 us (5%)
    pallas_call x1, Pallas kernels, scatter_slots(): pl.pallas_call(functools.partial(scatter_kernel, look, lead, first_group)...  640 us
    pallas_call x1, Pallas kernels, gather_slots(): pl.pallas_call(functools.partial(gather_kernel, lead), out_shape=[jax.Sha...  624 us
    pallas_call x1, Pallas kernels, ffn_call(): pl.pallas_call(functools.partial(ffn_kernel, group), grid_spec=pltpu.Pref...  102 us

profile of v6, /device:TPU:0, one launch (start us, length us, event | category | flops | bytes accessed | tf_op | source)
XLA Modules:
  0.0 1446.0 jit_solution(18425574565822322428)
XLA Ops:
  0.6 1.2 pad_add_fusion.2.places
  1.9 0.7 convert_element_type.54
  2.6 0.8 slice.35
  3.3 0.2 convert_reduce_fusion.3
  3.5 1.4 fusion.13
  4.9 0.6 iota_compare_fusion.7
  5.6 0.7 slice.34
  6.3 0.2 convert_reduce_fusion.2
  6.5 1.3 fusion.12
  7.8 0.1 multiply_add_fusion.1.table
  7.9 0.0 copy-start.5
  7.9 0.7 iota_compare_fusion.8
  8.6 0.7 select_reduce_fusion.table
  9.3 0.8 slice.39
  10.1 0.3 convert_reduce_fusion.1
  10.3 0.6 pad.8.gain_ref
  10.9 0.8 slice.36
  11.7 0.5 convert_reduce_fusion
  12.2 1.4 convert_reduce_fusion.4
  13.6 2.0 convert_reduce_fusion.5
  15.6 0.6 iota_compare_fusion.5
  16.2 0.7 iota_compare_fusion.6
  16.9 0.1 pad_add_fusion.1
  17.0 0.2 fusion.9
  17.2 0.8 copy.25.cos_ref
  18.1 0.8 copy.26.sin_ref
  18.9 6.9 convert_element_type.53.mine_ref
  25.8 0.0 copy-done.5
  25.8 624.1 %gather_slots.1 = (bf16[2,2,2,4,76,16,2048]{6,5,4,3,2,1,0:T(8,128)(2,1)}, bf16[2,2,2,4,16,128]{5,4,3,2,1,0:T(8,128)(2,1)}, bf16[320,16,2048]{2,1,0:T(8,128)(2,1)...) custom-call(bf16[76,16,2048]{2,1,0:T(8,128)(2,1)} %convert_element_t, ...), custom_call_target="tpu_custom_call" | custom-call | tf_op jit(solution)/shard_map/gather_slots/pallas_call | solution.py:1046
  649.9 1.8 multiply_reduce_fusion.2
  651.8 0.9 fusion.16
  652.7 0.0 copy-start
  652.7 102.4 %ffn.1 = (f32[256,2048]{1,0:T(8,128)}, f32[256,2048]{1,0:T(8,128)}, bf16[2432,16,2048]{2,1,0:T(8,128)(2,1)}) custom-call(s32[512]{0:T(512)} %get-tuple-element.78.gate_s, s32[512]{0:T(512)} %get-tuple-element.79.up_s, s32[512]{0:T(512)} %get-tuple-element.66.down_s, bf16[256,2048]{1,0:T(8,128)(2,1)} %get-tuple-element.27.normed_ref, ...), custom_call_target="tpu_custom_call" | custom-call | tf_op jit(solution)/shard_map/ffn/pallas_call | solution.py:671
  755.1 0.0 copy-start.3
  755.1 0.0 copy-start.4
  755.2 0.0 copy-done
  755.2 2.3 multiply_reduce_fusion
  757.5 0.0 copy-done.3
  757.5 0.1 copy-done.4
  757.6 4.4 fusion.15
  762.0 0.6 pad.9.gain_ref
  762.6 639.6 %scatter_slots.1 = (bf16[2,2,2,4,76,16,2048]{6,5,4,3,2,1,0:T(8,128)(2,1)}, f32[76,16,2048]{2,1,0:T(8,128)}, f32[8,2048]{1,0:T(8,128)}, f32[256,2048]{1,0:T(8,128...) custom-call(bf16[2,2,2,4,76,16,2048]{6,5,4,3,2,1,0:T(8,128)(2,1)} %b, ...), custom_call_target="tpu_custom_call", output_to_operand_aliasing={{0}: (0, {})} | custom-call | tf_op jit(solution)/shard_map/scatter_slots/pallas_call | solution.py:1628
  1402.2 0.0 copy-start.2
  1402.2 0.0 copy-done.1
  1402.2 2.2 fusion.2
  1404.5 0.0 copy-start.6
  1404.5 0.0 copy-start.7
  1404.5 0.0 copy-start.8
  1404.5 0.0 copy-done.2
  1404.5 3.5 fusion.4
  1408.1 0.8 slice.42
  1408.9 0.0 copy-done.6
  1408.9 0.0 copy-done.7
  1408.9 0.0 copy-done.8
  1408.9 0.7 multiply_add_fusion.3
  1409.6 0.0 slice-start.4
  1409.6 0.0 slice-start.5
  1409.6 18.0 %broadcast_select_fusion = (f32[76,16,2048]{2,1,0:T(8,128)}, f32[76,16,2048]{2,1,0:T(8,128)}) fusion(pred[76]{0:T(512)(128)(4,1)S(1)} %pad_add_fusion.1, f32[76,16,2048]{2,1,0:T(8,128)} %param.16, f32[76,16,2048]{2,1,0:T(8,128)} %get-tuple-element.40), kind=kLoop, calls=%fused_computation.4 | loop fusion | flops 14942208 | bytes 39845964 | tf_op jit(solution)/shard_map/jit(_where)/select_n | solution.py:1741
  1427.6 0.0 slice-done
  1427.6 0.0 slice-done.3
  1427.6 0.0 slice-done.1
  1427.6 1.0 slice-done.4
  1428.6 0.4 slice-done.5
  1429.0 16.7 %broadcast_select_fusion.1 = (f32[76,16,2048]{2,1,0:T(8,128)}, f32[76,16,2048]{2,1,0:T(8,128)}) fusion(pred[76]{0:T(512)(128)(4,1)S(1)} %pad_add_fusion.1, f32[76,16,2048]{2,1,0:T(8,128)} %get-tuple-element.51, f32[76,16,2048]{2,1,0:T(8,128)} %param.15, f32[76,16,2048]{2,1,0:T(8,128)S(1)} %bitcast.10, f32[76,16,2048]{2,1,0:T(8,128)S(1)} %bitcast.12), kind=kLoop, calls=%fused_computation.5 | loop fusion | flops 39845888 | bytes 59768908 | tf_op jit(solution)/shard_map/jit(_where)/select_n | solution.py:1740
  (17 shorter events, 0.1 us)
Async XLA Ops:
  7.9 17.9 %copy-start.5 = (s32[320]{0:T(512)}, s32[320]{0:T(512)S(1)}, u32[]{:S(2)}) copy-start(s32[320]{0:T(512)S(1)} %multiply_add_fusion.1.table) | copy-start | bytes 3844
  652.7 102.5 %copy-start = (f32[256,2048]{1,0:T(8,128)S(1)}, f32[256,2048]{1,0:T(8,128)}, u32[]{:S(2)}) copy-start(f32[256,2048]{1,0:T(8,128)} %get-tuple-element.26) | copy-start | bytes 6291460
  755.1 2.3 copy-start.3
  755.1 2.5 copy-start.4
  762.6 639.6 %copy-start.1 = (bf16[256,2048]{1,0:T(8,128)(2,1)S(1)}, bf16[256,2048]{1,0:T(8,128)(2,1)}, u32[]{:S(2)}) copy-start(bf16[256,2048]{1,0:T(8,128)(2,1)} %hidden_ref.3) | copy-start | bytes 3145732
  1402.2 2.3 copy-start.2
  1404.5 4.5 copy-start.6
  1404.5 4.4 copy-start.7
  1404.5 4.4 copy-start.8
  1409.6 18.0 %slice-start = ((s8[9961472]{0:T(1024)(128)(4,1)}), s8[4194304]{0:T(1024)(128)(4,1)S(1)}, s32[]{:S(2)}) async-start(s8[9961472]{0:T(1024)(128)(4,1)} %bitcast.9), calls=%async_computation | async-start | bytes 8388608
  1409.6 18.0 %slice-start.3 = ((s8[9961472]{0:T(1024)(128)(4,1)}), s8[4194304]{0:T(1024)(128)(4,1)S(1)}, s32[]{:S(2)}) async-start(s8[9961472]{0:T(1024)(128)(4,1)} %bitcast.11), calls=%async_computation.3 | async-start | bytes 8388608
  1409.6 18.0 %slice-start.1 = ((s8[9961472]{0:T(1024)(128)(4,1)}), s8[4194304]{0:T(1024)(128)(4,1)S(1)}, s32[]{:S(2)}) async-start(s8[9961472]{0:T(1024)(128)(4,1)} %bitcast.9), calls=%async_computation.1 | async-start | bytes 8388608
  1409.6 18.0 %slice-start.2 = ((s8[9961472]{0:T(1024)(128)(4,1)}), s8[1572864]{0:T(1024)(128)(4,1)S(1)}, s32[]{:S(2)}) async-start(s8[9961472]{0:T(1024)(128)(4,1)} %bitcast.9), calls=%async_computation.2 | async-start | bytes 3145728
  1409.6 19.0 %slice-start.4 = ((s8[9961472]{0:T(1024)(128)(4,1)}), s8[4194304]{0:T(1024)(128)(4,1)S(1)}, s32[]{:S(2)}) async-start(s8[9961472]{0:T(1024)(128)(4,1)} %bitcast.11), calls=%async_computation.4 | async-start | bytes 8388608
  1409.6 19.4 %slice-start.5 = ((s8[9961472]{0:T(1024)(128)(4,1)}), s8[1572864]{0:T(1024)(128)(4,1)S(1)}, s32[]{:S(2)}) async-start(s8[9961472]{0:T(1024)(128)(4,1)} %bitcast.11), calls=%async_computation.5 | async-start | bytes 3145728

commit v7 on v6

--- a/solution.py
+++ b/solution.py
@@ -719,31 +719,51 @@
     pl.semaphore_wait(barrier, len(hops))
 
 
-def split_slots(caps):
-    small = caps // 6
+GATHER_PLAN = (3, (0, 0, 0, 0), (10, 6), (11, 3))
+SCATTER_PLAN = (3, (4, 4, 0, 0), (4, 6), (40, 0))
+
+
+def split_slots(caps, plan):
+    small = caps * plan[0] // 16
     third = (caps - 2 * small) // 2
     counts = (small, small, third, caps - 2 * small - third)
     starts = (0, small, 2 * small, 2 * small + third)
     return counts, starts
 
 
-GATHER_DELAYS = (0, 1, 0, 0)
-SCATTER_DELAYS = (4, 4, 0, 0)
-
-
-def round_count(counts, delays):
-    return max(
-        delay + (2 * count - 1 if route < 2 else count)
-        for route, (count, delay) in enumerate(zip(counts, delays))
-    )
-
-
-def turn(route, at, counts, delays):
+def round_count(counts, plan):
+    share, delays, (dense, extra), (gap, pause) = plan
+    ends = []
+    for route in range(4):
+        at = [
+            t
+            for t in range(200)
+            if (t % 2 == 0 or dense <= t < dense + extra if route < 2 else not gap <= t < gap + pause)
+        ]
+        ends.append(delays[route] + at[counts[route] - 1] + 1)
+    return max(ends)
+
+
+def passed(at, edge):
+    return (at - edge + 64) // 64
+
+
+def turn(route, at, counts, plan):
+    share, delays, (dense, extra), (gap, pause) = plan
     at = at - delays[route]
     if route < 2:
-        live = (at >= 0) & (lax.rem(at + 64, 2) == 0) & (at < 2 * counts[route])
-        return live, at // 2
-    return (at >= 0) & (at < counts[route]), at
+        begun = passed(at, dense)
+        over = passed(at, dense + extra)
+        slow = at // 2
+        quick = dense // 2 + at - dense
+        late = dense // 2 + extra + (at - dense - extra) // 2
+        index = (1 - begun) * slow + (begun - over) * quick + over * late
+        even = lax.rem(at + 64, 2) == 0
+        live = (at >= 0) & (even | (begun - over == 1)) & (index < counts[route])
+        return live, index
+    index = at - pause * passed(at, gap)
+    live = (at >= 0) & ((at < gap) | (at >= gap + pause)) & (index < counts[route])
+    return live, index
 
 
 def slot_of(route, index, counts, starts, lead, early):
@@ -812,8 +832,8 @@
     hop_recv,
 ):
     y, x, c, z = position()
-    counts, starts = split_slots(mine_ref.shape[0])
-    rounds = round_count(counts, GATHER_DELAYS)
+    counts, starts = split_slots(mine_ref.shape[0], GATHER_PLAN)
+    rounds = round_count(counts, GATHER_PLAN)
     own = pltpu.make_async_copy(mine_ref, wall_ref.at[y, x, c, z], own_sem.at[0])
     own_gain = pltpu.make_async_copy(gain_ref, gains_ref.at[y, x, c, z], own_sem.at[1])
     own.start()
@@ -961,7 +981,7 @@
         inv = lax.rsqrt(jnp.mean(middle * middle, axis=1, keepdims=True) + norm_eps)
         normed_two_ref[...] = (middle * inv * all_gains_ref[1:2, :]).astype(normed_two_ref.dtype)
 
-    start = GATHER_DELAYS[3] + lead // 2 - 1 + stages
+    start = GATHER_PLAN[1][3] + lead // 2 - 1 + stages
     keep_both = pltpu.make_async_copy(keys, both_ref, side_sem.at[3])
 
     @pl.loop(0, rounds + stages)
@@ -971,7 +991,7 @@
                 if route == 4:
                     live, index = t == stage, 0
                 else:
-                    live, index = turn(route, t - stage, counts, GATHER_DELAYS)
+                    live, index = turn(route, t - stage, counts, GATHER_PLAN)
 
                 @pl.when(live)
                 def _(stage=stage, route=route, index=index):
@@ -1035,7 +1055,7 @@
     caps, rows, width = low_tiles.shape
     tokens = hidden.shape[0]
     length = tokens * 4
-    counts, starts = split_slots(caps)
+    counts, starts = split_slots(caps, GATHER_PLAN)
     kind = low_tiles.dtype
     vmem = pl.BlockSpec(memory_space=pltpu.VMEM)
     smem = pl.BlockSpec(memory_space=pltpu.SMEM)
@@ -1167,8 +1187,8 @@
 ):
     y, x, c, z = position()
     caps, rows, width = out_ref.shape
-    counts, starts = split_slots(caps)
-    rounds = round_count(counts, SCATTER_DELAYS)
+    counts, starts = split_slots(caps, SCATTER_PLAN)
+    rounds = round_count(counts, SCATTER_PLAN)
     stages = len(SCATTER_ROUTES[0])
     held = {}
     made = {}
@@ -1478,8 +1498,7 @@
     building = passing + 5
     stream(0).start()
 
-    @pl.loop(0, rounds + stages - 1)
-    def _(t):
+    def beside(t):
         for step in range(2):
 
             @pl.when(t == step)
@@ -1534,18 +1553,22 @@
             def _(step=step):
                 add_sums(step)
 
+    @pl.loop(0, rounds + stages - 1)
+    def _(t):
         items = [(stage, route) for stage in range(stages - 1, -1, -1) for route in range(4)]
 
         def run(which, work):
             stage, route = items[which]
-            live, index = turn(route, t - stage, counts, SCATTER_DELAYS)
+            live, index = turn(route, t - stage, counts, SCATTER_PLAN)
 
             @pl.when(live)
             def _():
                 work(route, stage, index)
 
-        far, near = look
+        far, near, place_beside = look
         for which in range(len(items) + far):
+            if which == place_beside:
+                beside(t)
             if which < len(items):
                 run(which, early)
             if far - near <= which < len(items) + far - near:
@@ -1575,12 +1598,12 @@
     lead,
     first_group,
     caps,
-    look=(4, 1),
+    look=(4, 1, 16),
 ):
     rows, width = grads_wall.shape[1:]
     kind = grads_wall.dtype
     wall = grads_wall.reshape(2, 2, 2, 4, caps, rows, width)
-    counts, starts = split_slots(caps)
+    counts, starts = split_slots(caps, SCATTER_PLAN)
     stages = len(SCATTER_ROUTES[0])
     scratch = []
     for route in range(4):

time: 1460 us -> 1410 us (0.966)
  Pallas kernels: 1370 us -> 1320 us
    pallas_call x1, Pallas kernels: 624 us -> 602 us  [gather_slots(): pl.pallas_call(functools.partial(gather_kernel, lead), out_shape=[jax.Sha...]
    pallas_call x1, Pallas kernels: 640 us -> 618 us  [scatter_slots(): pl.pallas_call(functools.partial(scatter_kernel, look, lead, first_group)...]
where the time goes in v7:
time: 1410 us; the launch traced here: 1400 us
  Pallas kernels  1320 us (94%)
  other arithmetic  69.4 us (5%)
    pallas_call x1, Pallas kernels, scatter_slots(): pl.pallas_call(functools.partial(scatter_kernel, look, lead, first_group)...  618 us
    pallas_call x1, Pallas kernels, gather_slots(): pl.pallas_call(functools.partial(gather_kernel, lead), out_shape=[jax.Sha...  602 us
    pallas_call x1, Pallas kernels, ffn_call(): pl.pallas_call(functools.partial(ffn_kernel, group), grid_spec=pltpu.Pref...  102 us

profile of v7, /device:TPU:0, one launch (start us, length us, event | category | flops | bytes accessed | tf_op | source)
XLA Modules:
  0.0 1402.4 jit_solution(7123130071025829728)
XLA Ops:
  0.6 1.2 pad_add_fusion.2.places
  1.9 0.7 convert_element_type.54
  2.6 0.8 slice.35
  3.3 0.2 convert_reduce_fusion.3
  3.5 1.4 fusion.13
  4.9 0.6 iota_compare_fusion.7
  5.6 0.7 slice.34
  6.3 0.2 convert_reduce_fusion.2
  6.5 1.3 fusion.12
  7.8 0.1 multiply_add_fusion.1.table
  7.9 0.0 copy-start.5
  7.9 0.7 iota_compare_fusion.8
  8.6 0.7 select_reduce_fusion.table
  9.3 0.8 slice.39
  10.1 0.3 convert_reduce_fusion.1
  10.3 0.6 pad.8.gain_ref
  10.9 0.8 slice.36
  11.7 0.5 convert_reduce_fusion
  12.2 1.4 convert_reduce_fusion.4
  13.6 2.0 convert_reduce_fusion.5
  15.6 0.6 iota_compare_fusion.5
  16.2 0.7 iota_compare_fusion.6
  16.9 0.1 pad_add_fusion.1
  17.0 0.2 fusion.9
  17.2 0.8 copy.25.cos_ref
  18.1 0.8 copy.26.sin_ref
  18.9 6.9 convert_element_type.53.mine_ref
  25.8 0.0 copy-done.5
  25.8 601.7 %gather_slots.1 = (bf16[2,2,2,4,76,16,2048]{6,5,4,3,2,1,0:T(8,128)(2,1)}, bf16[2,2,2,4,16,128]{5,4,3,2,1,0:T(8,128)(2,1)}, bf16[320,16,2048]{2,1,0:T(8,128)(2,1)...) custom-call(bf16[76,16,2048]{2,1,0:T(8,128)(2,1)} %convert_element_t, ...), custom_call_target="tpu_custom_call" | custom-call | tf_op jit(solution)/shard_map/gather_slots/pallas_call | solution.py:1066
  627.5 1.8 multiply_reduce_fusion.2
  629.3 0.9 fusion.16
  630.3 0.0 copy-start
  630.3 102.4 %ffn.1 = (f32[256,2048]{1,0:T(8,128)}, f32[256,2048]{1,0:T(8,128)}, bf16[2432,16,2048]{2,1,0:T(8,128)(2,1)}) custom-call(s32[512]{0:T(512)} %get-tuple-element.78.gate_s, s32[512]{0:T(512)} %get-tuple-element.79.up_s, s32[512]{0:T(512)} %get-tuple-element.66.down_s, bf16[256,2048]{1,0:T(8,128)(2,1)} %get-tuple-element.27.normed_ref, ...), custom_call_target="tpu_custom_call" | custom-call | tf_op jit(solution)/shard_map/ffn/pallas_call | solution.py:671
  732.7 0.0 copy-start.3
  732.7 0.0 copy-start.4
  732.7 0.0 copy-done
  732.7 2.3 multiply_reduce_fusion
  735.0 0.0 copy-done.3
  735.1 0.1 copy-done.4
  735.2 4.4 fusion.15
  739.6 0.6 pad.9.gain_ref
  740.2 618.5 %scatter_slots.1 = (bf16[2,2,2,4,76,16,2048]{6,5,4,3,2,1,0:T(8,128)(2,1)}, f32[76,16,2048]{2,1,0:T(8,128)}, f32[8,2048]{1,0:T(8,128)}, f32[256,2048]{1,0:T(8,128...) custom-call(bf16[2,2,2,4,76,16,2048]{6,5,4,3,2,1,0:T(8,128)(2,1)} %b, ...), custom_call_target="tpu_custom_call", output_to_operand_aliasing={{0}: (0, {})} | custom-call | tf_op jit(solution)/shard_map/scatter_slots/pallas_call | solution.py:1651
  1358.7 0.0 copy-start.2
  1358.7 0.0 copy-done.1
  1358.7 2.2 fusion.2
  1360.9 0.0 copy-start.6
  1360.9 0.0 copy-start.7
  1360.9 0.0 copy-start.8
  1361.0 0.0 copy-done.2
  1361.0 3.5 fusion.4
  1364.5 0.8 slice.42
  1365.4 0.0 copy-done.6
  1365.4 0.0 copy-done.7
  1365.4 0.0 copy-done.8
  1365.4 0.7 multiply_add_fusion.3
  1366.1 0.0 slice-start.4
  1366.1 0.0 slice-start.5
  1366.1 18.0 %broadcast_select_fusion = (f32[76,16,2048]{2,1,0:T(8,128)}, f32[76,16,2048]{2,1,0:T(8,128)}) fusion(pred[76]{0:T(512)(128)(4,1)S(1)} %pad_add_fusion.1, f32[76,16,2048]{2,1,0:T(8,128)} %param.16, f32[76,16,2048]{2,1,0:T(8,128)} %get-tuple-element.40), kind=kLoop, calls=%fused_computation.4 | loop fusion | flops 14942208 | bytes 39845964 | tf_op jit(solution)/shard_map/jit(_where)/select_n | solution.py:1764
  1384.0 0.0 slice-done
  1384.0 0.0 slice-done.3
  1384.0 0.0 slice-done.1
  1384.1 1.0 slice-done.4
  1385.1 0.4 slice-done.5
  1385.5 16.7 %broadcast_select_fusion.1 = (f32[76,16,2048]{2,1,0:T(8,128)}, f32[76,16,2048]{2,1,0:T(8,128)}) fusion(pred[76]{0:T(512)(128)(4,1)S(1)} %pad_add_fusion.1, f32[76,16,2048]{2,1,0:T(8,128)} %get-tuple-element.51, f32[76,16,2048]{2,1,0:T(8,128)} %param.15, f32[76,16,2048]{2,1,0:T(8,128)S(1)} %bitcast.10, f32[76,16,2048]{2,1,0:T(8,128)S(1)} %bitcast.12), kind=kLoop, calls=%fused_computation.5 | loop fusion | flops 39845888 | bytes 59768908 | tf_op jit(solution)/shard_map/jit(_where)/select_n | solution.py:1763
  (17 shorter events, 0.1 us)
Async XLA Ops:
  7.9 17.9 %copy-start.5 = (s32[320]{0:T(512)}, s32[320]{0:T(512)S(1)}, u32[]{:S(2)}) copy-start(s32[320]{0:T(512)S(1)} %multiply_add_fusion.1.table) | copy-start | bytes 3844
  630.3 102.5 %copy-start = (f32[256,2048]{1,0:T(8,128)S(1)}, f32[256,2048]{1,0:T(8,128)}, u32[]{:S(2)}) copy-start(f32[256,2048]{1,0:T(8,128)} %get-tuple-element.26) | copy-start | bytes 6291460
  732.7 2.3 copy-start.3
  732.7 2.5 copy-start.4
  740.2 618.5 %copy-start.1 = (bf16[256,2048]{1,0:T(8,128)(2,1)S(1)}, bf16[256,2048]{1,0:T(8,128)(2,1)}, u32[]{:S(2)}) copy-start(bf16[256,2048]{1,0:T(8,128)(2,1)} %hidden_ref.3) | copy-start | bytes 3145732
  1358.7 2.3 copy-start.2
  1360.9 4.5 copy-start.6
  1360.9 4.4 copy-start.7
  1360.9 4.4 copy-start.8
  1366.0 18.0 %slice-start = ((s8[9961472]{0:T(1024)(128)(4,1)}), s8[4194304]{0:T(1024)(128)(4,1)S(1)}, s32[]{:S(2)}) async-start(s8[9961472]{0:T(1024)(128)(4,1)} %bitcast.9), calls=%async_computation | async-start | bytes 8388608
  1366.0 18.0 %slice-start.3 = ((s8[9961472]{0:T(1024)(128)(4,1)}), s8[4194304]{0:T(1024)(128)(4,1)S(1)}, s32[]{:S(2)}) async-start(s8[9961472]{0:T(1024)(128)(4,1)} %bitcast.11), calls=%async_computation.3 | async-start | bytes 8388608
  1366.1 18.0 %slice-start.1 = ((s8[9961472]{0:T(1024)(128)(4,1)}), s8[4194304]{0:T(1024)(128)(4,1)S(1)}, s32[]{:S(2)}) async-start(s8[9961472]{0:T(1024)(128)(4,1)} %bitcast.9), calls=%async_computation.1 | async-start | bytes 8388608
  1366.1 18.0 %slice-start.2 = ((s8[9961472]{0:T(1024)(128)(4,1)}), s8[1572864]{0:T(1024)(128)(4,1)S(1)}, s32[]{:S(2)}) async-start(s8[9961472]{0:T(1024)(128)(4,1)} %bitcast.9), calls=%async_computation.2 | async-start | bytes 3145728
  1366.1 19.0 %slice-start.4 = ((s8[9961472]{0:T(1024)(128)(4,1)}), s8[4194304]{0:T(1024)(128)(4,1)S(1)}, s32[]{:S(2)}) async-start(s8[9961472]{0:T(1024)(128)(4,1)} %bitcast.11), calls=%async_computation.4 | async-start | bytes 8388608
  1366.1 19.4 %slice-start.5 = ((s8[9961472]{0:T(1024)(128)(4,1)}), s8[1572864]{0:T(1024)(128)(4,1)S(1)}, s32[]{:S(2)}) async-start(s8[9961472]{0:T(1024)(128)(4,1)} %bitcast.11), calls=%async_computation.5 | async-start | bytes 3145728

commit v8 on v7

--- a/solution.py
+++ b/solution.py
@@ -4,6 +4,7 @@
 import jax.experimental.pallas as pl
 import jax.experimental.pallas.tpu as pltpu
 import jax.numpy as jnp
+import numpy as np
 from jax import lax
 from jax.sharding import PartitionSpec as P
 
@@ -57,22 +58,18 @@
 
 
 def slot_numbers(owners, layout, caps):
-    placed = []
-    for first_tile, number, capacity, first_slot in layout:
-        mine = owners[first_tile : first_tile + number]
-        order = jnp.arange(number, dtype=jnp.int32)
-        earlier = (mine[:, None] == mine[None, :]) & (order[None, :] < order[:, None])
-        ranked = jnp.sum(earlier.astype(jnp.int32), axis=1)
-        placed.append(mine * caps + first_slot + ranked)
-    return placed
-
-
-def filled_mask(owners, layout, device):
-    masks = []
-    for first_tile, number, capacity, first_slot in layout:
-        count = jnp.sum((owners[first_tile : first_tile + number] == device).astype(jnp.int32))
-        masks.append(jnp.arange(capacity, dtype=jnp.int32) < count)
-    return jnp.concatenate(masks)
+    numbers = [entry[1] for entry in layout]
+    group = jnp.asarray(np.repeat(np.arange(4), numbers), jnp.int32)
+    base = jnp.asarray(np.repeat([entry[3] for entry in layout], numbers), jnp.int32)
+    kind = owners * 4 + group
+    order = jnp.arange(kind.shape[0], dtype=jnp.int32)
+    earlier = (kind[:, None] == kind[None, :]) & (order[:, None] < order[None, :])
+    return owners * caps + base + jnp.sum(earlier.astype(jnp.int32), axis=0)
+
+
+def filled_mask(slots, caps, device):
+    here = device * caps + jnp.arange(caps, dtype=jnp.int32)
+    return jnp.any(slots[None, :] == here[:, None], axis=1)
 
 
 def rope_tables(positions, block):
@@ -100,11 +97,17 @@
     return (lax.axis_size("dp"), lax.axis_size("fsdp")) == (8, 4)
 
 
-def forward_attention(low_tiles, low_gains, slots, places, hidden_in, cosine, sine, lead):
+def attention_slots(slots, layout, width, tile_rows):
+    query = width // tile_rows
+    return slots[:query], slots[query : layout[1][0]], slots[layout[1][0] : layout[2][0]]
+
+
+def forward_attention(low_tiles, low_gains, slots, places, hidden_in, cosine, sine, layout):
     caps, tile_rows, width = low_tiles.shape
-    slot_query, slot_both, slot_out = slots
+    lead = layout[2][3]
+    slot_query, slot_both, slot_out = attention_slots(slots, layout, width, tile_rows)
     if tuned_mesh():
-        table = jnp.concatenate(slots)
+        table = slots[: layout[2][0]]
         table = table // caps * lead + lax.rem(table, caps)
         (wall, weights, both, gains, normed, queries, attended, lse, middle, normed_two) = (
             gather_slots(low_tiles, low_gains, table, places, hidden_in, cosine, sine, lead)
@@ -126,7 +129,9 @@
 
 def backward_attention(
     grads_wall,
-    gain_two_term,
+    gain_terms,
+    grad_middle,
+    gains,
     weights,
     slots,
     places,
@@ -142,20 +147,20 @@
     layout,
     caps,
 ):
-    slot_query, slot_both, slot_out = slots
     local_len, width = normed.shape
+    tile_rows = weights.shape[1]
+    slot_query, slot_both, slot_out = attention_slots(slots, layout, width, tile_rows)
     kv_width = KV_HEADS * HEAD
     if tuned_mesh():
         lead = layout[2][3]
-        table = jnp.concatenate(slots)
+        table = slots[: layout[2][0]]
         table = table // caps * lead + lax.rem(table, caps)
         order = jnp.arange(table.shape[0], dtype=jnp.int32)
         here = jnp.arange(32 * lead, dtype=jnp.int32)
         tile_at = jnp.sum(jnp.where(table[None, :] == here[:, None], order[None, :], 0), axis=1)
-        terms = jnp.pad(gain_two_term[None, :], ((1, 6), (0, 0)))
-        grads, total, grad_normed = scatter_slots(
+        grads, total, input_grad = scatter_slots(
             grads_wall,
-            terms,
+            gain_terms,
             weights,
             tile_at,
             places,
@@ -168,13 +173,15 @@
             hidden_in,
             cosine,
             sine,
+            grad_middle,
+            gains,
             lead,
             layout[0][2],
             caps,
         )
         part = width // 32
         device = lax.axis_index(("dp", "fsdp"))
-        return grads, lax.dynamic_slice_in_dim(total[:2], device * part, part, 1), grad_normed
+        return grads, lax.dynamic_slice_in_dim(total[:2], device * part, part, 1), input_grad
     grad_attended, grads_wall = mix_back(slot_out, attended, branch, weights, grads_wall)
     grad_query, both_terms = attend_back(
         places, queries, both, grad_attended, lse, cosine, sine
@@ -193,10 +200,13 @@
     tokens = hidden_in.astype(jnp.float32)
     inv_one = lax.rsqrt(jnp.mean(tokens * tokens, axis=1, keepdims=True) + norm_eps)
     gain_one_term = jnp.sum(grad_normed * tokens * inv_one, axis=0)
-    gain_terms = jnp.stack([gain_one_term, gain_two_term])
+    gain_terms = jnp.stack([gain_one_term, gain_terms[1]])
+    scaled = grad_normed * gains[0]
+    part = jnp.mean(scaled * tokens, axis=1, keepdims=True)
+    input_grad = grad_middle + inv_one * scaled - tokens * inv_one**3 * part
     grads = lax.psum_scatter(grads_wall, ("dp", "fsdp"), scatter_dimension=0, tiled=True)
     gain_grad = lax.psum_scatter(gain_terms, ("dp", "fsdp"), scatter_dimension=1, tiled=True)
-    return grads.astype(jnp.float32), gain_grad, grad_normed
+    return grads.astype(jnp.float32), gain_grad, input_grad
 
 
 VMEM_ASK = 56 << 20
@@ -593,10 +603,9 @@
     )(places, queries, both, both, grad, lse, cosine, sine)
 
 
-def ffn_kernel(group, gate_s, up_s, down_s, normed_ref, cot_ref, wall_ref, out_ref, back_ref, grads_ref, held, made, load_sem, store_sem):
+def ffn_kernel(group, offsets, table, normed_ref, cot_ref, middle_ref, gains_ref, wall_ref, block_ref, grad_ref, branch_ref, gain_ref, grads_ref, out_ref, back_ref, held, made, load_sem, store_sem):
     step = pl.program_id(0)
     steps = pl.num_programs(0)
-    tables = (gate_s, up_s, down_s)
     tile_rows = wall_ref.shape[1]
     width = wall_ref.shape[2]
     rows = group * tile_rows
@@ -605,7 +614,7 @@
         for kind in range(3):
             @pl.loop(0, group, unroll=True)
             def _(t, kind=kind):
-                pltpu.make_async_copy(wall_ref.at[tables[kind][at * group + t]], held.at[buf, kind, t], load_sem.at[buf]).start()
+                pltpu.make_async_copy(wall_ref.at[table[offsets[kind] + at * group + t]], held.at[buf, kind, t], load_sem.at[buf]).start()
 
     def drain(buf):
         pltpu.make_async_copy(made.at[buf], made.at[buf], store_sem.at[buf]).wait()
@@ -630,8 +639,7 @@
 
     normed = normed_ref[...]
     cot = cot_ref[...]
-    w_gate = held[buf, 0].reshape(rows, width)
-    w_up = held[buf, 1].reshape(rows, width)
+    w_both = held[buf, 0:2].reshape(2 * rows, width)
     w_down = held[buf, 2].reshape(rows, width)
     nt = (((1,), (1,)), ((), ()))
     nn = (((1,), (0,)), ((), ()))
@@ -640,46 +648,72 @@
     def dot(a, b, dims):
         return lax.dot_general(a, b, dims, preferred_element_type=jnp.float32)
 
-    gate = dot(normed, w_gate, nt)
-    up = dot(normed, w_up, nt)
+    gate_up = dot(normed, w_both, nt)
+    gate = gate_up[:, :rows]
+    up = gate_up[:, rows:]
     hidden = dot(cot, w_down, nt)
     sig = jax.nn.sigmoid(gate)
     silu = gate * sig
     act = (silu * up).astype(jnp.bfloat16)
     g_gate = (hidden * up * sig * (1.0 + gate * (1.0 - sig))).astype(jnp.bfloat16)
     g_up = (hidden * silu).astype(jnp.bfloat16)
+    g_both = jnp.concatenate([g_gate, g_up], axis=1)
     out_ref[...] += dot(act, w_down, nn)
-    back_ref[...] += dot(g_gate, w_gate, nn) + dot(g_up, w_up, nn)
-    made[buf, 0] = dot(g_gate, normed, tn).astype(jnp.bfloat16).reshape(group, tile_rows, width)
-    made[buf, 1] = dot(g_up, normed, tn).astype(jnp.bfloat16).reshape(group, tile_rows, width)
+    back_ref[...] += dot(g_both, w_both, nn)
+    made[buf, 0:2] = dot(g_both, normed, tn).astype(jnp.bfloat16).reshape(2, group, tile_rows, width)
     made[buf, 2] = dot(act, cot, tn).astype(jnp.bfloat16).reshape(group, tile_rows, width)
     for kind in range(3):
         @pl.loop(0, group, unroll=True)
         def _(t, kind=kind):
-            pltpu.make_async_copy(made.at[buf, kind, t], grads_ref.at[tables[kind][step * group + t]], store_sem.at[buf]).start()
+            pltpu.make_async_copy(made.at[buf, kind, t], grads_ref.at[table[offsets[kind] + step * group + t]], store_sem.at[buf]).start()
 
     @pl.when(step == steps - 1)
     def _():
+        middle = middle_ref[...]
+        inv = lax.rsqrt(jnp.mean(middle * middle, axis=1, keepdims=True) + norm_eps)
+        back = back_ref[...]
+        scaled = back * gains_ref[1:2, :]
+        part = jnp.mean(scaled * middle, axis=1, keepdims=True)
+        grad = cot_ref[...].astype(jnp.float32) + inv * scaled - middle * inv**3 * part
+        grad_ref[...] = grad
+        branch_ref[...] = grad.astype(jnp.bfloat16)
+        block_ref[...] = (middle + out_ref[...]).astype(jnp.bfloat16)
+        term = jnp.sum(back * middle * inv, axis=0, keepdims=True)
+        line = lax.broadcasted_iota(jnp.int32, gain_ref.shape, 0)
+        gain_ref[...] = jnp.where(line == 1, term, 0.0)
         drain(1 - buf)
         drain(buf)
 
-def ffn_call(gate_s, up_s, down_s, normed, cot, wall, group=16):
+def ffn_call(table, offsets, number, normed, cot, middle, gains, wall, group=32):
     tokens, width = normed.shape
-    steps = gate_s.shape[0] // group
+    steps = number // group
     tr = wall.shape[1]
     full = pl.BlockSpec((tokens, width), lambda i, *_: (0, 0))
     return pl.pallas_call(
-        functools.partial(ffn_kernel, group),
+        functools.partial(ffn_kernel, group, offsets),
         grid_spec=pltpu.PrefetchScalarGridSpec(
-            num_scalar_prefetch=3, grid=(steps,),
-            in_specs=[full, full, pl.BlockSpec(memory_space=pl.ANY)],
-            out_specs=[full, full, pl.BlockSpec(memory_space=pl.ANY)],
-            scratch_shapes=[pltpu.VMEM((2, 3, group, tr, width), jnp.bfloat16), pltpu.VMEM((2, 3, group, tr, width), jnp.bfloat16),
-                pltpu.SemaphoreType.DMA((2,)), pltpu.SemaphoreType.DMA((2,))]),
-        out_shape=[jax.ShapeDtypeStruct((tokens, width), jnp.float32), jax.ShapeDtypeStruct((tokens, width), jnp.float32), jax.ShapeDtypeStruct(wall.shape, jnp.bfloat16)],
-        compiler_params=pltpu.CompilerParams(vmem_limit_bytes=56 << 20, dimension_semantics=("arbitrary",)),
+            num_scalar_prefetch=1, grid=(steps,),
+            in_specs=[full, full, full, full_spec(gains.shape), any_spec()],
+            out_specs=[full, full, full, full_spec((8, width)), any_spec()],
+            scratch_shapes=[
+                pltpu.VMEM((tokens, width), jnp.float32),
+                pltpu.VMEM((tokens, width), jnp.float32),
+                pltpu.VMEM((2, 3, group, tr, width), jnp.bfloat16),
+                pltpu.VMEM((2, 3, group, tr, width), jnp.bfloat16),
+                pltpu.SemaphoreType.DMA((2,)),
+                pltpu.SemaphoreType.DMA((2,)),
+            ],
+        ),
+        out_shape=[
+            jax.ShapeDtypeStruct((tokens, width), jnp.bfloat16),
+            jax.ShapeDtypeStruct((tokens, width), jnp.float32),
+            jax.ShapeDtypeStruct((tokens, width), jnp.bfloat16),
+            jax.ShapeDtypeStruct((8, width), jnp.float32),
+            jax.ShapeDtypeStruct(wall.shape, jnp.bfloat16),
+        ],
+        compiler_params=pltpu.CompilerParams(vmem_limit_bytes=60 << 20, dimension_semantics=("arbitrary",)),
         name="ffn",
-    )(gate_s, up_s, down_s, normed, cot, wall)
+    )(table, normed, cot, middle, gains, wall)
 
 
 MESH = pl.DeviceIdType.MESH
@@ -720,7 +754,7 @@
 
 
 GATHER_PLAN = (3, (0, 0, 0, 0), (10, 6), (11, 3))
-SCATTER_PLAN = (3, (4, 4, 0, 0), (4, 6), (40, 0))
+SCATTER_PLAN = (3, (5, 5, 0, 0), (4, 6), (40, 0))
 
 
 def split_slots(caps, plan):
@@ -1174,10 +1208,12 @@
     hidden_ref,
     cos_ref,
     sin_ref,
+    grad_ref,
+    gains_ref,
     wall_ref,
     out_ref,
     total_ref,
-    back_ref,
+    input_ref,
     core_ref,
     first_ref,
     second_ref,
@@ -1217,6 +1253,7 @@
         hop_send,
         hop_recv,
         built_sem,
+        back_ref,
     ) = scratch[8:]
     enter(("x", "y", "core", "z", "back"))
 
@@ -1348,7 +1385,11 @@
         if step == 0:
             hidden = hidden_ref[...].astype(jnp.float32)
             inv = lax.rsqrt(jnp.mean(hidden * hidden, axis=1, keepdims=True) + norm_eps)
-            term = jnp.sum(back_ref[...] * hidden * inv, axis=0, keepdims=True)
+            back = back_ref[...]
+            term = jnp.sum(back * hidden * inv, axis=0, keepdims=True)
+            scaled = back * gains_ref[0:1, :]
+            part = jnp.mean(scaled * hidden, axis=1, keepdims=True)
+            input_ref[...] = grad_ref[...] + inv * scaled - hidden * inv**3 * part
             line = lax.broadcasted_iota(jnp.int32, gain_ref.shape, 0)
             sums[0] = jnp.where(line == 0, term, gain_ref[...])
         elif step < 4:
@@ -1595,10 +1636,12 @@
     hidden,
     cosine,
     sine,
+    grad_middle,
+    gains,
     lead,
     first_group,
     caps,
-    look=(4, 1, 16),
+    look=(5, 2, 17),
 ):
     rows, width = grads_wall.shape[1:]
     kind = grads_wall.dtype
@@ -1644,6 +1687,7 @@
         dma((3,)),
         dma((3,)),
         dma((2,)),
+        pltpu.VMEM((tokens, width), jnp.float32),
     ]
     vmem = pl.BlockSpec(memory_space=pltpu.VMEM)
     smem = pl.BlockSpec(memory_space=pltpu.SMEM)
@@ -1661,7 +1705,7 @@
             jax.ShapeDtypeStruct((3, 2) + tile, kind),
             jax.ShapeDtypeStruct(tile, kind),
         ],
-        in_specs=[anyw, vmem, anyw, smem, smem] + [vmem] * 9,
+        in_specs=[anyw, vmem, anyw, smem, smem] + [vmem] * 11,
         out_specs=[anyw, anyw, vmem, vmem] + [anyw] * 5,
         scratch_shapes=scratch,
         input_output_aliases={0: 0},
@@ -1671,7 +1715,7 @@
         name="scatter_slots",
     )(
         wall, gain_terms, weights, table, places, branch, attended, queries, both, lse, normed,
-        hidden, cosine, sine,
+        hidden, cosine, sine, grad_middle, gains,
     )
     return out[1], out[2], out[3]
 
@@ -1691,13 +1735,8 @@
     devices = lax.axis_size("dp") * lax.axis_size("fsdp")
     caps, tile_rows, model_width = master.shape
     layout = section_layout(devices, tile_rows)
-    slot_qkv, slot_out, slot_ffn, slot_down = slot_numbers(owners, layout, caps)
-    query_tiles = model_width // tile_rows
-    slot_query, slot_both = slot_qkv[:query_tiles], slot_qkv[query_tiles:]
-    half = slot_ffn.shape[0] // 2
-    lead = layout[2][3]
-    tokens = hidden_in.astype(jnp.float32)
-    local_len = tokens.shape[0]
+    slots = slot_numbers(owners, layout, caps)
+    local_len = hidden_in.shape[0]
     first = lax.axis_index("fsdp") * local_len
     positions = first + jnp.arange(local_len, dtype=jnp.int32)
     places = jnp.concatenate([first[None].astype(jnp.int32), piece_starts[0]])
@@ -1707,34 +1746,30 @@
     ) = forward_attention(
         master.astype(jnp.bfloat16),
         gain_master.astype(jnp.bfloat16),
-        (slot_query, slot_both, slot_out),
+        slots,
         places,
         hidden_in,
         cosine,
         sine,
-        lead,
+        layout,
     )
-    gain_attn = gains_low[0]
-    gain_ffn = gains_low[1]
-    inv_one = lax.rsqrt(jnp.mean(tokens * tokens, axis=1, keepdims=True) + norm_eps)
-    inv_two = lax.rsqrt(jnp.mean(middle * middle, axis=1, keepdims=True) + norm_eps)
-    ffn_out, grad_normed_two, grads_wall = ffn_call(
-        slot_ffn[:half], slot_ffn[half:], slot_down, normed_two, out_cotangent, wall
+    block_out, grad_middle, grad_branch, gain_terms, grads_wall = ffn_call(
+        slots,
+        (layout[2][0], layout[2][0] + layout[2][1] // 2, layout[3][0]),
+        layout[3][1],
+        normed_two,
+        out_cotangent,
+        middle,
+        gains_low,
+        wall,
     )
-    block_out = (middle + ffn_out).astype(jnp.bfloat16)
-    scaled_two = grad_normed_two * gain_ffn
-    grad_middle = (
-        out_cotangent.astype(jnp.float32)
-        + inv_two * scaled_two
-        - middle * inv_two**3 * jnp.mean(scaled_two * middle, axis=1, keepdims=True)
-    )
-    gain_two_term = jnp.sum(grad_normed_two * middle * inv_two, axis=0)
-    grad_branch = grad_middle.astype(jnp.bfloat16)
-    weight_grad, gain_grad, grad_normed = backward_attention(
+    weight_grad, gain_grad, input_grad = backward_attention(
         grads_wall,
-        gain_two_term,
+        gain_terms,
+        grad_middle,
+        gains_low,
         weights,
-        (slot_query, slot_both, slot_out),
+        slots,
         places,
         grad_branch,
         attended,
@@ -1748,14 +1783,8 @@
         layout,
         caps,
     )
-    keep_slot = filled_mask(owners, layout, lax.axis_index(("dp", "fsdp")))[:, None, None]
+    keep_slot = filled_mask(slots, caps, lax.axis_index(("dp", "fsdp")))[:, None, None]
     weight_grad = jnp.where(keep_slot, weight_grad, 0.0)
-    scaled_one = grad_normed * gain_attn
-    input_grad = (
-        grad_middle
-        + inv_one * scaled_one
-        - tokens * inv_one**3 * jnp.mean(scaled_one * tokens, axis=1, keepdims=True)
-    )
     step = float(STEP)
     new_one, new_two, new_weights = adam_step(
         master, moment_one, moment_two, weight_grad, step, decay_rate, learn_rate

time: 1410 us -> 1390 us (0.986)
  other arithmetic: 69.4 us -> 48.5 us
where the time goes in v8:
time: 1390 us; the launch traced here: 1380 us
  Pallas kernels  1320 us (95%)
  other arithmetic  48.5 us (3%)
    pallas_call x1, Pallas kernels, scatter_slots(): pl.pallas_call(functools.partial(scatter_kernel, look, lead, first_group)...  620 us
    pallas_call x1, Pallas kernels, gather_slots(): pl.pallas_call(functools.partial(gather_kernel, lead), out_shape=[jax.Sha...  602 us
    pallas_call x1, Pallas kernels, ffn_call(): pl.pallas_call(functools.partial(ffn_kernel, group, offsets), grid_spec=p...  101 us

profile of v8, /device:TPU:0, one launch (start us, length us, event | category | flops | bytes accessed | tf_op | source)
XLA Modules:
  0.0 1376.7 jit_solution(11937283931081357574)
XLA Ops:
  0.7 1.2 pad_add_fusion.places
  1.9 0.7 convert_element_type.20
  2.6 0.6 pad.4.gain_ref
  3.2 0.7 multiply_add_fusion.1
  3.9 1.2 convert_reduce_fusion
  5.1 0.7 add_add_fusion.table
  5.8 0.0 copy-start.2
  5.8 0.2 compare_reduce_fusion
  6.1 0.0 copy-start.3
  6.1 0.7 select_reduce_fusion.table
  6.8 0.2 fusion.2
  7.0 0.8 copy.27.cos_ref
  7.9 0.8 copy.28.sin_ref
  8.7 6.9 convert_element_type.19.mine_ref
  15.6 0.0 copy-done.3
  15.6 601.7 %gather_slots.1 = (bf16[2,2,2,4,76,16,2048]{6,5,4,3,2,1,0:T(8,128)(2,1)}, bf16[2,2,2,4,16,128]{5,4,3,2,1,0:T(8,128)(2,1)}, bf16[320,16,2048]{2,1,0:T(8,128)(2,1)...) custom-call(bf16[76,16,2048]{2,1,0:T(8,128)(2,1)} %convert_element_t, ...), custom_call_target="tpu_custom_call" | custom-call | tf_op jit(solution)/shard_map/gather_slots/pallas_call | solution.py:1100
  617.4 0.0 copy-done.2
  617.4 100.5 %ffn.1 = (bf16[256,2048]{1,0:T(8,128)(2,1)}, f32[256,2048]{1,0:T(8,128)}, bf16[256,2048]{1,0:T(8,128)(2,1)}, f32[8,2048]{1,0:T(8,128)}, bf16[2432,16,2048]{2,1,0:T(8,128)(2,1)}) custom-call(s32[1856]{0:T(1024)} %copy-done.2, bf16[256,2048]{1,0:T(8,128)(2,1)} %get-tuple-element.28.normed_ref, bf16[256,2048]{1,0:T(8,128)(2,1)} %cot_ref.1, ...), custom_call_target="tpu_custom_call" | custom-call | tf_op jit(solution)/shard_map/ffn/pallas_call | solution.py:692
  717.9 0.0 copy-start.4
  717.9 0.0 copy-start.5
  717.9 0.0 copy-start.6
  717.9 620.4 %scatter_slots.1 = (bf16[2,2,2,4,76,16,2048]{6,5,4,3,2,1,0:T(8,128)(2,1)}, f32[76,16,2048]{2,1,0:T(8,128)}, f32[8,2048]{1,0:T(8,128)}, f32[256,2048]{1,0:T(8,128...) custom-call(bf16[2,2,2,4,76,16,2048]{6,5,4,3,2,1,0:T(8,128)(2,1)} %b, ...), custom_call_target="tpu_custom_call", output_to_operand_aliasing={{0}: (0, {})} | custom-call | tf_op jit(solution)/shard_map/scatter_slots/pallas_call | solution.py:1695
  1338.4 0.8 slice.8
  1339.2 0.0 copy-done.4
  1339.2 0.0 copy-done.5
  1339.2 0.0 copy-done.6
  1339.2 0.7 multiply_add_fusion.4
  1339.9 13.1 broadcast_select_fusion
  1353.0 0.0 copy-start
  1353.0 0.0 copy-start.1
  1353.0 22.1 %broadcast_select_fusion.1 = (f32[76,16,2048]{2,1,0:T(8,128)}, f32[76,16,2048]{2,1,0:T(8,128)}) fusion(pred[76]{0:T(512)(128)(4,1)S(1)} %compare_reduce_fusion, f32[76,16,2048]{2,1,0:T(8,128)S(1)} %get-tuple-element.71, f32[76,16,2048]{2,1,0:T(8,128)} %param.17, f32[76,16,2048]{2,1,0:T(8,128)} %param.16, f32[76,16,2048]{2,1,0:T(8,128)} %param.18), kind=kLoop, calls=%fused_computation.8 | loop fusion | flops 39845888 | bytes 59768908 | tf_op jit(solution)/shard_map/jit(_where)/select_n | solution.py:1792
  1375.2 0.0 copy-done
  1375.2 0.0 copy-done.1
  1375.2 1.3 copy.33
  (7 shorter events, 0.1 us)
Async XLA Ops:
  5.8 611.5 %copy-start.2 = (s32[1856]{0:T(1024)}, s32[1856]{0:T(1024)S(1)}, u32[]{:S(2)}) copy-start(s32[1856]{0:T(1024)S(1)} %add_add_fusion.table) | copy-start | bytes 22276
  6.1 9.5 copy-start.3
  717.9 621.3 %copy-start.4 = (f32[2,64]{1,0:T(2,128)S(1)}, f32[2,64]{1,0:T(2,128)}, u32[]{:S(2)}) copy-start(f32[2,64]{1,0:T(2,128)} %param.19) | copy-start | bytes 1540
  717.9 621.3 %copy-start.5 = (f32[2,64]{1,0:T(2,128)S(1)}, f32[2,64]{1,0:T(2,128)}, u32[]{:S(2)}) copy-start(f32[2,64]{1,0:T(2,128)} %param.20) | copy-start | bytes 1540
  717.9 621.3 %copy-start.6 = (f32[2,64]{1,0:T(2,128)S(1)}, f32[2,64]{1,0:T(2,128)}, u32[]{:S(2)}) copy-start(f32[2,64]{1,0:T(2,128)} %param.21) | copy-start | bytes 1540
  1353.0 22.1 %copy-start = (f32[76,16,2048]{2,1,0:T(8,128)}, f32[76,16,2048]{2,1,0:T(8,128)S(1)}, u32[]{:S(2)}) copy-start(f32[76,16,2048]{2,1,0:T(8,128)S(1)} %get-tuple-element.71) | copy-start | bytes 29884420
  1353.0 22.1 %copy-start.1 = (f32[256,2048]{1,0:T(8,128)S(1)}, f32[256,2048]{1,0:T(8,128)}, u32[]{:S(2)}) copy-start(f32[256,2048]{1,0:T(8,128)} %get-tuple-element.70) | copy-start | bytes 6291460

commit v9 on v8

--- a/solution.py
+++ b/solution.py
@@ -102,17 +102,18 @@
     return slots[:query], slots[query : layout[1][0]], slots[layout[1][0] : layout[2][0]]
 
 
-def forward_attention(low_tiles, low_gains, slots, places, hidden_in, cosine, sine, layout):
-    caps, tile_rows, width = low_tiles.shape
+def forward_attention(own_tiles, low_gains, slots, places, hidden_in, cosine, sine, layout):
+    caps, tile_rows, width = own_tiles.shape
     lead = layout[2][3]
     slot_query, slot_both, slot_out = attention_slots(slots, layout, width, tile_rows)
     if tuned_mesh():
         table = slots[: layout[2][0]]
         table = table // caps * lead + lax.rem(table, caps)
         (wall, weights, both, gains, normed, queries, attended, lse, middle, normed_two) = (
-            gather_slots(low_tiles, low_gains, table, places, hidden_in, cosine, sine, lead)
+            gather_slots(own_tiles, low_gains, table, places, hidden_in, cosine, sine, lead)
         )
         return wall, weights, gains, both, normed, queries, attended, lse, middle, normed_two
+    low_tiles = own_tiles.astype(jnp.bfloat16)
     wall = lax.all_gather(low_tiles, ("dp", "fsdp"), axis=0, tiled=True)
     gains = lax.all_gather(low_gains, ("dp", "fsdp"), axis=1, tiled=True).astype(jnp.float32)
     tokens = hidden_in.astype(jnp.float32)
@@ -746,11 +747,19 @@
     return (y * 4 + x * 2 + c, z)
 
 
-def enter(hops):
+def greet(hops):
     barrier = pltpu.get_barrier_semaphore()
     for hop in hops:
         pl.semaphore_signal(barrier, inc=1, device_id=target(hop), device_id_type=MESH)
-    pl.semaphore_wait(barrier, len(hops))
+
+
+def meet(hops):
+    pl.semaphore_wait(pltpu.get_barrier_semaphore(), len(hops))
+
+
+def enter(hops):
+    greet(hops)
+    meet(hops)
 
 
 GATHER_PLAN = (3, (0, 0, 0, 0), (10, 6), (11, 3))
@@ -853,6 +862,10 @@
     middle_ref,
     normed_two_ref,
     own_sem,
+    load_sem,
+    store_sem,
+    wide_ref,
+    low_ref,
     send_sem,
     recv_sem,
     tiles,
@@ -868,13 +881,46 @@
     y, x, c, z = position()
     counts, starts = split_slots(mine_ref.shape[0], GATHER_PLAN)
     rounds = round_count(counts, GATHER_PLAN)
-    own = pltpu.make_async_copy(mine_ref, wall_ref.at[y, x, c, z], own_sem.at[0])
-    own_gain = pltpu.make_async_copy(gain_ref, gains_ref.at[y, x, c, z], own_sem.at[1])
-    own.start()
+    own_gain = pltpu.make_async_copy(gain_ref, gains_ref.at[y, x, c, z], own_sem)
     own_gain.start()
-    enter(("x", "y", "core", "z", "back"))
-    own.wait()
+    greet(("x", "y", "core", "z", "back"))
+    few = wide_ref.shape[1]
+    parts_own = mine_ref.shape[0] // few
+
+    def load_own(i):
+        return pltpu.make_async_copy(
+            mine_ref.at[pl.ds(i * few, few)], wide_ref.at[lax.rem(i, 2)], load_sem.at[lax.rem(i, 2)]
+        )
+
+    def store_own(i):
+        return pltpu.make_async_copy(
+            low_ref.at[lax.rem(i, 2)],
+            wall_ref.at[y, x, c, z, pl.ds(i * few, few)],
+            store_sem.at[lax.rem(i, 2)],
+        )
+
+    load_own(0).start()
+    load_own(1).start()
+
+    @pl.loop(0, parts_own)
+    def _(i):
+        load_own(i).wait()
+
+        @pl.when(i >= 2)
+        def _():
+            store_own(i - 2).wait()
+
+        low_ref[lax.rem(i, 2)] = wide_ref[lax.rem(i, 2)].astype(low_ref.dtype)
+        store_own(i).start()
+
+        @pl.when(i + 2 < parts_own)
+        def _():
+            load_own(i + 2).start()
+
+    store_own(parts_own - 2).wait()
+    store_own(parts_own - 1).wait()
     own_gain.wait()
+    meet(("x", "y", "core", "z", "back"))
 
     def region(route, stage):
         hops = GATHER_ROUTES[route % 4]
@@ -1085,12 +1131,13 @@
             keep_both.wait()
 
 
-def gather_slots(low_tiles, low_gains, table, places, hidden, cosine, sine, lead):
-    caps, rows, width = low_tiles.shape
+def gather_slots(own_tiles, low_gains, table, places, hidden, cosine, sine, lead):
+    caps, rows, width = own_tiles.shape
+    few = max(size for size in range(1, caps // 3) if caps % size == 0)
     tokens = hidden.shape[0]
     length = tokens * 4
     counts, starts = split_slots(caps, GATHER_PLAN)
-    kind = low_tiles.dtype
+    kind = low_gains.dtype
     vmem = pl.BlockSpec(memory_space=pltpu.VMEM)
     smem = pl.BlockSpec(memory_space=pltpu.SMEM)
     anyw = pl.BlockSpec(memory_space=pl.ANY)
@@ -1112,10 +1159,14 @@
             jax.ShapeDtypeStruct((tokens, width), jnp.float32),
             jax.ShapeDtypeStruct((tokens, width), kind),
         ],
-        in_specs=[vmem, vmem, smem, smem, vmem, vmem, vmem],
+        in_specs=[anyw, vmem, smem, smem, vmem, vmem, vmem],
         out_specs=[anyw] * 4 + [vmem] * 7,
         scratch_shapes=[
+            pltpu.SemaphoreType.DMA,
             pltpu.SemaphoreType.DMA((2,)),
+            pltpu.SemaphoreType.DMA((2,)),
+            pltpu.VMEM((2, few, rows, width), own_tiles.dtype),
+            pltpu.VMEM((2, few, rows, width), kind),
             pltpu.SemaphoreType.DMA((5, 6)),
             pltpu.SemaphoreType.DMA((5, 6, max(counts))),
             pltpu.VMEM((32 * lead, rows, width), kind),
@@ -1132,7 +1183,7 @@
             collective_id=0, has_side_effects=True, vmem_limit_bytes=62 << 20
         ),
         name="gather_slots",
-    )(low_tiles, padded, table, places, hidden, cosine, sine)
+    )(own_tiles, padded, table, places, hidden, cosine, sine)
     return [outs[0].reshape(32 * caps, rows, width)] + list(outs[2:])
 
 
@@ -1744,7 +1795,7 @@
     (
         wall, weights, gains_low, both, normed, queries, attended, lse, middle, normed_two
     ) = forward_attention(
-        master.astype(jnp.bfloat16),
+        master,
         gain_master.astype(jnp.bfloat16),
         slots,
         places,

time: 1390 us -> 1400 us (level)
  Pallas kernels: 1320 us -> 1340 us
where the time goes in v9:
time: 1400 us; the launch traced here: 1380 us
  Pallas kernels  1340 us (96%)
  other arithmetic  41.6 us (3%)
    pallas_call x1, Pallas kernels, scatter_slots(): pl.pallas_call(functools.partial(scatter_kernel, look, lead, first_group)...  633 us
    pallas_call x1, Pallas kernels, gather_slots(): pl.pallas_call(functools.partial(gather_kernel, lead), out_shape=[jax.Sha...  604 us
    pallas_call x1, Pallas kernels, ffn_call(): pl.pallas_call(functools.partial(ffn_kernel, group, offsets), grid_spec=p...  100 us

profile of v9, /device:TPU:0, one launch (start us, length us, event | category | flops | bytes accessed | tf_op | source)
XLA Modules:
  0.0 1384.7 jit_solution(7471585883823921267)
XLA Ops:
  0.7 1.2 pad_add_fusion.places
  1.9 0.7 convert_element_type.16
  2.6 0.6 pad.4.gain_ref
  3.2 0.7 multiply_add_fusion.1
  3.9 1.2 convert_reduce_fusion
  5.1 0.7 add_add_fusion.table
  5.8 0.0 copy-start.2
  5.8 0.2 compare_reduce_fusion
  6.1 0.0 copy-start.3
  6.1 0.7 select_reduce_fusion.table
  6.8 0.2 fusion.2
  7.0 0.8 copy.27.cos_ref
  7.9 0.8 copy.28.sin_ref
  8.7 0.0 copy-done.3
  8.7 604.1 %gather_slots.1 = (bf16[2,2,2,4,76,16,2048]{6,5,4,3,2,1,0:T(8,128)(2,1)}, bf16[2,2,2,4,16,128]{5,4,3,2,1,0:T(8,128)(2,1)}, bf16[320,16,2048]{2,1,0:T(8,128)(2,1)...) custom-call(f32[76,16,2048]{2,1,0:T(8,128)} %mine_ref.1, ...), custom_call_target="tpu_custom_call" | custom-call | tf_op jit(solution)/shard_map/gather_slots/pallas_call | solution.py:1147
  612.8 0.0 copy-done.2
  612.8 100.5 %ffn.1 = (bf16[256,2048]{1,0:T(8,128)(2,1)}, f32[256,2048]{1,0:T(8,128)}, bf16[256,2048]{1,0:T(8,128)(2,1)}, f32[8,2048]{1,0:T(8,128)}, bf16[2432,16,2048]{2,1,0:T(8,128)(2,1)}) custom-call(s32[1856]{0:T(1024)} %copy-done.2, bf16[256,2048]{1,0:T(8,128)(2,1)} %get-tuple-element.28.normed_ref, bf16[256,2048]{1,0:T(8,128)(2,1)} %cot_ref.1, ...), custom_call_target="tpu_custom_call" | custom-call | tf_op jit(solution)/shard_map/ffn/pallas_call | solution.py:693
  713.3 0.0 copy-start.4
  713.3 0.0 copy-start.5
  713.3 0.0 copy-start.6
  713.3 632.9 %scatter_slots.1 = (bf16[2,2,2,4,76,16,2048]{6,5,4,3,2,1,0:T(8,128)(2,1)}, f32[76,16,2048]{2,1,0:T(8,128)}, f32[8,2048]{1,0:T(8,128)}, f32[256,2048]{1,0:T(8,128...) custom-call(bf16[2,2,2,4,76,16,2048]{6,5,4,3,2,1,0:T(8,128)(2,1)} %b, ...), custom_call_target="tpu_custom_call", output_to_operand_aliasing={{0}: (0, {})} | custom-call | tf_op jit(solution)/shard_map/scatter_slots/pallas_call | solution.py:1746
  1346.3 0.8 slice.8
  1347.1 0.0 copy-done.4
  1347.1 0.0 copy-done.5
  1347.1 0.0 copy-done.6
  1347.1 0.7 multiply_add_fusion.4
  1347.8 13.1 broadcast_select_fusion
  1360.9 0.0 copy-start
  1360.9 0.0 copy-start.1
  1360.9 22.1 %broadcast_select_fusion.1 = (f32[76,16,2048]{2,1,0:T(8,128)}, f32[76,16,2048]{2,1,0:T(8,128)}) fusion(pred[76]{0:T(512)(128)(4,1)S(1)} %compare_reduce_fusion, f32[76,16,2048]{2,1,0:T(8,128)S(1)} %get-tuple-element.71, f32[76,16,2048]{2,1,0:T(8,128)} %param.17, f32[76,16,2048]{2,1,0:T(8,128)} %mine_ref.1, f32[76,16,2048]{2,1,0:T(8,128)} %param.18), kind=kLoop, calls=%fused_computation.8 | loop fusion | flops 39845888 | bytes 59768908 | tf_op jit(solution)/shard_map/jit(_where)/select_n | solution.py:1843
  1383.0 0.0 copy-done
  1383.0 0.0 copy-done.1
  1383.0 1.3 copy.33
  (7 shorter events, 0.1 us)
Async XLA Ops:
  5.8 607.0 %copy-start.2 = (s32[1856]{0:T(1024)}, s32[1856]{0:T(1024)S(1)}, u32[]{:S(2)}) copy-start(s32[1856]{0:T(1024)S(1)} %add_add_fusion.table) | copy-start | bytes 22276
  6.1 2.6 copy-start.3
  713.3 633.8 %copy-start.4 = (f32[2,64]{1,0:T(2,128)S(1)}, f32[2,64]{1,0:T(2,128)}, u32[]{:S(2)}) copy-start(f32[2,64]{1,0:T(2,128)} %param.19) | copy-start | bytes 1540
  713.3 633.8 %copy-start.5 = (f32[2,64]{1,0:T(2,128)S(1)}, f32[2,64]{1,0:T(2,128)}, u32[]{:S(2)}) copy-start(f32[2,64]{1,0:T(2,128)} %param.20) | copy-start | bytes 1540
  713.3 633.8 %copy-start.6 = (f32[2,64]{1,0:T(2,128)S(1)}, f32[2,64]{1,0:T(2,128)}, u32[]{:S(2)}) copy-start(f32[2,64]{1,0:T(2,128)} %param.21) | copy-start | bytes 1540
  1360.9 22.1 %copy-start = (f32[76,16,2048]{2,1,0:T(8,128)}, f32[76,16,2048]{2,1,0:T(8,128)S(1)}, u32[]{:S(2)}) copy-start(f32[76,16,2048]{2,1,0:T(8,128)S(1)} %get-tuple-element.71) | copy-start | bytes 29884420
  1360.9 22.1 %copy-start.1 = (f32[256,2048]{1,0:T(8,128)S(1)}, f32[256,2048]{1,0:T(8,128)}, u32[]{:S(2)}) copy-start(f32[256,2048]{1,0:T(8,128)} %get-tuple-element.70) | copy-start | bytes 6291460

commit v10 on v8

--- a/solution.py
+++ b/solution.py
@@ -73,15 +73,12 @@
 
 
 def rope_tables(positions, block):
-    half_dim = HEAD // 2
-    inverse = rope_base ** (-(jnp.arange(half_dim, dtype=jnp.float32) * 2.0 / HEAD))
+    lane = jnp.arange(block, dtype=jnp.int32)
+    pair = lax.rem(lane, HEAD // 2).astype(jnp.float32)
+    inverse = rope_base ** (-(pair * 2.0 / HEAD))
     angles = positions[:, None] * inverse[None, :]
-    cosine = jnp.cos(angles)
-    sine = jnp.sin(angles)
-    return (
-        jnp.tile(jnp.concatenate([cosine, cosine], axis=1), (1, block // HEAD)),
-        jnp.tile(jnp.concatenate([-sine, sine], axis=1), (1, block // HEAD)),
-    )
+    sign = jnp.where(lax.rem(lane, HEAD) < HEAD // 2, -1.0, 1.0)
+    return jnp.cos(angles), jnp.sin(angles) * sign[None, :]
 
 
 def turn_back(grads, cosine, sine):

time: 1390 us -> 1390 us (level)
  no operation moved by 1% of the time
where the time goes in v10:
time: 1390 us; the launch traced here: 1380 us
  Pallas kernels  1320 us (95%)
  other arithmetic  50.1 us (4%)
    pallas_call x1, Pallas kernels, scatter_slots(): pl.pallas_call(functools.partial(scatter_kernel, look, lead, first_group)...  620 us
    pallas_call x1, Pallas kernels, gather_slots(): pl.pallas_call(functools.partial(gather_kernel, lead), out_shape=[jax.Sha...  602 us
    pallas_call x1, Pallas kernels, ffn_call(): pl.pallas_call(functools.partial(ffn_kernel, group, offsets), grid_spec=p...  100 us

profile of v10, /device:TPU:0, one launch (start us, length us, event | category | flops | bytes accessed | tf_op | source)
XLA Modules:
  0.0 1376.6 jit_solution(18243657807395105852)
XLA Ops:
  0.7 1.2 pad_add_fusion.places
  1.9 0.7 convert_element_type.27
  2.6 0.6 pad.4.gain_ref
  3.2 0.7 multiply_add_fusion.1
  3.9 1.2 convert_reduce_fusion
  5.1 0.7 add_add_fusion.table
  5.8 0.0 copy-start.2
  5.8 0.2 compare_reduce_fusion
  6.1 0.0 copy-start.3
  6.1 0.7 select_reduce_fusion.table
  6.8 1.8 fusion.2
  8.6 6.9 convert_element_type.26.mine_ref
  15.5 0.0 copy-done.3
  15.5 601.7 %gather_slots.1 = (bf16[2,2,2,4,76,16,2048]{6,5,4,3,2,1,0:T(8,128)(2,1)}, bf16[2,2,2,4,16,128]{5,4,3,2,1,0:T(8,128)(2,1)}, bf16[320,16,2048]{2,1,0:T(8,128)(2,1)...) custom-call(bf16[76,16,2048]{2,1,0:T(8,128)(2,1)} %convert_element_t, ...), custom_call_target="tpu_custom_call" | custom-call | tf_op jit(solution)/shard_map/gather_slots/pallas_call | solution.py:1097
  617.2 0.0 copy-done.2
  617.2 100.5 %ffn.1 = (bf16[256,2048]{1,0:T(8,128)(2,1)}, f32[256,2048]{1,0:T(8,128)}, bf16[256,2048]{1,0:T(8,128)(2,1)}, f32[8,2048]{1,0:T(8,128)}, bf16[2432,16,2048]{2,1,0:T(8,128)(2,1)}) custom-call(s32[1856]{0:T(1024)} %copy-done.2, bf16[256,2048]{1,0:T(8,128)(2,1)} %get-tuple-element.28.normed_ref, bf16[256,2048]{1,0:T(8,128)(2,1)} %cot_ref.1, ...), custom_call_target="tpu_custom_call" | custom-call | tf_op jit(solution)/shard_map/ffn/pallas_call | solution.py:689
  717.7 0.0 copy-start.4
  717.7 0.0 copy-start.5
  717.7 0.0 copy-start.6
  717.7 620.5 %scatter_slots.1 = (bf16[2,2,2,4,76,16,2048]{6,5,4,3,2,1,0:T(8,128)(2,1)}, f32[76,16,2048]{2,1,0:T(8,128)}, f32[8,2048]{1,0:T(8,128)}, f32[256,2048]{1,0:T(8,128...) custom-call(bf16[2,2,2,4,76,16,2048]{6,5,4,3,2,1,0:T(8,128)(2,1)} %b, ...), custom_call_target="tpu_custom_call", output_to_operand_aliasing={{0}: (0, {})} | custom-call | tf_op jit(solution)/shard_map/scatter_slots/pallas_call | solution.py:1692
  1338.2 0.8 slice.8
  1339.1 0.0 copy-done.4
  1339.1 0.0 copy-done.5
  1339.1 0.0 copy-done.6
  1339.1 0.7 multiply_add_fusion.4
  1339.8 13.1 broadcast_select_fusion
  1352.9 0.0 copy-start
  1352.9 0.0 copy-start.1
  1352.9 22.1 %broadcast_select_fusion.1 = (f32[76,16,2048]{2,1,0:T(8,128)}, f32[76,16,2048]{2,1,0:T(8,128)}) fusion(pred[76]{0:T(512)(128)(4,1)S(1)} %compare_reduce_fusion, f32[76,16,2048]{2,1,0:T(8,128)S(1)} %get-tuple-element.70, f32[76,16,2048]{2,1,0:T(8,128)} %param.17, f32[76,16,2048]{2,1,0:T(8,128)} %param.16, f32[76,16,2048]{2,1,0:T(8,128)} %param.18), kind=kLoop, calls=%fused_computation.8 | loop fusion | flops 39845888 | bytes 59768908 | tf_op jit(solution)/shard_map/jit(_where)/select_n | solution.py:1789
  1375.0 0.0 copy-done
  1375.0 0.0 copy-done.1
  1375.0 1.3 copy.25
  (4 shorter events, 0.0 us)
Async XLA Ops:
  5.8 611.4 %copy-start.2 = (s32[1856]{0:T(1024)}, s32[1856]{0:T(1024)S(1)}, u32[]{:S(2)}) copy-start(s32[1856]{0:T(1024)S(1)} %add_add_fusion.table) | copy-start | bytes 22276
  6.1 9.4 copy-start.3
  717.7 621.4 %copy-start.4 = (f32[2,64]{1,0:T(2,128)S(1)}, f32[2,64]{1,0:T(2,128)}, u32[]{:S(2)}) copy-start(f32[2,64]{1,0:T(2,128)} %param.19) | copy-start | bytes 1540
  717.7 621.4 %copy-start.5 = (f32[2,64]{1,0:T(2,128)S(1)}, f32[2,64]{1,0:T(2,128)}, u32[]{:S(2)}) copy-start(f32[2,64]{1,0:T(2,128)} %param.20) | copy-start | bytes 1540
  717.7 621.4 %copy-start.6 = (f32[2,64]{1,0:T(2,128)S(1)}, f32[2,64]{1,0:T(2,128)}, u32[]{:S(2)}) copy-start(f32[2,64]{1,0:T(2,128)} %param.21) | copy-start | bytes 1540
  1352.9 22.1 %copy-start = (f32[76,16,2048]{2,1,0:T(8,128)}, f32[76,16,2048]{2,1,0:T(8,128)S(1)}, u32[]{:S(2)}) copy-start(f32[76,16,2048]{2,1,0:T(8,128)S(1)} %get-tuple-element.70) | copy-start | bytes 29884420
  1352.9 22.1 %copy-start.1 = (f32[256,2048]{1,0:T(8,128)S(1)}, f32[256,2048]{1,0:T(8,128)}, u32[]{:S(2)}) copy-start(f32[256,2048]{1,0:T(8,128)} %get-tuple-element.69) | copy-start | bytes 6291460
